TPU v7x, 32 devices: a whole 2x2x4 slice. The times are simulated.
32 devices in a mesh: tiles: 8 (over z, x), far: 4 (over y, core).
Axes of the slice: x: 2, y: 2, z: 4, core: 2. Of those that a mesh axis runs over, the one named last changes fastest.
Arguments:
- panel_geometry: float32 [32, 6, 128], P('tiles'), may hold values from -1 to 1
- adjoint: bfloat16 [32, 16, 128], P('tiles', 'far'), may hold values from -6 to 6
- strengths: bfloat16 [32, 16, 128], P('tiles', 'far'), may hold values from -6 to 6
- pair_target: int32 [256], P('tiles'), may hold values from 0 to 3
- pair_owner: int32 [256, 1], P('tiles'), may hold values from 0 to 7; in each aligned block of 32 rows (0 to 31, 32 to 63, ...) at most 8 rows name the same one
- pair_source: int32 [256], P('tiles'), may hold values from 0 to 3
- pair_order: int32 [256], P('tiles'), may hold values from 1 to 3
- pair_count: int32 [8], P('tiles'), may hold values from 24 to 32, as said below
- corner_vertex: int32 [32, 4, 128], P('tiles'), may hold values from 0 to 4095, as said below
Outputs:
- vertex_grad: float32 [3, 4096], P(None, 'tiles')
Inputs may be any that keep to these rules, and one draw needn't show every extreme that they name: `pair_owner`: in the 32 slots of one list no owner is named more than 8 times; some list names one owner exactly 8 times. `pair_count`: some list is full with 32 live pairs. `corner_vertex`: every corner of a panel on tiles index t is a vertex owned by index t, t - 1, t + 1 or t + 8 / 2 (cyclically; the last is the mirrored half of the airframe); vertex v is owned by index v // 512.
All inputs are finite; a program needn't handle non-finite values.
Results may differ from a plain program's by a relative error of at most 0.00035.
Values may be sent and summed in bfloat16 or wider, within the bound.
No kernel may reach another device: no remote copies, remote signals or barrier semaphores. Data moves between devices by JAX's collectives and lax.ppermute only.
A program may use at most 128 MiB of HBM per device.

v0:
```python
import jax
import jax.numpy as jnp
from jax import lax
from jax.experimental import pallas as pl
from jax.experimental.pallas import tpu as pltpu
from jax.sharding import PartitionSpec as P

SMEM = pltpu.SMEM
VMEM = pltpu.VMEM
LANES = 128
HEAD = 5
SPARE = 2
GROUP = 32
LIMIT = 48 * 1024 * 1024


def pack_kernel(me_ref, parity_ref, geom_ref, strength_ref, corner_ref, out_ref):
    tiles, blocks, _, _ = out_ref.shape
    width = strength_ref.shape[2]
    shift = (blocks * width).bit_length() - 1
    me = me_ref[0]
    even = parity_ref[0] == 0
    shapes = []
    for b in range(blocks):
        vertex = corner_ref[b]
        offset = (vertex >> shift) - me
        offset = jnp.where(offset < 0, offset + tiles, offset)
        slot = jnp.where(
            offset == 0,
            0,
            jnp.where(offset == 1, 1, jnp.where(offset == tiles - 1, 2, 3)),
        )
        place = ((slot << shift) + (vertex & ((1 << shift) - 1))).astype(jnp.float32)
        span = float(4 << shift)
        for half in range(2):
            code = place[2 * half : 2 * half + 1] * span + place[2 * half + 1 : 2 * half + 2]
            rows = [geom_ref[3 * half + c, b : b + 1] for c in range(3)] + [code]
            shapes.append(jnp.concatenate(rows, axis=0))
    for b in range(blocks):
        shape = jnp.where(even, shapes[b], shapes[blocks + b])
        block = jnp.concatenate([strength_ref[b].astype(jnp.float32), shape], axis=1)
        for t in range(tiles):
            out_ref[t, b] = block


def split3(value):
    first = value.astype(jnp.bfloat16).astype(jnp.float32)
    rest = value - first
    second = rest.astype(jnp.bfloat16).astype(jnp.float32)
    return first, second, rest - second


def sort_kernel(
    me_ref,
    parity_ref,
    target_ref,
    owner_ref,
    source_ref,
    order_ref,
    count_ref,
    info_ref,
):
    live = count_ref[0]
    total = target_ref.shape[0]
    for k in range(HEAD + total, HEAD + total + SPARE):
        info_ref[k] = 0

    def note(order, state):
        def one(k, state):
            at, turn = state
            mine = order_ref[k] == order
            word = (owner_ref[k] << 18) | (order << 16) | (source_ref[k] << 8) | target_ref[k]
            info_ref[at] = word
            return at + jnp.where(mine, turn, 0), jnp.where(mine, 1 - turn, turn)

        return lax.fori_loop(0, live, one, state)

    third = note(3, (HEAD, 1 - parity_ref[0]))
    second = note(2, third)
    first, _ = note(1, second)
    for k in range(SPARE):
        info_ref[first + k] = 0
    info_ref[0] = me_ref[0]
    info_ref[1] = (third[0] - HEAD + 1) // 2
    info_ref[2] = (second[0] - HEAD + 1) // 2
    info_ref[3] = (first - HEAD + 1) // 2
    info_ref[4] = parity_ref[0]


def prep_kernel(geom_ref, adjoint_ref, partner_ref, centre_ref, left_ref):
    blocks, _, width = adjoint_ref.shape
    for b in range(blocks):
        point = jnp.concatenate([geom_ref[c, b : b + 1] for c in range(3)], axis=0)
        rows = [point, jnp.ones((1, width), jnp.float32)]
        rows += [jnp.sum(point * point, axis=0, keepdims=True)]
        rows += [jnp.zeros((3, width), jnp.float32)]
        x1, x2, x3 = split3(jnp.concatenate(rows, axis=0))
        values = [adjoint_ref[b].astype(jnp.float32), partner_ref[b].astype(jnp.float32)]
        rows = [x1, x1, x1, x2, x2, x3] + values
        left_ref[b] = jnp.concatenate(rows, axis=0).T.astype(jnp.bfloat16)
        for c in range(3):
            centre_ref[b, c] = jnp.broadcast_to(point[c : c + 1], (width, width)).T


def pair_kernel(
    info_ref,
    centre_ref,
    left_ref,
    mine_ref,
    other_ref,
    out_ref,
    product_ref,
    row_acc,
    grad_ref,
    joined_ref,
    shape_ref,
):
    tiles, blocks, _, _ = mine_ref.shape
    width = centre_ref.shape[3]
    me = info_ref[0]
    even = info_ref[4] == 0

    def settle(tile, carry):
        for b in range(blocks):
            mine = mine_ref[tile, b, :, width : 2 * width]
            other = other_ref[tile, b, :, width : 2 * width]
            shape_ref[tile, b] = jnp.where(even, mine, other)
            shape_ref[tile, blocks + b] = jnp.where(even, other, mine)
        return carry

    lax.fori_loop(0, tiles, settle, 0, unroll=min(tiles, 8))
    grad_ref[...] = jnp.zeros(grad_ref.shape, jnp.float32)
    row_acc[...] = jnp.zeros(row_acc.shape, jnp.float32)
    blank = jnp.zeros((4, width), jnp.float32)
    row_ids = lax.broadcasted_iota(jnp.int32, (8, width), 0)

    def reach_of(order):
        return 0.25 * jnp.where(
            order == 3, 0.7745966692414834, jnp.where(order == 2, 0.5773502691896258, 0.0)
        )

    def read(k):
        word = info_ref[HEAD + k]
        return word & 255, word >> 18, (word >> 8) & 255, (word >> 16) & 3

    def multiply(k, slot):
        target, owner, source, order = read(k)
        third = order == 3
        alive = jnp.where(order > 0, 1.0, 0.0).astype(jnp.float32)
        reach = reach_of(order)
        scale_mid = jnp.where(third, (4.0 / 9.0 / 512.0) ** (-2.0 / 3.0), 0.0)
        scale_side = jnp.where(
            third, (5.0 / 18.0 / 512.0) ** (-2.0 / 3.0), (0.5 / 512.0) ** (-2.0 / 3.0)
        )
        floor_mid = jnp.where(third, 0.0625 * (4.0 / 9.0 / 512.0) ** (-2.0 / 3.0), 3.0e38)
        floor_side = 0.0625 * scale_side
        point = shape_ref[owner, 2 * source]
        extent = shape_ref[owner, 2 * source + 1] * reach
        inside = row_ids < 3
        point = jnp.where(inside, jnp.concatenate([point, blank], axis=0), 0.0)
        extent = jnp.where(inside, jnp.concatenate([extent, blank], axis=0), 0.0)
        values = [ref[owner, source, :, 0:width] * alive for ref in (mine_ref, other_ref)]
        empty = jnp.zeros((8, width), jnp.float32)
        nodes = (
            (point, scale_mid, floor_mid),
            (point + extent, scale_side, floor_side),
            (point - extent, scale_side, floor_side),
        )
        columns = []
        for node, scale, floor in nodes:
            norm = jnp.sum(node * node, axis=0, keepdims=True) * scale + floor
            rows = jnp.where(
                row_ids == 3,
                norm,
                jnp.where(row_ids == 4, scale, node * (-2.0 * scale)),
            )
            p1, p2, p3 = split3(rows)
            columns.append(jnp.concatenate([p1, p2, p3, p1, p2, p1, empty], axis=0))
        columns.append(jnp.concatenate([empty] * 6 + values, axis=0))
        product_ref[slot] = jnp.dot(
            left_ref[target],
            jnp.concatenate(columns, axis=1).astype(jnp.bfloat16),
            preferred_element_type=jnp.float32,
        )

    def one_pair(k, slot, nodes):
        target, owner, source, order = read(k)
        reach = reach_of(order)
        point = [shape_ref[owner, 2 * source, c : c + 1] for c in range(3)]
        extent = [shape_ref[owner, 2 * source + 1, c : c + 1] * reach for c in range(3)]
        columns = [jnp.zeros((8, width), jnp.float32) for _ in range(3)]
        for start in range(0, width, GROUP):
            rows = slice(start, start + GROUP)
            sums = [row_acc[target, c, rows] for c in range(3)]

            def cubed(node):
                i = lax.rsqrt(product_ref[slot, rows, node * width : (node + 1) * width])
                return i * i * i

            coupling = product_ref[slot, rows, 3 * width : 4 * width]
            f_plus = cubed(1)
            if nodes == 1:
                even = (coupling + coupling) * f_plus
            else:
                f_minus = cubed(2)
                both = f_plus + f_minus
                even = coupling * (both + cubed(0) if nodes == 3 else both)
                odd = coupling * (f_plus - f_minus)
            for c in range(3):
                pulled = even * (centre_ref[target, c, rows] - point[c])
                if nodes > 1:
                    pulled = pulled - odd * extent[c]
                sums[c] = sums[c] + pulled
                for r in range(0, GROUP, 8):
                    columns[c] = columns[c] + pulled[r : r + 8]
            for c in range(3):
                row_acc[target, c, rows] = sums[c]
        sums = jnp.concatenate(
            [jnp.sum(columns[c], axis=0, keepdims=True) for c in range(3)], axis=0
        )
        grad_ref[owner * blocks + source, 0:3] += sums

    def two_pairs(nodes):
        def body(step, carry):
            for slot in range(2):
                multiply(2 * step + slot + 1, 1 - slot)
                one_pair(2 * step + slot, slot, nodes)
            return carry

        return body

    multiply(0, 0)
    lax.fori_loop(0, info_ref[1], two_pairs(3), 0)
    lax.fori_loop(info_ref[1], info_ref[2], two_pairs(2), 0)
    lax.fori_loop(info_ref[2], info_ref[3], two_pairs(1), 0)
    for b in range(blocks):
        total = jnp.concatenate(
            [jnp.sum(row_acc[b, c], axis=1, keepdims=True) for c in range(3)]
            + [jnp.zeros((width, 5), jnp.float32)],
            axis=1,
        )
        grad_ref[me * blocks + b] -= total.T

    high = blocks * width // LANES
    keys = 4 * high
    shift = (blocks * width).bit_length() + 1
    key_ids = lax.broadcasted_iota(jnp.int32, (keys, width), 0).astype(jnp.bfloat16)
    lane_ids = lax.broadcasted_iota(jnp.int32, (LANES, width), 0).astype(jnp.bfloat16)
    zero = jnp.zeros((keys, width), jnp.bfloat16)
    one = jnp.ones((keys, width), jnp.bfloat16)

    def wide(row):
        return jnp.broadcast_to(row, (keys, width))

    def narrow(value):
        return value.astype(jnp.float32).astype(jnp.bfloat16)

    def scatter(tile, carry):
        result = None
        for b in range(blocks):
            spread = []
            for c in range(3):
                grad = wide(grad_ref[tile * blocks + b, c : c + 1])
                upper = grad.astype(jnp.bfloat16)
                spread += [upper, (grad - upper.astype(jnp.float32)).astype(jnp.bfloat16)]
            parts = []
            hots = []
            for half in range(2):
                code = wide(shape_ref[tile, 2 * b + half, 3:4]).astype(jnp.int32)
                for place in (code >> shift, code & ((1 << shift) - 1)):
                    mask = key_ids == narrow(place >> 7)
                    low = narrow(place & (LANES - 1))
                    parts.append(
                        jnp.concatenate([jnp.where(mask, s, zero) for s in spread], axis=0)
                    )
                    hots.append(
                        jnp.concatenate(
                            [
                                jnp.where(lane_ids[g : g + keys] == low, one, zero)
                                for g in range(0, LANES, keys)
                            ],
                            axis=0,
                        )
                    )
            product = lax.dot_general(
                jnp.concatenate(parts, axis=1),
                jnp.concatenate(hots, axis=1),
                (((1,), (1,)), ((), ())),
                preferred_element_type=jnp.float32,
            )
            result = product if result is None else result + product
        for c in range(3):
            joined_ref[tile, c] = (
                result[2 * c * keys : (2 * c + 1) * keys]
                + result[(2 * c + 1) * keys : (2 * c + 2) * keys]
            )
        return carry

    def collect(dest, carry):
        for c in range(3):
            total = jnp.zeros((high, LANES), jnp.float32)
            for slot, by in enumerate((0, tiles - 1, 1, tiles - tiles // 2)):
                tile = lax.rem(dest + by, tiles)
                total = total + joined_ref[tile, c, slot * high : (slot + 1) * high]
            part = out_ref.shape[2]
            for f in range(out_ref.shape[1]):
                first = f * part % high
                out_ref[dest, f, :, c * LANES : (c + 1) * LANES] = total[first : first + part]
        return carry

    lax.fori_loop(0, tiles, scatter, 0, unroll=min(tiles, 8))
    lax.fori_loop(0, tiles, collect, 0, unroll=min(tiles, 8))


def sum_kernel(got_ref, out_ref):
    out_ref[...] = jnp.sum(got_ref[...], axis=0)


def last_kernel(parity_ref, mine_ref, other_ref, out_ref):
    part = mine_ref.shape[0]
    even = parity_ref[0] == 0
    mine, other = mine_ref[...], other_ref[...]
    halves = (jnp.where(even, mine, other), jnp.where(even, other, mine))
    for i, half in enumerate(halves):
        for r in range(part):
            h = i * part + r
            for c in range(3):
                out_ref[c : c + 1, h * LANES : (h + 1) * LANES] = half[
                    r : r + 1, c * LANES : (c + 1) * LANES
                ]


def per_device(
    panel_geometry,
    adjoint,
    strengths,
    pair_target,
    pair_owner,
    pair_source,
    pair_order,
    pair_count,
    corner_vertex,
):
    tiles = lax.axis_size("tiles")
    far = lax.axis_size("far")
    blocks, _, width = panel_geometry.shape
    high = blocks * width // LANES
    parity = lax.axis_index("far").astype(jnp.int32) & 1
    me = lax.axis_index("tiles").astype(jnp.int32).reshape(1)
    parity = parity.reshape(1)
    swap = [(f ^ 1, f) for f in range(far)]
    smem = pl.BlockSpec(memory_space=SMEM)
    vmem = pl.BlockSpec(memory_space=VMEM)
    params = pltpu.CompilerParams(vmem_limit_bytes=LIMIT)
    geometry = panel_geometry.transpose(1, 0, 2)
    packed = pl.pallas_call(
        pack_kernel,
        out_shape=jax.ShapeDtypeStruct((tiles, blocks, 4, 2 * width), jnp.float32),
        in_specs=[smem] * 2 + [vmem] * 3,
        out_specs=vmem,
    )(me, parity, geometry, strengths, corner_vertex)
    got = lax.all_to_all(packed, "tiles", split_axis=0, concat_axis=0, tiled=True)
    partner = lax.ppermute(adjoint, "far", swap)
    pairs = pair_target.shape[0]
    info = pl.pallas_call(
        sort_kernel,
        out_shape=jax.ShapeDtypeStruct((HEAD + pairs + SPARE,), jnp.int32),
        in_specs=[smem] * 7,
        out_specs=smem,
        cost_estimate=pl.CostEstimate(flops=4000000, bytes_accessed=900000, transcendentals=0),
    )(
        me,
        parity,
        pair_target,
        pair_owner[:, 0],
        pair_source,
        pair_order,
        pair_count,
    )
    centre, left = pl.pallas_call(
        prep_kernel,
        out_shape=(
            jax.ShapeDtypeStruct((blocks, 3, width, width), jnp.float32),
            jax.ShapeDtypeStruct((blocks, width, 56), jnp.bfloat16),
        ),
        compiler_params=params,
        cost_estimate=pl.CostEstimate(flops=4000000, bytes_accessed=900000, transcendentals=0),
    )(geometry, adjoint, partner)
    got, info, left = lax.optimization_barrier((got, info, left))
    other = lax.ppermute(got, "far", swap)
    partial = pl.pallas_call(
        pair_kernel,
        out_shape=jax.ShapeDtypeStruct((tiles, far, high // 2, 3 * LANES), jnp.float32),
        in_specs=[smem] + [vmem] * 4,
        out_specs=vmem,
        scratch_shapes=[
            VMEM((2, width, 4 * width), jnp.float32),
            VMEM((blocks, 3, width, width), jnp.float32),
            VMEM((tiles * blocks, 8, width), jnp.float32),
            VMEM((tiles, 3, 4 * high, LANES), jnp.float32),
            VMEM((tiles, 2 * blocks, 4, width), jnp.float32),
        ],
        compiler_params=params,
    )(info, centre, left, got, other)
    partial = partial.reshape(tiles * far, high // 2, 3 * LANES)
    shares = lax.all_to_all(partial, ("tiles", "far"), split_axis=0, concat_axis=0, tiled=True)
    mine = pl.pallas_call(
        sum_kernel,
        out_shape=jax.ShapeDtypeStruct((high // 2, 3 * LANES), jnp.float32),
        compiler_params=params,
    )(shares)
    other = lax.ppermute(mine, "far", swap)
    return pl.pallas_call(
        last_kernel,
        out_shape=jax.ShapeDtypeStruct((3, blocks * width), jnp.float32),
        in_specs=[smem, vmem, vmem],
        out_specs=vmem,
        compiler_params=params,
    )(parity, mine, other)


def solution(mesh):
    placed = (
        P("tiles", None, None),
        P("tiles", "far", None),
        P("tiles", "far", None),
        P("tiles"),
        P("tiles", None),
        P("tiles"),
        P("tiles"),
        P("tiles"),
        P("tiles", None, None),
    )
    return jax.shard_map(
        per_device, mesh=mesh, in_specs=placed, out_specs=P(None, "tiles"), check_vma=False
    )
```

profile of v0, /device:TPU:0, one launch (start us, length us, event | category | flops | bytes accessed | tf_op | source)
XLA Modules:
  0.0 33.9 jit_solution(2075160827798539112)
XLA Ops:
  0.0 1.4 %shard_map.91 = f32[8,4,4,256]{3,2,1,0:T(4,128)} custom-call(s32[1]{0:T(128)} %bitcast.1.me_ref, s32[1]{0:T(128)} %bitcast.parity_ref, f32[6,4,128]{2,1,0:T(4,128)} %bitcast.6, bf16[4,4,128]{2,1,0:T(4,128)(2,1)} %strength_ref.1, s32[4,4,128]{2,1,0:T(4,128)} %corner_ref.1), custom_call_target="tpu_custom_call" | custom-call | tf_op jit(solution)/shard_map/pallas_call | solution.py:356
  1.4 0.0 copy-start.1
  1.4 7.4 %all-to-all-start = ((f32[8,4,4,256]{3,2,1,0:T(4,128)}), f32[8,4,4,256]{3,2,1,0:T(4,128)S(1)}, u32[]{:S(2)}, u32[]{:S(2)}) async-start(f32[8,4,4,256]{3,2,1,0:T(4,128)} %shard_map.91), calls=%async_computation | async-start | bytes 262144 | tf_op jit(solution)/shard_map/all_to_all | solution.py:362
  8.8 0.0 copy-done.1
  8.8 0.0 copy-start
  8.8 0.1 collective-permute-start
  9.5 2.0 %shard_map.92.info_ref = s32[39]{0:T(128)} custom-call(s32[1]{0:T(128)} %bitcast.1.me_ref, s32[1]{0:T(128)} %bitcast.parity_ref, s32[32]{0:T(128)} %target_ref.1, s32[32]{0:T(128)} %bitcast.8, s32[32]{0:T(128)} %source_ref.1, s32[32]{0:T(128)} %order_ref.1, s32[1]{0:T(128)S(6)} %copy.10.count_ref), custom_call_target="tpu_custom_call" | custom-call | flops 4000000 | bytes 900000 | tf_op jit(solution)/shard_map/pallas_call | solution.py:365
  11.6 0.0 collective-permute-done.partner_ref
  11.6 0.0 copy-done
  11.6 0.3 shard_map.93
  11.9 4.2 %all-to-all-done.mine_ref = f32[8,4,4,256]{3,2,1,0:T(4,128)S(1)} async-done(((f32[8,4,4,256]{3,2,1,0:T(4,128)}), f32[8,4,4,256]{3,2,1,0:T(4,128)S(1)}, u32[]{:S(2)}, u32[]{:S(2)}) %all-to-all-start) | async-done | bytes 131104 | tf_op jit(solution)/shard_map/all_to_all | solution.py:362
  16.1 0.0 copy-start.2
  16.1 0.0 collective-permute-start.1
  16.1 1.3 %collective-permute-done.1.other_ref = f32[8,4,4,256]{3,2,1,0:T(4,128)S(1)} collective-permute-done((f32[8,4,4,256]{3,2,1,0:T(4,128)S(1)}, f32[8,4,4,256]{3,2,1,0:T(4,128)S(1)}, u32[]{:S(2)}, u32[]{:S(2)}) %collective-permute-start.1) | collective-permute-done | bytes 131104 | tf_op jit(solution)/shard_map/ppermute | solution.py:390
  17.5 0.0 copy-done.2
  17.5 4.4 %shard_map.94 = f32[8,4,2,384]{3,2,1,0:T(2,128)S(1)} custom-call(s32[39]{0:T(128)S(1)} %copy-done.2, f32[4,3,128,128]{3,2,1,0:T(8,128)S(1)} %get-tuple-element.12.centre_ref, bf16[4,128,56]{2,1,0:T(8,128)(2,1)S(1)} %get-tuple-element.13.left_ref, f32[8,4,4,256]{3,2,1,0:T(4,128)S(1)} %all-to-all-done.mine_ref, ...), custom_call_target="tpu_custom_call" | custom-call | tf_op jit(solution)/shard_map/pallas_call | solution.py:391
  21.9 10.1 %all_to_all.10.got_ref = f32[32,2,384]{2,1,0:T(2,128)S(1)} all-to-all(f32[32,2,384]{2,1,0:T(2,128)S(1)} %bitcast.5), channel_id=1, replica_groups=mesh['tiles'=8,'far'=4] {'tiles','far'}, dimensions={0} | all-to-all | bytes 196608 | tf_op jit(solution)/shard_map/all_to_all | solution.py:406
  32.0 0.1 shard_map.95.mine_ref
  32.1 0.2 collective-permute-start.2
  32.3 1.0 %collective-permute-done.2.other_ref = f32[2,384]{1,0:T(2,128)S(1)} collective-permute-done((f32[2,384]{1,0:T(2,128)S(1)}, f32[2,384]{1,0:T(2,128)S(1)}, u32[]{:S(2)}, u32[]{:S(2)}) %collective-permute-start.2) | collective-permute-done | bytes 3104 | tf_op jit(solution)/shard_map/ppermute | solution.py:412
  33.3 0.6 %shard_map.96 = f32[3,512]{1,0:T(4,128)} custom-call(s32[1]{0:T(128)} %bitcast.parity_ref, f32[2,384]{1,0:T(2,128)S(1)} %shard_map.95.mine_ref, f32[2,384]{1,0:T(2,128)S(1)} %collective-permute-done.2.other_ref), custom_call_target="tpu_custom_call" | custom-call | tf_op jit(solution)/shard_map/pallas_call | solution.py:413
Async XLA Ops:
  1.4 7.4 %copy-start.1 = (bf16[4,4,128]{2,1,0:T(4,128)(2,1)S(1)}, bf16[4,4,128]{2,1,0:T(4,128)(2,1)}, u32[]{:S(2)}) copy-start(bf16[4,4,128]{2,1,0:T(4,128)(2,1)} %adjoint_ref.1) | copy-start | bytes 12292
  1.4 14.7 %all-to-all-start = ((f32[8,4,4,256]{3,2,1,0:T(4,128)}), f32[8,4,4,256]{3,2,1,0:T(4,128)S(1)}, u32[]{:S(2)}, u32[]{:S(2)}) async-start(f32[8,4,4,256]{3,2,1,0:T(4,128)} %shard_map.91), calls=%async_computation | async-start | bytes 262144 | tf_op jit(solution)/shard_map/all_to_all | solution.py:362
  8.8 2.8 %copy-start = (f32[4,6,128]{2,0,1:T(4,128)S(1)}, f32[4,6,128]{2,0,1:T(4,128)}, u32[]{:S(2)}) copy-start(f32[4,6,128]{2,0,1:T(4,128)} %param.9) | copy-start | bytes 36868
  8.8 2.8 %collective-permute-start = (bf16[4,4,128]{2,1,0:T(4,128)(2,1)S(1)}, bf16[4,4,128]{2,1,0:T(4,128)(2,1)S(1)}, u32[]{:S(2)}, u32[]{:S(2)}) collective-permute-start(bf16[4,4,128]{2,1,0:T(4,128)(2,1)S(1)} %copy-done.1), channel_id=1, source_target_pairs={{1,0},{0,1},{3,2},{2,3},{5,4},{4,5},{7,6},{6,7},{9,8},{8,9},{11,10... | collective-permute-start | bytes 12296 | tf_op jit(solution)/shard_map/ppermute | solution.py:363
  16.1 1.4 %copy-start.2 = (s32[39]{0:T(128)S(1)}, s32[39]{0:T(128)}, u32[]{:S(2)}) copy-start(s32[39]{0:T(128)} %shard_map.92.info_ref) | copy-start | bytes 472
  16.1 1.3 %collective-permute-start.1 = (f32[8,4,4,256]{3,2,1,0:T(4,128)S(1)}, f32[8,4,4,256]{3,2,1,0:T(4,128)S(1)}, u32[]{:S(2)}, u32[]{:S(2)}) collective-permute-start(f32[8,4,4,256]{3,2,1,0:T(4,128)S(1)} %all-to-all-done.mine_ref), channel_id=1, source_target_pairs={{1,0},{0,1},{3,2},{2,3},{5,4},{4,5},{7,6},{6,7},{9,8},{8,9},{11,10... | collective-permute-start | bytes 393224 | tf_op jit(solution)/shard_map/ppermute | solution.py:390
  32.1 1.2 %collective-permute-start.2 = (f32[2,384]{1,0:T(2,128)S(1)}, f32[2,384]{1,0:T(2,128)S(1)}, u32[]{:S(2)}, u32[]{:S(2)}) collective-permute-start(f32[2,384]{1,0:T(2,128)S(1)} %shard_map.95.mine_ref), channel_id=1, source_target_pairs={{1,0},{0,1},{3,2},{2,3},{5,4},{4,5},{7,6},{6,7},{9,8},{8,9},{11,10... | collective-permute-start | bytes 9224 | tf_op jit(solution)/shard_map/ppermute | solution.py:412
where the time goes:
time: 34.3 us; the launch traced here: 33.9 us
  blocking collectives  10.1 us (29%)
  Pallas kernels  8.84 us (26%)
  starting transfers between devices  7.64 us (22%)
  waiting for transfers between devices  6.63 us (19%)
  between operations  0.7 us (2%)
    all_to_all x1, blocking collectives, per_device(): lax.all_to_all(partial, ('tiles', 'far'), split_axis=0, concat_axis=0, ti...  10.1 us
    all_to_all x1, starting transfers between devices, per_device(): lax.all_to_all(packed, 'tiles', split_axis=0, concat_axis=0, tiled=True)  7.38 us
    pallas_call x1, Pallas kernels, per_device(): pl.pallas_call(pair_kernel, out_shape=jax.ShapeDtypeStruct((tiles, far, h...  4.44 us
    all_to_all x1, waiting for transfers between devices, per_device(): lax.all_to_all(packed, 'tiles', split_axis=0, concat_axis=0, tiled=True)  4.23 us
    pallas_call x1, Pallas kernels, per_device(): pl.pallas_call(sort_kernel, out_shape=jax.ShapeDtypeStruct((HEAD + pairs...  2.02 us
    pallas_call x1, Pallas kernels, per_device(): pl.pallas_call(pack_kernel, out_shape=jax.ShapeDtypeStruct((tiles, blocks...  1.41 us
    ppermute x1, waiting for transfers between devices, per_device(): other = lax.ppermute(got, 'far', swap)  1.35 us
    ppermute x1, waiting for transfers between devices, per_device(): other = lax.ppermute(mine, 'far', swap)  1.05 us
  transfers between devices with their start and end apart: 4, of which 3 were waited for; matrix products, arithmetic and copies ran while one was open for 0% of the time, Pallas kernels for 7%

commit v1 on v0

--- a/solution.py
+++ b/solution.py
@@ -58,33 +58,40 @@
     source_ref,
     order_ref,
     count_ref,
+    blocks,
     info_ref,
 ):
-    live = count_ref[0]
-    total = target_ref.shape[0]
-    for k in range(HEAD + total, HEAD + total + SPARE):
-        info_ref[k] = 0
-
-    def note(order, state):
-        def one(k, state):
-            at, turn = state
-            mine = order_ref[k] == order
-            word = (owner_ref[k] << 18) | (order << 16) | (source_ref[k] << 8) | target_ref[k]
-            info_ref[at] = word
-            return at + jnp.where(mine, turn, 0), jnp.where(mine, 1 - turn, turn)
-
-        return lax.fori_loop(0, live, one, state)
-
-    third = note(3, (HEAD, 1 - parity_ref[0]))
-    second = note(2, third)
-    first, _ = note(1, second)
-    for k in range(SPARE):
-        info_ref[first + k] = 0
-    info_ref[0] = me_ref[0]
-    info_ref[1] = (third[0] - HEAD + 1) // 2
-    info_ref[2] = (second[0] - HEAD + 1) // 2
-    info_ref[3] = (first - HEAD + 1) // 2
-    info_ref[4] = parity_ref[0]
+    pairs = order_ref.shape[1]
+    lanes = info_ref.shape[1]
+    bits = (blocks - 1).bit_length()
+    parity = parity_ref[0]
+    order = order_ref[...]
+    place = lax.broadcasted_iota(jnp.int32, (1, pairs), 1)
+    live = place < count_ref[0]
+    word = (owner_ref[...] << bits | source_ref[...]) << bits | target_ref[...]
+    word = (word << 2 | order).astype(jnp.float32)
+    key = jnp.where(live, (3 - order) * pairs + place, 3 * pairs + place).astype(jnp.float32)
+    across = lax.broadcasted_iota(jnp.int32, (pairs, pairs), 1)
+    down = lax.broadcasted_iota(jnp.int32, (pairs, pairs), 0)
+
+    def upright(row):
+        spread = jnp.broadcast_to(row, (pairs, pairs))
+        return jnp.sum(jnp.where(across == down, spread, 0.0), axis=1, keepdims=True)
+
+    key_down = upright(key)
+    rank = jnp.sum(jnp.where(key < key_down, 1.0, 0.0), axis=1, keepdims=True).astype(jnp.int32)
+    kept = (rank & 1 == parity) & (rank < count_ref[0])
+    at = jnp.where(kept, HEAD + (rank >> 1), -1)
+    wide_lane = lax.broadcasted_iota(jnp.int32, (pairs, lanes), 1)
+    words = jnp.sum(jnp.where(wide_lane == at, upright(word), 0.0), axis=0, keepdims=True)
+    info = words.astype(jnp.int32)
+    lane = lax.broadcasted_iota(jnp.int32, (1, lanes), 1)
+    info = jnp.where(lane == 0, me_ref[0], jnp.where(lane == 4, parity, info))
+    for i in range(3):
+        upto = jnp.where(live & (order >= 3 - i), 1.0, 0.0)
+        total = jnp.sum(upto, axis=1, keepdims=True).astype(jnp.int32)
+        info = jnp.where(lane == i + 1, (((total + 1 - parity) >> 1) + 1) >> 1, info)
+    info_ref[...] = info
 
 
 def prep_kernel(geom_ref, adjoint_ref, partner_ref, centre_ref, left_ref):
@@ -117,8 +124,9 @@
 ):
     tiles, blocks, _, _ = mine_ref.shape
     width = centre_ref.shape[3]
-    me = info_ref[0]
-    even = info_ref[4] == 0
+    bits = (blocks - 1).bit_length()
+    me = info_ref[0, 0]
+    even = info_ref[0, 4] == 0
 
     def settle(tile, carry):
         for b in range(blocks):
@@ -140,8 +148,10 @@
         )
 
     def read(k):
-        word = info_ref[HEAD + k]
-        return word & 255, word >> 18, (word >> 8) & 255, (word >> 16) & 3
+        word = info_ref[0, HEAD + k]
+        inner = word >> 2
+        outer = inner >> bits
+        return inner & (blocks - 1), outer >> bits, outer & (blocks - 1), word & 3
 
     def multiply(k, slot):
         target, owner, source, order = read(k)
@@ -230,9 +240,9 @@
         return body
 
     multiply(0, 0)
-    lax.fori_loop(0, info_ref[1], two_pairs(3), 0)
-    lax.fori_loop(info_ref[1], info_ref[2], two_pairs(2), 0)
-    lax.fori_loop(info_ref[2], info_ref[3], two_pairs(1), 0)
+    lax.fori_loop(0, info_ref[0, 1], two_pairs(3), 0)
+    lax.fori_loop(info_ref[0, 1], info_ref[0, 2], two_pairs(2), 0)
+    lax.fori_loop(info_ref[0, 2], info_ref[0, 3], two_pairs(1), 0)
     for b in range(blocks):
         total = jnp.concatenate(
             [jnp.sum(row_acc[b, c], axis=1, keepdims=True) for c in range(3)]
@@ -363,18 +373,18 @@
     partner = lax.ppermute(adjoint, "far", swap)
     pairs = pair_target.shape[0]
     info = pl.pallas_call(
-        sort_kernel,
-        out_shape=jax.ShapeDtypeStruct((HEAD + pairs + SPARE,), jnp.int32),
-        in_specs=[smem] * 7,
-        out_specs=smem,
+        lambda *refs: sort_kernel(*refs[:-1], blocks, refs[-1]),
+        out_shape=jax.ShapeDtypeStruct((1, -(-(HEAD + pairs // 2 + SPARE + 1) // LANES) * LANES), jnp.int32),
+        in_specs=[smem] * 2 + [vmem] * 4 + [smem],
+        out_specs=vmem,
         cost_estimate=pl.CostEstimate(flops=4000000, bytes_accessed=900000, transcendentals=0),
     )(
         me,
         parity,
-        pair_target,
-        pair_owner[:, 0],
-        pair_source,
-        pair_order,
+        pair_target.reshape(1, pairs),
+        pair_owner.reshape(1, pairs),
+        pair_source.reshape(1, pairs),
+        pair_order.reshape(1, pairs),
         pair_count,
     )
     centre, left = pl.pallas_call(

time: 34.3 us -> 34.3 us (level)
  waiting for transfers between devices: 6.63 us -> 7.3 us
  Pallas kernels: 8.84 us -> 8.28 us
    all_to_all x1, waiting for transfers between devices: 4.23 us -> 4.9 us  [per_device(): lax.all_to_all(packed, 'tiles', split_axis=0, concat_axis=0, tiled=True)]
    pallas_call x1, Pallas kernels: 2.02 us -> 1.37 us  [per_device(): pl.pallas_call(lambda *refs: sort_kernel(*refs[:-1], blocks, refs[-1]), o...]
  transfers between devices with their start and end apart: 4 -> 4, of which waited for: 3 -> 3; matrix products, arithmetic and copies ran while one was open for 0% -> 0% of each run, Pallas kernels for 7% -> 5%
where the time goes in v1:
time: 34.3 us; the launch traced here: 33.9 us
  blocking collectives  10 us (29%)
  Pallas kernels  8.28 us (24%)
  starting transfers between devices  7.64 us (22%)
  waiting for transfers between devices  7.3 us (21%)
  between operations  0.68 us (2%)
    all_to_all x1, blocking collectives, per_device(): lax.all_to_all(partial, ('tiles', 'far'), split_axis=0, concat_axis=0, ti...  10 us
    all_to_all x1, starting transfers between devices, per_device(): lax.all_to_all(packed, 'tiles', split_axis=0, concat_axis=0, tiled=True)  7.38 us
    all_to_all x1, waiting for transfers between devices, per_device(): lax.all_to_all(packed, 'tiles', split_axis=0, concat_axis=0, tiled=True)  4.9 us
    pallas_call x1, Pallas kernels, per_device(): pl.pallas_call(pair_kernel, out_shape=jax.ShapeDtypeStruct((tiles, far, h...  4.52 us
    pallas_call x1, Pallas kernels, per_device(): pl.pallas_call(pack_kernel, out_shape=jax.ShapeDtypeStruct((tiles, blocks...  1.41 us
    pallas_call x1, Pallas kernels, per_device(): pl.pallas_call(lambda *refs: sort_kernel(*refs[:-1], blocks, refs[-1]), o...  1.37 us
    ppermute x1, waiting for transfers between devices, per_device(): other = lax.ppermute(got, 'far', swap)  1.35 us
    ppermute x1, waiting for transfers between devices, per_device(): other = lax.ppermute(mine, 'far', swap)  1.05 us
  transfers between devices with their start and end apart: 4, of which 3 were waited for; matrix products, arithmetic and copies ran while one was open for 0% of the time, Pallas kernels for 5%

profile of v1, /device:TPU:0, one launch (start us, length us, event | category | flops | bytes accessed | tf_op | source)
XLA Modules:
  0.0 33.9 jit_solution(61515929203027012)
XLA Ops:
  0.0 1.4 %shard_map.91 = f32[8,4,4,256]{3,2,1,0:T(4,128)} custom-call(s32[1]{0:T(128)} %bitcast.1.me_ref.refs_0_, s32[1]{0:T(128)} %bitcast.parity_ref.refs_1_, f32[6,4,128]{2,1,0:T(4,128)} %bitcast.9, bf16[4,4,128]{2,1,0:T(4,128)(2,1)} %strength_ref.1, s32[4,4,128]{2,1,0:T(4,128)} %corner_ref.1), custom_call_target="tpu_custom_call" | custom-call | tf_op jit(solution)/shard_map/pallas_call | solution.py:366
  1.4 0.0 copy-start.1
  1.4 7.4 %all-to-all-start = ((f32[8,4,4,256]{3,2,1,0:T(4,128)}), f32[8,4,4,256]{3,2,1,0:T(4,128)S(1)}, u32[]{:S(2)}, u32[]{:S(2)}) async-start(f32[8,4,4,256]{3,2,1,0:T(4,128)} %shard_map.91), calls=%async_computation | async-start | bytes 262144 | tf_op jit(solution)/shard_map/all_to_all | solution.py:372
  8.8 0.0 copy-done.1
  8.8 0.0 copy-start
  8.8 0.1 collective-permute-start
  9.5 1.4 %shard_map.92.info_ref = s32[1,128]{1,0:T(1,128)} custom-call(s32[1]{0:T(128)} %bitcast.1.me_ref.refs_0_, s32[1]{0:T(128)} %bitcast.parity_ref.refs_1_, s32[1,32]{1,0:T(1,128)} %bitcast.11, s32[1,32]{1,0:T(1,128)} %bitcast.12, s32[1,32]{1,0:T(1,128)} %bitcast.13, s32[1,32]{1,0:T(1,128)} %bitcast.14, s32[1]{0:T(128)S(6)} %copy.10.refs_6_), custom_call_target="tpu_custom_call" | custom-call | flops 4000000 | bytes 900000 | tf_op jit(solution)/shard_map/pallas_call | solution.py:375
  10.9 0.0 collective-permute-done.partner_ref
  10.9 0.0 copy-done
  10.9 0.3 shard_map.93
  11.2 4.9 %all-to-all-done.mine_ref = f32[8,4,4,256]{3,2,1,0:T(4,128)S(1)} async-done(((f32[8,4,4,256]{3,2,1,0:T(4,128)}), f32[8,4,4,256]{3,2,1,0:T(4,128)S(1)}, u32[]{:S(2)}, u32[]{:S(2)}) %all-to-all-start) | async-done | bytes 131104 | tf_op jit(solution)/shard_map/all_to_all | solution.py:372
  16.1 0.0 copy-start.2
  16.1 0.0 collective-permute-start.1
  16.1 1.3 %collective-permute-done.1.other_ref = f32[8,4,4,256]{3,2,1,0:T(4,128)S(1)} collective-permute-done((f32[8,4,4,256]{3,2,1,0:T(4,128)S(1)}, f32[8,4,4,256]{3,2,1,0:T(4,128)S(1)}, u32[]{:S(2)}, u32[]{:S(2)}) %collective-permute-start.1) | collective-permute-done | bytes 131104 | tf_op jit(solution)/shard_map/ppermute | solution.py:400
  17.5 0.0 copy-done.2
  17.5 4.5 %shard_map.94 = f32[8,4,2,384]{3,2,1,0:T(2,128)S(1)} custom-call(s32[1,128]{1,0:T(1,128)S(1)} %copy-done.2, f32[4,3,128,128]{3,2,1,0:T(8,128)S(1)} %get-tuple-element.12.centre_ref, bf16[4,128,56]{2,1,0:T(8,128)(2,1)S(1)} %get-tuple-element.13.left_ref, f32[8,4,4,256]{3,2,1,0:T(4,128)S(1)} %all-to-all-done.mine_ref, ...), custom_call_target="tpu_custom_call" | custom-call | tf_op jit(solution)/shard_map/pallas_call | solution.py:401
  22.0 10.0 %all_to_all.10.got_ref = f32[32,2,384]{2,1,0:T(2,128)S(1)} all-to-all(f32[32,2,384]{2,1,0:T(2,128)S(1)} %bitcast.8), channel_id=1, replica_groups=mesh['tiles'=8,'far'=4] {'tiles','far'}, dimensions={0} | all-to-all | bytes 196608 | tf_op jit(solution)/shard_map/all_to_all | solution.py:416
  32.0 0.1 shard_map.95.mine_ref
  32.1 0.2 collective-permute-start.2
  32.3 1.0 %collective-permute-done.2.other_ref = f32[2,384]{1,0:T(2,128)S(1)} collective-permute-done((f32[2,384]{1,0:T(2,128)S(1)}, f32[2,384]{1,0:T(2,128)S(1)}, u32[]{:S(2)}, u32[]{:S(2)}) %collective-permute-start.2) | collective-permute-done | bytes 3104 | tf_op jit(solution)/shard_map/ppermute | solution.py:422
  33.3 0.6 %shard_map.96 = f32[3,512]{1,0:T(4,128)} custom-call(s32[1]{0:T(128)} %bitcast.parity_ref.refs_1_, f32[2,384]{1,0:T(2,128)S(1)} %shard_map.95.mine_ref, f32[2,384]{1,0:T(2,128)S(1)} %collective-permute-done.2.other_ref), custom_call_target="tpu_custom_call" | custom-call | tf_op jit(solution)/shard_map/pallas_call | solution.py:423
Async XLA Ops:
  1.4 7.4 %copy-start.1 = (bf16[4,4,128]{2,1,0:T(4,128)(2,1)S(1)}, bf16[4,4,128]{2,1,0:T(4,128)(2,1)}, u32[]{:S(2)}) copy-start(bf16[4,4,128]{2,1,0:T(4,128)(2,1)} %adjoint_ref.1) | copy-start | bytes 12292
  1.4 14.7 %all-to-all-start = ((f32[8,4,4,256]{3,2,1,0:T(4,128)}), f32[8,4,4,256]{3,2,1,0:T(4,128)S(1)}, u32[]{:S(2)}, u32[]{:S(2)}) async-start(f32[8,4,4,256]{3,2,1,0:T(4,128)} %shard_map.91), calls=%async_computation | async-start | bytes 262144 | tf_op jit(solution)/shard_map/all_to_all | solution.py:372
  8.8 2.1 %copy-start = (f32[4,6,128]{2,0,1:T(4,128)S(1)}, f32[4,6,128]{2,0,1:T(4,128)}, u32[]{:S(2)}) copy-start(f32[4,6,128]{2,0,1:T(4,128)} %param.9) | copy-start | bytes 36868
  8.8 2.1 %collective-permute-start = (bf16[4,4,128]{2,1,0:T(4,128)(2,1)S(1)}, bf16[4,4,128]{2,1,0:T(4,128)(2,1)S(1)}, u32[]{:S(2)}, u32[]{:S(2)}) collective-permute-start(bf16[4,4,128]{2,1,0:T(4,128)(2,1)S(1)} %copy-done.1), channel_id=1, source_target_pairs={{1,0},{0,1},{3,2},{2,3},{5,4},{4,5},{7,6},{6,7},{9,8},{8,9},{11,10... | collective-permute-start | bytes 12296 | tf_op jit(solution)/shard_map/ppermute | solution.py:373
  16.1 1.4 %copy-start.2 = (s32[1,128]{1,0:T(1,128)S(1)}, s32[1,128]{1,0:T(1,128)}, u32[]{:S(2)}) copy-start(s32[1,128]{1,0:T(1,128)} %shard_map.92.info_ref) | copy-start | bytes 1540
  16.1 1.3 %collective-permute-start.1 = (f32[8,4,4,256]{3,2,1,0:T(4,128)S(1)}, f32[8,4,4,256]{3,2,1,0:T(4,128)S(1)}, u32[]{:S(2)}, u32[]{:S(2)}) collective-permute-start(f32[8,4,4,256]{3,2,1,0:T(4,128)S(1)} %all-to-all-done.mine_ref), channel_id=1, source_target_pairs={{1,0},{0,1},{3,2},{2,3},{5,4},{4,5},{7,6},{6,7},{9,8},{8,9},{11,10... | collective-permute-start | bytes 393224 | tf_op jit(solution)/shard_map/ppermute | solution.py:400
  32.1 1.2 %collective-permute-start.2 = (f32[2,384]{1,0:T(2,128)S(1)}, f32[2,384]{1,0:T(2,128)S(1)}, u32[]{:S(2)}, u32[]{:S(2)}) collective-permute-start(f32[2,384]{1,0:T(2,128)S(1)} %shard_map.95.mine_ref), channel_id=1, source_target_pairs={{1,0},{0,1},{3,2},{2,3},{5,4},{4,5},{7,6},{6,7},{9,8},{8,9},{11,10... | collective-permute-start | bytes 9224 | tf_op jit(solution)/shard_map/ppermute | solution.py:422

commit v2 on v1

--- a/solution.py
+++ b/solution.py
@@ -118,7 +118,7 @@
     out_ref,
     product_ref,
     row_acc,
-    grad_ref,
+    sums_ref,
     joined_ref,
     shape_ref,
 ):
@@ -137,7 +137,8 @@
         return carry
 
     lax.fori_loop(0, tiles, settle, 0, unroll=min(tiles, 8))
-    grad_ref[...] = jnp.zeros(grad_ref.shape, jnp.float32)
+    sums_ref[...] = jnp.zeros(sums_ref.shape, jnp.float32)
+    joined_ref[...] = jnp.zeros(joined_ref.shape, jnp.float32)
     row_acc[...] = jnp.zeros(row_acc.shape, jnp.float32)
     blank = jnp.zeros((4, width), jnp.float32)
     row_ids = lax.broadcasted_iota(jnp.int32, (8, width), 0)
@@ -225,31 +226,8 @@
                     columns[c] = columns[c] + pulled[r : r + 8]
             for c in range(3):
                 row_acc[target, c, rows] = sums[c]
-        sums = jnp.concatenate(
-            [jnp.sum(columns[c], axis=0, keepdims=True) for c in range(3)], axis=0
-        )
-        grad_ref[owner * blocks + source, 0:3] += sums
-
-    def two_pairs(nodes):
-        def body(step, carry):
-            for slot in range(2):
-                multiply(2 * step + slot + 1, 1 - slot)
-                one_pair(2 * step + slot, slot, nodes)
-            return carry
-
-        return body
-
-    multiply(0, 0)
-    lax.fori_loop(0, info_ref[0, 1], two_pairs(3), 0)
-    lax.fori_loop(info_ref[0, 1], info_ref[0, 2], two_pairs(2), 0)
-    lax.fori_loop(info_ref[0, 2], info_ref[0, 3], two_pairs(1), 0)
-    for b in range(blocks):
-        total = jnp.concatenate(
-            [jnp.sum(row_acc[b, c], axis=1, keepdims=True) for c in range(3)]
-            + [jnp.zeros((width, 5), jnp.float32)],
-            axis=1,
-        )
-        grad_ref[me * blocks + b] -= total.T
+        for c in range(3):
+            sums_ref[slot, c : c + 1] = jnp.sum(columns[c], axis=0, keepdims=True)
 
     high = blocks * width // LANES
     keys = 4 * high
@@ -265,46 +243,72 @@
     def narrow(value):
         return value.astype(jnp.float32).astype(jnp.bfloat16)
 
-    def scatter(tile, carry):
-        result = None
-        for b in range(blocks):
-            spread = []
-            for c in range(3):
-                grad = wide(grad_ref[tile * blocks + b, c : c + 1])
-                upper = grad.astype(jnp.bfloat16)
-                spread += [upper, (grad - upper.astype(jnp.float32)).astype(jnp.bfloat16)]
-            parts = []
-            hots = []
-            for half in range(2):
-                code = wide(shape_ref[tile, 2 * b + half, 3:4]).astype(jnp.int32)
-                for place in (code >> shift, code & ((1 << shift) - 1)):
-                    mask = key_ids == narrow(place >> 7)
-                    low = narrow(place & (LANES - 1))
-                    parts.append(
-                        jnp.concatenate([jnp.where(mask, s, zero) for s in spread], axis=0)
+    def scatter(tile, b, slot):
+        spread = []
+        for c in range(3):
+            grad = wide(sums_ref[slot, c : c + 1])
+            upper = grad.astype(jnp.bfloat16)
+            spread += [upper, (grad - upper.astype(jnp.float32)).astype(jnp.bfloat16)]
+        parts = []
+        hots = []
+        for half in range(2):
+            code = wide(shape_ref[tile, 2 * b + half, 3:4]).astype(jnp.int32)
+            for place in (code >> shift, code & ((1 << shift) - 1)):
+                mask = key_ids == narrow(place >> 7)
+                low = narrow(place & (LANES - 1))
+                parts.append(jnp.concatenate([jnp.where(mask, s, zero) for s in spread], axis=0))
+                hots.append(
+                    jnp.concatenate(
+                        [
+                            jnp.where(lane_ids[g : g + keys] == low, one, zero)
+                            for g in range(0, LANES, keys)
+                        ],
+                        axis=0,
                     )
-                    hots.append(
-                        jnp.concatenate(
-                            [
-                                jnp.where(lane_ids[g : g + keys] == low, one, zero)
-                                for g in range(0, LANES, keys)
-                            ],
-                            axis=0,
-                        )
-                    )
-            product = lax.dot_general(
-                jnp.concatenate(parts, axis=1),
-                jnp.concatenate(hots, axis=1),
-                (((1,), (1,)), ((), ())),
-                preferred_element_type=jnp.float32,
-            )
-            result = product if result is None else result + product
+                )
+        result = lax.dot_general(
+            jnp.concatenate(parts, axis=1),
+            jnp.concatenate(hots, axis=1),
+            (((1,), (1,)), ((), ())),
+            preferred_element_type=jnp.float32,
+        )
+        before = [joined_ref[tile, c] for c in range(3)]
         for c in range(3):
             joined_ref[tile, c] = (
-                result[2 * c * keys : (2 * c + 1) * keys]
+                before[c]
+                + result[2 * c * keys : (2 * c + 1) * keys]
                 + result[(2 * c + 1) * keys : (2 * c + 2) * keys]
             )
-        return carry
+
+    def scatter_pair(k, slot):
+        _, owner, source, _ = read(k)
+        scatter(owner, source, slot)
+
+    def two_pairs(nodes):
+        def body(step, carry):
+            for slot in range(2):
+                k = 2 * step + slot
+                multiply(k + 1, 1 - slot)
+                scatter_pair(k - 1, 1 - slot)
+                one_pair(k, slot, nodes)
+            return carry
+
+        return body
+
+    multiply(0, 0)
+    lax.fori_loop(0, info_ref[0, 1], two_pairs(3), 0)
+    lax.fori_loop(info_ref[0, 1], info_ref[0, 2], two_pairs(2), 0)
+    lax.fori_loop(info_ref[0, 2], info_ref[0, 3], two_pairs(1), 0)
+    scatter_pair(2 * info_ref[0, 3] - 1, 1)
+    for b in range(blocks):
+        total = jnp.concatenate(
+            [jnp.sum(row_acc[b, c], axis=1, keepdims=True) for c in range(3)]
+            + [jnp.zeros((width, 5), jnp.float32)],
+            axis=1,
+        )
+        sums_ref[2 + b] = -total.T
+    for b in range(blocks):
+        scatter(me, b, 2 + b)
 
     def collect(dest, carry):
         for c in range(3):
@@ -318,7 +322,6 @@
                 out_ref[dest, f, :, c * LANES : (c + 1) * LANES] = total[first : first + part]
         return carry
 
-    lax.fori_loop(0, tiles, scatter, 0, unroll=min(tiles, 8))
     lax.fori_loop(0, tiles, collect, 0, unroll=min(tiles, 8))
 
 
@@ -406,7 +409,7 @@
         scratch_shapes=[
             VMEM((2, width, 4 * width), jnp.float32),
             VMEM((blocks, 3, width, width), jnp.float32),
-            VMEM((tiles * blocks, 8, width), jnp.float32),
+            VMEM((2 + blocks, 8, width), jnp.float32),
             VMEM((tiles, 3, 4 * high, LANES), jnp.float32),
             VMEM((tiles, 2 * blocks, 4, width), jnp.float32),
         ],

time: 34.3 us -> 33.6 us (0.980)
  Pallas kernels: 8.28 us -> 7.86 us
    pallas_call x1, Pallas kernels: 4.52 us -> 4.11 us  [per_device(): pl.pallas_call(pair_kernel, out_shape=jax.ShapeDtypeStruct((tiles, far, h...]
    all_to_all x1, blocking collectives: 10 us -> 9.68 us  [per_device(): lax.all_to_all(partial, ('tiles', 'far'), split_axis=0, concat_axis=0, ti...]
where the time goes in v2:
time: 33.6 us; the launch traced here: 33.2 us
  blocking collectives  9.68 us (29%)
  Pallas kernels  7.86 us (23%)
  starting transfers between devices  7.64 us (23%)
  waiting for transfers between devices  7.3 us (22%)
  between operations  0.69 us (2%)
    all_to_all x1, blocking collectives, per_device(): lax.all_to_all(partial, ('tiles', 'far'), split_axis=0, concat_axis=0, ti...  9.68 us
    all_to_all x1, starting transfers between devices, per_device(): lax.all_to_all(packed, 'tiles', split_axis=0, concat_axis=0, tiled=True)  7.38 us
    all_to_all x1, waiting for transfers between devices, per_device(): lax.all_to_all(packed, 'tiles', split_axis=0, concat_axis=0, tiled=True)  4.9 us
    pallas_call x1, Pallas kernels, per_device(): pl.pallas_call(pair_kernel, out_shape=jax.ShapeDtypeStruct((tiles, far, h...  4.11 us
    pallas_call x1, Pallas kernels, per_device(): pl.pallas_call(pack_kernel, out_shape=jax.ShapeDtypeStruct((tiles, blocks...  1.41 us
    pallas_call x1, Pallas kernels, per_device(): pl.pallas_call(lambda *refs: sort_kernel(*refs[:-1], blocks, refs[-1]), o...  1.37 us
    ppermute x1, waiting for transfers between devices, per_device(): other = lax.ppermute(got, 'far', swap)  1.35 us
    ppermute x1, waiting for transfers between devices, per_device(): other = lax.ppermute(mine, 'far', swap)  1.05 us
  transfers between devices with their start and end apart: 4, of which 3 were waited for; matrix products, arithmetic and copies ran while one was open for 0% of the time, Pallas kernels for 5%

profile of v2, /device:TPU:0, one launch (start us, length us, event | category | flops | bytes accessed | tf_op | source)
XLA Modules:
  0.0 33.2 jit_solution(6182560980224487799)
XLA Ops:
  0.0 1.4 %shard_map.91 = f32[8,4,4,256]{3,2,1,0:T(4,128)} custom-call(s32[1]{0:T(128)} %bitcast.1.me_ref.refs_0_, s32[1]{0:T(128)} %bitcast.parity_ref.refs_1_, f32[6,4,128]{2,1,0:T(4,128)} %bitcast.9, bf16[4,4,128]{2,1,0:T(4,128)(2,1)} %strength_ref.1, s32[4,4,128]{2,1,0:T(4,128)} %corner_ref.1), custom_call_target="tpu_custom_call" | custom-call | tf_op jit(solution)/shard_map/pallas_call | solution.py:369
  1.4 0.0 copy-start.1
  1.4 7.4 %all-to-all-start = ((f32[8,4,4,256]{3,2,1,0:T(4,128)}), f32[8,4,4,256]{3,2,1,0:T(4,128)S(1)}, u32[]{:S(2)}, u32[]{:S(2)}) async-start(f32[8,4,4,256]{3,2,1,0:T(4,128)} %shard_map.91), calls=%async_computation | async-start | bytes 262144 | tf_op jit(solution)/shard_map/all_to_all | solution.py:375
  8.8 0.0 copy-done.1
  8.8 0.0 copy-start
  8.8 0.1 collective-permute-start
  9.5 1.4 %shard_map.92.info_ref = s32[1,128]{1,0:T(1,128)} custom-call(s32[1]{0:T(128)} %bitcast.1.me_ref.refs_0_, s32[1]{0:T(128)} %bitcast.parity_ref.refs_1_, s32[1,32]{1,0:T(1,128)} %bitcast.11, s32[1,32]{1,0:T(1,128)} %bitcast.12, s32[1,32]{1,0:T(1,128)} %bitcast.13, s32[1,32]{1,0:T(1,128)} %bitcast.14, s32[1]{0:T(128)S(6)} %copy.10.refs_6_), custom_call_target="tpu_custom_call" | custom-call | flops 4000000 | bytes 900000 | tf_op jit(solution)/shard_map/pallas_call | solution.py:378
  10.9 0.0 collective-permute-done.partner_ref
  10.9 0.0 copy-done
  10.9 0.3 shard_map.93
  11.2 4.9 %all-to-all-done.mine_ref = f32[8,4,4,256]{3,2,1,0:T(4,128)S(1)} async-done(((f32[8,4,4,256]{3,2,1,0:T(4,128)}), f32[8,4,4,256]{3,2,1,0:T(4,128)S(1)}, u32[]{:S(2)}, u32[]{:S(2)}) %all-to-all-start) | async-done | bytes 131104 | tf_op jit(solution)/shard_map/all_to_all | solution.py:375
  16.1 0.0 copy-start.2
  16.1 0.0 collective-permute-start.1
  16.1 1.3 %collective-permute-done.1.other_ref = f32[8,4,4,256]{3,2,1,0:T(4,128)S(1)} collective-permute-done((f32[8,4,4,256]{3,2,1,0:T(4,128)S(1)}, f32[8,4,4,256]{3,2,1,0:T(4,128)S(1)}, u32[]{:S(2)}, u32[]{:S(2)}) %collective-permute-start.1) | collective-permute-done | bytes 131104 | tf_op jit(solution)/shard_map/ppermute | solution.py:403
  17.5 0.0 copy-done.2
  17.5 4.1 %shard_map.94 = f32[8,4,2,384]{3,2,1,0:T(2,128)S(1)} custom-call(s32[1,128]{1,0:T(1,128)S(1)} %copy-done.2, f32[4,3,128,128]{3,2,1,0:T(8,128)S(1)} %get-tuple-element.12.centre_ref, bf16[4,128,56]{2,1,0:T(8,128)(2,1)S(1)} %get-tuple-element.13.left_ref, f32[8,4,4,256]{3,2,1,0:T(4,128)S(1)} %all-to-all-done.mine_ref, ...), custom_call_target="tpu_custom_call" | custom-call | tf_op jit(solution)/shard_map/pallas_call | solution.py:404
  21.6 9.7 %all_to_all.10.got_ref = f32[32,2,384]{2,1,0:T(2,128)S(1)} all-to-all(f32[32,2,384]{2,1,0:T(2,128)S(1)} %bitcast.8), channel_id=1, replica_groups=mesh['tiles'=8,'far'=4] {'tiles','far'}, dimensions={0} | all-to-all | bytes 196608 | tf_op jit(solution)/shard_map/all_to_all | solution.py:419
  31.3 0.1 shard_map.95.mine_ref
  31.3 0.2 collective-permute-start.2
  31.5 1.0 %collective-permute-done.2.other_ref = f32[2,384]{1,0:T(2,128)S(1)} collective-permute-done((f32[2,384]{1,0:T(2,128)S(1)}, f32[2,384]{1,0:T(2,128)S(1)}, u32[]{:S(2)}, u32[]{:S(2)}) %collective-permute-start.2) | collective-permute-done | bytes 3104 | tf_op jit(solution)/shard_map/ppermute | solution.py:425
  32.6 0.6 %shard_map.96 = f32[3,512]{1,0:T(4,128)} custom-call(s32[1]{0:T(128)} %bitcast.parity_ref.refs_1_, f32[2,384]{1,0:T(2,128)S(1)} %shard_map.95.mine_ref, f32[2,384]{1,0:T(2,128)S(1)} %collective-permute-done.2.other_ref), custom_call_target="tpu_custom_call" | custom-call | tf_op jit(solution)/shard_map/pallas_call | solution.py:426
Async XLA Ops:
  1.4 7.4 %copy-start.1 = (bf16[4,4,128]{2,1,0:T(4,128)(2,1)S(1)}, bf16[4,4,128]{2,1,0:T(4,128)(2,1)}, u32[]{:S(2)}) copy-start(bf16[4,4,128]{2,1,0:T(4,128)(2,1)} %adjoint_ref.1) | copy-start | bytes 12292
  1.4 14.7 %all-to-all-start = ((f32[8,4,4,256]{3,2,1,0:T(4,128)}), f32[8,4,4,256]{3,2,1,0:T(4,128)S(1)}, u32[]{:S(2)}, u32[]{:S(2)}) async-start(f32[8,4,4,256]{3,2,1,0:T(4,128)} %shard_map.91), calls=%async_computation | async-start | bytes 262144 | tf_op jit(solution)/shard_map/all_to_all | solution.py:375
  8.8 2.1 %copy-start = (f32[4,6,128]{2,0,1:T(4,128)S(1)}, f32[4,6,128]{2,0,1:T(4,128)}, u32[]{:S(2)}) copy-start(f32[4,6,128]{2,0,1:T(4,128)} %param.9) | copy-start | bytes 36868
  8.8 2.1 %collective-permute-start = (bf16[4,4,128]{2,1,0:T(4,128)(2,1)S(1)}, bf16[4,4,128]{2,1,0:T(4,128)(2,1)S(1)}, u32[]{:S(2)}, u32[]{:S(2)}) collective-permute-start(bf16[4,4,128]{2,1,0:T(4,128)(2,1)S(1)} %copy-done.1), channel_id=1, source_target_pairs={{1,0},{0,1},{3,2},{2,3},{5,4},{4,5},{7,6},{6,7},{9,8},{8,9},{11,10... | collective-permute-start | bytes 12296 | tf_op jit(solution)/shard_map/ppermute | solution.py:376
  16.1 1.4 %copy-start.2 = (s32[1,128]{1,0:T(1,128)S(1)}, s32[1,128]{1,0:T(1,128)}, u32[]{:S(2)}) copy-start(s32[1,128]{1,0:T(1,128)} %shard_map.92.info_ref) | copy-start | bytes 1540
  16.1 1.3 %collective-permute-start.1 = (f32[8,4,4,256]{3,2,1,0:T(4,128)S(1)}, f32[8,4,4,256]{3,2,1,0:T(4,128)S(1)}, u32[]{:S(2)}, u32[]{:S(2)}) collective-permute-start(f32[8,4,4,256]{3,2,1,0:T(4,128)S(1)} %all-to-all-done.mine_ref), channel_id=1, source_target_pairs={{1,0},{0,1},{3,2},{2,3},{5,4},{4,5},{7,6},{6,7},{9,8},{8,9},{11,10... | collective-permute-start | bytes 393224 | tf_op jit(solution)/shard_map/ppermute | solution.py:403
  31.3 1.2 %collective-permute-start.2 = (f32[2,384]{1,0:T(2,128)S(1)}, f32[2,384]{1,0:T(2,128)S(1)}, u32[]{:S(2)}, u32[]{:S(2)}) collective-permute-start(f32[2,384]{1,0:T(2,128)S(1)} %shard_map.95.mine_ref), channel_id=1, source_target_pairs={{1,0},{0,1},{3,2},{2,3},{5,4},{4,5},{7,6},{6,7},{9,8},{8,9},{11,10... | collective-permute-start | bytes 9224 | tf_op jit(solution)/shard_map/ppermute | solution.py:425

commit v3 on v2

--- a/solution.py
+++ b/solution.py
@@ -154,7 +154,7 @@
         outer = inner >> bits
         return inner & (blocks - 1), outer >> bits, outer & (blocks - 1), word & 3
 
-    def multiply(k, slot):
+    def multiply(k, slot, nodes):
         target, owner, source, order = read(k)
         third = order == 3
         alive = jnp.where(order > 0, 1.0, 0.0).astype(jnp.float32)
@@ -172,13 +172,13 @@
         extent = jnp.where(inside, jnp.concatenate([extent, blank], axis=0), 0.0)
         values = [ref[owner, source, :, 0:width] * alive for ref in (mine_ref, other_ref)]
         empty = jnp.zeros((8, width), jnp.float32)
-        nodes = (
-            (point, scale_mid, floor_mid),
+        quadrature = (
             (point + extent, scale_side, floor_side),
             (point - extent, scale_side, floor_side),
+            (point, scale_mid, floor_mid),
         )
         columns = []
-        for node, scale, floor in nodes:
+        for node, scale, floor in quadrature[:nodes]:
             norm = jnp.sum(node * node, axis=0, keepdims=True) * scale + floor
             rows = jnp.where(
                 row_ids == 3,
@@ -187,8 +187,8 @@
             )
             p1, p2, p3 = split3(rows)
             columns.append(jnp.concatenate([p1, p2, p3, p1, p2, p1, empty], axis=0))
-        columns.append(jnp.concatenate([empty] * 6 + values, axis=0))
-        product_ref[slot] = jnp.dot(
+        columns.insert(1, jnp.concatenate([empty] * 6 + values, axis=0))
+        product_ref[slot, :, 0 : (nodes + 1) * width] = jnp.dot(
             left_ref[target],
             jnp.concatenate(columns, axis=1).astype(jnp.bfloat16),
             preferred_element_type=jnp.float32,
@@ -204,18 +204,18 @@
             rows = slice(start, start + GROUP)
             sums = [row_acc[target, c, rows] for c in range(3)]
 
-            def cubed(node):
-                i = lax.rsqrt(product_ref[slot, rows, node * width : (node + 1) * width])
+            def cubed(part):
+                i = lax.rsqrt(product_ref[slot, rows, part * width : (part + 1) * width])
                 return i * i * i
 
-            coupling = product_ref[slot, rows, 3 * width : 4 * width]
-            f_plus = cubed(1)
+            coupling = product_ref[slot, rows, width : 2 * width]
+            f_plus = cubed(0)
             if nodes == 1:
                 even = (coupling + coupling) * f_plus
             else:
                 f_minus = cubed(2)
                 both = f_plus + f_minus
-                even = coupling * (both + cubed(0) if nodes == 3 else both)
+                even = coupling * (both + cubed(3) if nodes == 3 else both)
                 odd = coupling * (f_plus - f_minus)
             for c in range(3):
                 pulled = even * (centre_ref[target, c, rows] - point[c])
@@ -281,34 +281,42 @@
             )
 
     def scatter_pair(k, slot):
-        _, owner, source, _ = read(k)
+        _, owner, source, _ = read(jnp.maximum(k, 0))
         scatter(owner, source, slot)
 
     def two_pairs(nodes):
         def body(step, carry):
-            for slot in range(2):
-                k = 2 * step + slot
-                multiply(k + 1, 1 - slot)
-                scatter_pair(k - 1, 1 - slot)
-                one_pair(k, slot, nodes)
+            for now in range(2):
+
+                @pl.when(lax.rem(step, 2) == now)
+                def _():
+                    for i in range(2):
+                        multiply(2 * step + 2 + i, 2 * (1 - now) + i, nodes)
+                    for i in range(2):
+                        scatter_pair(2 * step - 2 + i, 2 * (1 - now) + i)
+                        one_pair(2 * step + i, 2 * now + i, nodes)
+
             return carry
 
         return body
 
-    multiply(0, 0)
+    for i in range(2):
+        multiply(i, i, 3)
+    steps = info_ref[0, 3]
     lax.fori_loop(0, info_ref[0, 1], two_pairs(3), 0)
     lax.fori_loop(info_ref[0, 1], info_ref[0, 2], two_pairs(2), 0)
-    lax.fori_loop(info_ref[0, 2], info_ref[0, 3], two_pairs(1), 0)
-    scatter_pair(2 * info_ref[0, 3] - 1, 1)
+    lax.fori_loop(info_ref[0, 2], steps, two_pairs(1), 0)
+    for i in range(2):
+        scatter_pair(2 * steps - 2 + i, 2 * lax.rem(steps + 1, 2) + i)
     for b in range(blocks):
         total = jnp.concatenate(
             [jnp.sum(row_acc[b, c], axis=1, keepdims=True) for c in range(3)]
             + [jnp.zeros((width, 5), jnp.float32)],
             axis=1,
         )
-        sums_ref[2 + b] = -total.T
+        sums_ref[4 + b] = -total.T
     for b in range(blocks):
-        scatter(me, b, 2 + b)
+        scatter(me, b, 4 + b)
 
     def collect(dest, carry):
         for c in range(3):
@@ -407,9 +415,9 @@
         in_specs=[smem] + [vmem] * 4,
         out_specs=vmem,
         scratch_shapes=[
-            VMEM((2, width, 4 * width), jnp.float32),
+            VMEM((4, width, 4 * width), jnp.float32),
             VMEM((blocks, 3, width, width), jnp.float32),
-            VMEM((2 + blocks, 8, width), jnp.float32),
+            VMEM((4 + blocks, 8, width), jnp.float32),
             VMEM((tiles, 3, 4 * high, LANES), jnp.float32),
             VMEM((tiles, 2 * blocks, 4, width), jnp.float32),
         ],

time: 33.6 us -> 34.6 us (1.030)
  Pallas kernels: 7.86 us -> 8.64 us
    pallas_call x1, Pallas kernels: 4.11 us -> 4.88 us  [per_device(): pl.pallas_call(pair_kernel, out_shape=jax.ShapeDtypeStruct((tiles, far, h...]
where the time goes in v3:
time: 34.6 us; the launch traced here: 34.2 us
  blocking collectives  9.89 us (29%)
  Pallas kernels  8.64 us (25%)
  starting transfers between devices  7.64 us (22%)
  waiting for transfers between devices  7.3 us (21%)
  between operations  0.69 us (2%)
    all_to_all x1, blocking collectives, per_device(): lax.all_to_all(partial, ('tiles', 'far'), split_axis=0, concat_axis=0, ti...  9.89 us
    all_to_all x1, starting transfers between devices, per_device(): lax.all_to_all(packed, 'tiles', split_axis=0, concat_axis=0, tiled=True)  7.38 us
    all_to_all x1, waiting for transfers between devices, per_device(): lax.all_to_all(packed, 'tiles', split_axis=0, concat_axis=0, tiled=True)  4.9 us
    pallas_call x1, Pallas kernels, per_device(): pl.pallas_call(pair_kernel, out_shape=jax.ShapeDtypeStruct((tiles, far, h...  4.88 us
    pallas_call x1, Pallas kernels, per_device(): pl.pallas_call(pack_kernel, out_shape=jax.ShapeDtypeStruct((tiles, blocks...  1.41 us
    pallas_call x1, Pallas kernels, per_device(): pl.pallas_call(lambda *refs: sort_kernel(*refs[:-1], blocks, refs[-1]), o...  1.37 us
    ppermute x1, waiting for transfers between devices, per_device(): other = lax.ppermute(got, 'far', swap)  1.35 us
    ppermute x1, waiting for transfers between devices, per_device(): other = lax.ppermute(mine, 'far', swap)  1.05 us
  transfers between devices with their start and end apart: 4, of which 3 were waited for; matrix products, arithmetic and copies ran while one was open for 0% of the time, Pallas kernels for 5%

profile of v3, /device:TPU:0, one launch (start us, length us, event | category | flops | bytes accessed | tf_op | source)
XLA Modules:
  0.0 34.2 jit_solution(8376363395564357012)
XLA Ops:
  0.0 1.4 %shard_map.91 = f32[8,4,4,256]{3,2,1,0:T(4,128)} custom-call(s32[1]{0:T(128)} %bitcast.1.me_ref.refs_0_, s32[1]{0:T(128)} %bitcast.parity_ref.refs_1_, f32[6,4,128]{2,1,0:T(4,128)} %bitcast.9, bf16[4,4,128]{2,1,0:T(4,128)(2,1)} %strength_ref.1, s32[4,4,128]{2,1,0:T(4,128)} %corner_ref.1), custom_call_target="tpu_custom_call" | custom-call | tf_op jit(solution)/shard_map/pallas_call | solution.py:377
  1.4 0.0 copy-start.1
  1.4 7.4 %all-to-all-start = ((f32[8,4,4,256]{3,2,1,0:T(4,128)}), f32[8,4,4,256]{3,2,1,0:T(4,128)S(1)}, u32[]{:S(2)}, u32[]{:S(2)}) async-start(f32[8,4,4,256]{3,2,1,0:T(4,128)} %shard_map.91), calls=%async_computation | async-start | bytes 262144 | tf_op jit(solution)/shard_map/all_to_all | solution.py:383
  8.8 0.0 copy-done.1
  8.8 0.0 copy-start
  8.8 0.1 collective-permute-start
  9.5 1.4 %shard_map.92.info_ref = s32[1,128]{1,0:T(1,128)} custom-call(s32[1]{0:T(128)} %bitcast.1.me_ref.refs_0_, s32[1]{0:T(128)} %bitcast.parity_ref.refs_1_, s32[1,32]{1,0:T(1,128)} %bitcast.11, s32[1,32]{1,0:T(1,128)} %bitcast.12, s32[1,32]{1,0:T(1,128)} %bitcast.13, s32[1,32]{1,0:T(1,128)} %bitcast.14, s32[1]{0:T(128)S(6)} %copy.10.refs_6_), custom_call_target="tpu_custom_call" | custom-call | flops 4000000 | bytes 900000 | tf_op jit(solution)/shard_map/pallas_call | solution.py:386
  10.9 0.0 collective-permute-done.partner_ref
  10.9 0.0 copy-done
  10.9 0.3 shard_map.93
  11.2 4.9 %all-to-all-done.mine_ref = f32[8,4,4,256]{3,2,1,0:T(4,128)S(1)} async-done(((f32[8,4,4,256]{3,2,1,0:T(4,128)}), f32[8,4,4,256]{3,2,1,0:T(4,128)S(1)}, u32[]{:S(2)}, u32[]{:S(2)}) %all-to-all-start) | async-done | bytes 131104 | tf_op jit(solution)/shard_map/all_to_all | solution.py:383
  16.1 0.0 copy-start.2
  16.1 0.0 collective-permute-start.1
  16.1 1.3 %collective-permute-done.1.other_ref = f32[8,4,4,256]{3,2,1,0:T(4,128)S(1)} collective-permute-done((f32[8,4,4,256]{3,2,1,0:T(4,128)S(1)}, f32[8,4,4,256]{3,2,1,0:T(4,128)S(1)}, u32[]{:S(2)}, u32[]{:S(2)}) %collective-permute-start.1) | collective-permute-done | bytes 131104 | tf_op jit(solution)/shard_map/ppermute | solution.py:411
  17.5 0.0 copy-done.2
  17.5 4.9 %shard_map.94 = f32[8,4,2,384]{3,2,1,0:T(2,128)S(1)} custom-call(s32[1,128]{1,0:T(1,128)S(1)} %copy-done.2, f32[4,3,128,128]{3,2,1,0:T(8,128)S(1)} %get-tuple-element.12.centre_ref, bf16[4,128,56]{2,1,0:T(8,128)(2,1)S(1)} %get-tuple-element.13.left_ref, f32[8,4,4,256]{3,2,1,0:T(4,128)S(1)} %all-to-all-done.mine_ref, ...), custom_call_target="tpu_custom_call" | custom-call | tf_op jit(solution)/shard_map/pallas_call | solution.py:412
  22.4 9.9 %all_to_all.10.got_ref = f32[32,2,384]{2,1,0:T(2,128)S(1)} all-to-all(f32[32,2,384]{2,1,0:T(2,128)S(1)} %bitcast.8), channel_id=1, replica_groups=mesh['tiles'=8,'far'=4] {'tiles','far'}, dimensions={0} | all-to-all | bytes 196608 | tf_op jit(solution)/shard_map/all_to_all | solution.py:427
  32.3 0.1 shard_map.95.mine_ref
  32.3 0.2 collective-permute-start.2
  32.5 1.0 %collective-permute-done.2.other_ref = f32[2,384]{1,0:T(2,128)S(1)} collective-permute-done((f32[2,384]{1,0:T(2,128)S(1)}, f32[2,384]{1,0:T(2,128)S(1)}, u32[]{:S(2)}, u32[]{:S(2)}) %collective-permute-start.2) | collective-permute-done | bytes 3104 | tf_op jit(solution)/shard_map/ppermute | solution.py:433
  33.6 0.6 %shard_map.96 = f32[3,512]{1,0:T(4,128)} custom-call(s32[1]{0:T(128)} %bitcast.parity_ref.refs_1_, f32[2,384]{1,0:T(2,128)S(1)} %shard_map.95.mine_ref, f32[2,384]{1,0:T(2,128)S(1)} %collective-permute-done.2.other_ref), custom_call_target="tpu_custom_call" | custom-call | tf_op jit(solution)/shard_map/pallas_call | solution.py:434
Async XLA Ops:
  1.4 7.4 %copy-start.1 = (bf16[4,4,128]{2,1,0:T(4,128)(2,1)S(1)}, bf16[4,4,128]{2,1,0:T(4,128)(2,1)}, u32[]{:S(2)}) copy-start(bf16[4,4,128]{2,1,0:T(4,128)(2,1)} %adjoint_ref.1) | copy-start | bytes 12292
  1.4 14.7 %all-to-all-start = ((f32[8,4,4,256]{3,2,1,0:T(4,128)}), f32[8,4,4,256]{3,2,1,0:T(4,128)S(1)}, u32[]{:S(2)}, u32[]{:S(2)}) async-start(f32[8,4,4,256]{3,2,1,0:T(4,128)} %shard_map.91), calls=%async_computation | async-start | bytes 262144 | tf_op jit(solution)/shard_map/all_to_all | solution.py:383
  8.8 2.1 %copy-start = (f32[4,6,128]{2,0,1:T(4,128)S(1)}, f32[4,6,128]{2,0,1:T(4,128)}, u32[]{:S(2)}) copy-start(f32[4,6,128]{2,0,1:T(4,128)} %param.9) | copy-start | bytes 36868
  8.8 2.1 %collective-permute-start = (bf16[4,4,128]{2,1,0:T(4,128)(2,1)S(1)}, bf16[4,4,128]{2,1,0:T(4,128)(2,1)S(1)}, u32[]{:S(2)}, u32[]{:S(2)}) collective-permute-start(bf16[4,4,128]{2,1,0:T(4,128)(2,1)S(1)} %copy-done.1), channel_id=1, source_target_pairs={{1,0},{0,1},{3,2},{2,3},{5,4},{4,5},{7,6},{6,7},{9,8},{8,9},{11,10... | collective-permute-start | bytes 12296 | tf_op jit(solution)/shard_map/ppermute | solution.py:384
  16.1 1.4 %copy-start.2 = (s32[1,128]{1,0:T(1,128)S(1)}, s32[1,128]{1,0:T(1,128)}, u32[]{:S(2)}) copy-start(s32[1,128]{1,0:T(1,128)} %shard_map.92.info_ref) | copy-start | bytes 1540
  16.1 1.3 %collective-permute-start.1 = (f32[8,4,4,256]{3,2,1,0:T(4,128)S(1)}, f32[8,4,4,256]{3,2,1,0:T(4,128)S(1)}, u32[]{:S(2)}, u32[]{:S(2)}) collective-permute-start(f32[8,4,4,256]{3,2,1,0:T(4,128)S(1)} %all-to-all-done.mine_ref), channel_id=1, source_target_pairs={{1,0},{0,1},{3,2},{2,3},{5,4},{4,5},{7,6},{6,7},{9,8},{8,9},{11,10... | collective-permute-start | bytes 393224 | tf_op jit(solution)/shard_map/ppermute | solution.py:411
  32.3 1.2 %collective-permute-start.2 = (f32[2,384]{1,0:T(2,128)S(1)}, f32[2,384]{1,0:T(2,128)S(1)}, u32[]{:S(2)}, u32[]{:S(2)}) collective-permute-start(f32[2,384]{1,0:T(2,128)S(1)} %shard_map.95.mine_ref), channel_id=1, source_target_pairs={{1,0},{0,1},{3,2},{2,3},{5,4},{4,5},{7,6},{6,7},{9,8},{8,9},{11,10... | collective-permute-start | bytes 9224 | tf_op jit(solution)/shard_map/ppermute | solution.py:433

commit v4 on v2

--- a/solution.py
+++ b/solution.py
@@ -10,7 +10,6 @@
 LANES = 128
 HEAD = 5
 SPARE = 2
-GROUP = 32
 LIMIT = 48 * 1024 * 1024
 
 
@@ -154,7 +153,7 @@
         outer = inner >> bits
         return inner & (blocks - 1), outer >> bits, outer & (blocks - 1), word & 3
 
-    def multiply(k, slot):
+    def multiply(k, slot, nodes):
         target, owner, source, order = read(k)
         third = order == 3
         alive = jnp.where(order > 0, 1.0, 0.0).astype(jnp.float32)
@@ -172,13 +171,13 @@
         extent = jnp.where(inside, jnp.concatenate([extent, blank], axis=0), 0.0)
         values = [ref[owner, source, :, 0:width] * alive for ref in (mine_ref, other_ref)]
         empty = jnp.zeros((8, width), jnp.float32)
-        nodes = (
-            (point, scale_mid, floor_mid),
+        quadrature = (
             (point + extent, scale_side, floor_side),
             (point - extent, scale_side, floor_side),
+            (point, scale_mid, floor_mid),
         )
         columns = []
-        for node, scale, floor in nodes:
+        for node, scale, floor in quadrature[:nodes]:
             norm = jnp.sum(node * node, axis=0, keepdims=True) * scale + floor
             rows = jnp.where(
                 row_ids == 3,
@@ -187,8 +186,8 @@
             )
             p1, p2, p3 = split3(rows)
             columns.append(jnp.concatenate([p1, p2, p3, p1, p2, p1, empty], axis=0))
-        columns.append(jnp.concatenate([empty] * 6 + values, axis=0))
-        product_ref[slot] = jnp.dot(
+        columns.insert(1, jnp.concatenate([empty] * 6 + values, axis=0))
+        product_ref[slot, :, 0 : (nodes + 1) * width] = jnp.dot(
             left_ref[target],
             jnp.concatenate(columns, axis=1).astype(jnp.bfloat16),
             preferred_element_type=jnp.float32,
@@ -197,35 +196,36 @@
     def one_pair(k, slot, nodes):
         target, owner, source, order = read(k)
         reach = reach_of(order)
-        point = [shape_ref[owner, 2 * source, c : c + 1] for c in range(3)]
-        extent = [shape_ref[owner, 2 * source + 1, c : c + 1] * reach for c in range(3)]
-        columns = [jnp.zeros((8, width), jnp.float32) for _ in range(3)]
-        for start in range(0, width, GROUP):
-            rows = slice(start, start + GROUP)
+        eight = (8, width)
+        point = [jnp.broadcast_to(shape_ref[owner, 2 * source, c : c + 1], eight) for c in range(3)]
+        extent = [
+            jnp.broadcast_to(shape_ref[owner, 2 * source + 1, c : c + 1], eight) * reach
+            for c in range(3)
+        ]
+        columns = [jnp.zeros(eight, jnp.float32) for _ in range(3)]
+        for start in range(0, width, 8):
+            rows = slice(start, start + 8)
             sums = [row_acc[target, c, rows] for c in range(3)]
 
-            def cubed(node):
-                i = lax.rsqrt(product_ref[slot, rows, node * width : (node + 1) * width])
+            def cubed(part):
+                i = lax.rsqrt(product_ref[slot, rows, part * width : (part + 1) * width])
                 return i * i * i
 
-            coupling = product_ref[slot, rows, 3 * width : 4 * width]
-            f_plus = cubed(1)
+            coupling = product_ref[slot, rows, width : 2 * width]
+            f_plus = cubed(0)
             if nodes == 1:
                 even = (coupling + coupling) * f_plus
             else:
                 f_minus = cubed(2)
                 both = f_plus + f_minus
-                even = coupling * (both + cubed(0) if nodes == 3 else both)
+                even = coupling * (both + cubed(3) if nodes == 3 else both)
                 odd = coupling * (f_plus - f_minus)
             for c in range(3):
                 pulled = even * (centre_ref[target, c, rows] - point[c])
                 if nodes > 1:
                     pulled = pulled - odd * extent[c]
-                sums[c] = sums[c] + pulled
-                for r in range(0, GROUP, 8):
-                    columns[c] = columns[c] + pulled[r : r + 8]
-            for c in range(3):
-                row_acc[target, c, rows] = sums[c]
+                columns[c] = columns[c] + pulled
+                row_acc[target, c, rows] = sums[c] + pulled
         for c in range(3):
             sums_ref[slot, c : c + 1] = jnp.sum(columns[c], axis=0, keepdims=True)
 
@@ -249,9 +249,10 @@
             grad = wide(sums_ref[slot, c : c + 1])
             upper = grad.astype(jnp.bfloat16)
             spread += [upper, (grad - upper.astype(jnp.float32)).astype(jnp.bfloat16)]
-        parts = []
-        hots = []
+        result = None
         for half in range(2):
+            parts = []
+            hots = []
             code = wide(shape_ref[tile, 2 * b + half, 3:4]).astype(jnp.int32)
             for place in (code >> shift, code & ((1 << shift) - 1)):
                 mask = key_ids == narrow(place >> 7)
@@ -266,12 +267,13 @@
                         axis=0,
                     )
                 )
-        result = lax.dot_general(
-            jnp.concatenate(parts, axis=1),
-            jnp.concatenate(hots, axis=1),
-            (((1,), (1,)), ((), ())),
-            preferred_element_type=jnp.float32,
-        )
+            product = lax.dot_general(
+                jnp.concatenate(parts, axis=1),
+                jnp.concatenate(hots, axis=1),
+                (((1,), (1,)), ((), ())),
+                preferred_element_type=jnp.float32,
+            )
+            result = product if result is None else result + product
         before = [joined_ref[tile, c] for c in range(3)]
         for c in range(3):
             joined_ref[tile, c] = (
@@ -288,14 +290,14 @@
         def body(step, carry):
             for slot in range(2):
                 k = 2 * step + slot
-                multiply(k + 1, 1 - slot)
+                multiply(k + 1, 1 - slot, nodes)
                 scatter_pair(k - 1, 1 - slot)
                 one_pair(k, slot, nodes)
             return carry
 
         return body
 
-    multiply(0, 0)
+    multiply(0, 0, 3)
     lax.fori_loop(0, info_ref[0, 1], two_pairs(3), 0)
     lax.fori_loop(info_ref[0, 1], info_ref[0, 2], two_pairs(2), 0)
     lax.fori_loop(info_ref[0, 2], info_ref[0, 3], two_pairs(1), 0)

time: 33.6 us -> 33.4 us (level)
  Pallas kernels: 7.86 us -> 7.07 us
  blocking collectives: 9.68 us -> 10.4 us
    pallas_call x1, Pallas kernels: 4.11 us -> 3.31 us  [per_device(): pl.pallas_call(pair_kernel, out_shape=jax.ShapeDtypeStruct((tiles, far, h...]
    all_to_all x1, blocking collectives: 9.68 us -> 10.4 us  [per_device(): lax.all_to_all(partial, ('tiles', 'far'), split_axis=0, concat_axis=0, ti...]
where the time goes in v4:
time: 33.4 us; the launch traced here: 33.1 us
  blocking collectives  10.4 us (31%)
  starting transfers between devices  7.64 us (23%)
  waiting for transfers between devices  7.3 us (22%)
  Pallas kernels  7.07 us (21%)
  between operations  0.69 us (2%)
    all_to_all x1, blocking collectives, per_device(): lax.all_to_all(partial, ('tiles', 'far'), split_axis=0, concat_axis=0, ti...  10.4 us
    all_to_all x1, starting transfers between devices, per_device(): lax.all_to_all(packed, 'tiles', split_axis=0, concat_axis=0, tiled=True)  7.38 us
    all_to_all x1, waiting for transfers between devices, per_device(): lax.all_to_all(packed, 'tiles', split_axis=0, concat_axis=0, tiled=True)  4.9 us
    pallas_call x1, Pallas kernels, per_device(): pl.pallas_call(pair_kernel, out_shape=jax.ShapeDtypeStruct((tiles, far, h...  3.31 us
    pallas_call x1, Pallas kernels, per_device(): pl.pallas_call(pack_kernel, out_shape=jax.ShapeDtypeStruct((tiles, blocks...  1.41 us
    pallas_call x1, Pallas kernels, per_device(): pl.pallas_call(lambda *refs: sort_kernel(*refs[:-1], blocks, refs[-1]), o...  1.37 us
    ppermute x1, waiting for transfers between devices, per_device(): other = lax.ppermute(got, 'far', swap)  1.35 us
    ppermute x1, waiting for transfers between devices, per_device(): other = lax.ppermute(mine, 'far', swap)  1.05 us
  transfers between devices with their start and end apart: 4, of which 3 were waited for; matrix products, arithmetic and copies ran while one was open for 0% of the time, Pallas kernels for 5%

profile of v4, /device:TPU:0, one launch (start us, length us, event | category | flops | bytes accessed | tf_op | source)
XLA Modules:
  0.0 33.1 jit_solution(1893006656616274872)
XLA Ops:
  0.0 1.4 %shard_map.91 = f32[8,4,4,256]{3,2,1,0:T(4,128)} custom-call(s32[1]{0:T(128)} %bitcast.1.me_ref.refs_0_, s32[1]{0:T(128)} %bitcast.parity_ref.refs_1_, f32[6,4,128]{2,1,0:T(4,128)} %bitcast.9, bf16[4,4,128]{2,1,0:T(4,128)(2,1)} %strength_ref.1, s32[4,4,128]{2,1,0:T(4,128)} %corner_ref.1), custom_call_target="tpu_custom_call" | custom-call | tf_op jit(solution)/shard_map/pallas_call | solution.py:371
  1.4 0.0 copy-start.1
  1.4 7.4 %all-to-all-start = ((f32[8,4,4,256]{3,2,1,0:T(4,128)}), f32[8,4,4,256]{3,2,1,0:T(4,128)S(1)}, u32[]{:S(2)}, u32[]{:S(2)}) async-start(f32[8,4,4,256]{3,2,1,0:T(4,128)} %shard_map.91), calls=%async_computation | async-start | bytes 262144 | tf_op jit(solution)/shard_map/all_to_all | solution.py:377
  8.8 0.0 copy-done.1
  8.8 0.0 copy-start
  8.8 0.1 collective-permute-start
  9.5 1.4 %shard_map.92.info_ref = s32[1,128]{1,0:T(1,128)} custom-call(s32[1]{0:T(128)} %bitcast.1.me_ref.refs_0_, s32[1]{0:T(128)} %bitcast.parity_ref.refs_1_, s32[1,32]{1,0:T(1,128)} %bitcast.11, s32[1,32]{1,0:T(1,128)} %bitcast.12, s32[1,32]{1,0:T(1,128)} %bitcast.13, s32[1,32]{1,0:T(1,128)} %bitcast.14, s32[1]{0:T(128)S(6)} %copy.10.refs_6_), custom_call_target="tpu_custom_call" | custom-call | flops 4000000 | bytes 900000 | tf_op jit(solution)/shard_map/pallas_call | solution.py:380
  10.9 0.0 collective-permute-done.partner_ref
  10.9 0.0 copy-done
  10.9 0.3 shard_map.93
  11.2 4.9 %all-to-all-done.mine_ref = f32[8,4,4,256]{3,2,1,0:T(4,128)S(1)} async-done(((f32[8,4,4,256]{3,2,1,0:T(4,128)}), f32[8,4,4,256]{3,2,1,0:T(4,128)S(1)}, u32[]{:S(2)}, u32[]{:S(2)}) %all-to-all-start) | async-done | bytes 131104 | tf_op jit(solution)/shard_map/all_to_all | solution.py:377
  16.1 0.0 copy-start.2
  16.1 0.0 collective-permute-start.1
  16.1 1.3 %collective-permute-done.1.other_ref = f32[8,4,4,256]{3,2,1,0:T(4,128)S(1)} collective-permute-done((f32[8,4,4,256]{3,2,1,0:T(4,128)S(1)}, f32[8,4,4,256]{3,2,1,0:T(4,128)S(1)}, u32[]{:S(2)}, u32[]{:S(2)}) %collective-permute-start.1) | collective-permute-done | bytes 131104 | tf_op jit(solution)/shard_map/ppermute | solution.py:405
  17.5 0.0 copy-done.2
  17.5 3.3 %shard_map.94 = f32[8,4,2,384]{3,2,1,0:T(2,128)S(1)} custom-call(s32[1,128]{1,0:T(1,128)S(1)} %copy-done.2, f32[4,3,128,128]{3,2,1,0:T(8,128)S(1)} %get-tuple-element.12.centre_ref, bf16[4,128,56]{2,1,0:T(8,128)(2,1)S(1)} %get-tuple-element.13.left_ref, f32[8,4,4,256]{3,2,1,0:T(4,128)S(1)} %all-to-all-done.mine_ref, ...), custom_call_target="tpu_custom_call" | custom-call | tf_op jit(solution)/shard_map/pallas_call | solution.py:406
  20.8 10.4 %all_to_all.10.got_ref = f32[32,2,384]{2,1,0:T(2,128)S(1)} all-to-all(f32[32,2,384]{2,1,0:T(2,128)S(1)} %bitcast.8), channel_id=1, replica_groups=mesh['tiles'=8,'far'=4] {'tiles','far'}, dimensions={0} | all-to-all | bytes 196608 | tf_op jit(solution)/shard_map/all_to_all | solution.py:421
  31.2 0.1 shard_map.95.mine_ref
  31.2 0.2 collective-permute-start.2
  31.4 1.0 %collective-permute-done.2.other_ref = f32[2,384]{1,0:T(2,128)S(1)} collective-permute-done((f32[2,384]{1,0:T(2,128)S(1)}, f32[2,384]{1,0:T(2,128)S(1)}, u32[]{:S(2)}, u32[]{:S(2)}) %collective-permute-start.2) | collective-permute-done | bytes 3104 | tf_op jit(solution)/shard_map/ppermute | solution.py:427
  32.5 0.6 %shard_map.96 = f32[3,512]{1,0:T(4,128)} custom-call(s32[1]{0:T(128)} %bitcast.parity_ref.refs_1_, f32[2,384]{1,0:T(2,128)S(1)} %shard_map.95.mine_ref, f32[2,384]{1,0:T(2,128)S(1)} %collective-permute-done.2.other_ref), custom_call_target="tpu_custom_call" | custom-call | tf_op jit(solution)/shard_map/pallas_call | solution.py:428
Async XLA Ops:
  1.4 7.4 %copy-start.1 = (bf16[4,4,128]{2,1,0:T(4,128)(2,1)S(1)}, bf16[4,4,128]{2,1,0:T(4,128)(2,1)}, u32[]{:S(2)}) copy-start(bf16[4,4,128]{2,1,0:T(4,128)(2,1)} %adjoint_ref.1) | copy-start | bytes 12292
  1.4 14.7 %all-to-all-start = ((f32[8,4,4,256]{3,2,1,0:T(4,128)}), f32[8,4,4,256]{3,2,1,0:T(4,128)S(1)}, u32[]{:S(2)}, u32[]{:S(2)}) async-start(f32[8,4,4,256]{3,2,1,0:T(4,128)} %shard_map.91), calls=%async_computation | async-start | bytes 262144 | tf_op jit(solution)/shard_map/all_to_all | solution.py:377
  8.8 2.1 %copy-start = (f32[4,6,128]{2,0,1:T(4,128)S(1)}, f32[4,6,128]{2,0,1:T(4,128)}, u32[]{:S(2)}) copy-start(f32[4,6,128]{2,0,1:T(4,128)} %param.9) | copy-start | bytes 36868
  8.8 2.1 %collective-permute-start = (bf16[4,4,128]{2,1,0:T(4,128)(2,1)S(1)}, bf16[4,4,128]{2,1,0:T(4,128)(2,1)S(1)}, u32[]{:S(2)}, u32[]{:S(2)}) collective-permute-start(bf16[4,4,128]{2,1,0:T(4,128)(2,1)S(1)} %copy-done.1), channel_id=1, source_target_pairs={{1,0},{0,1},{3,2},{2,3},{5,4},{4,5},{7,6},{6,7},{9,8},{8,9},{11,10... | collective-permute-start | bytes 12296 | tf_op jit(solution)/shard_map/ppermute | solution.py:378
  16.1 1.4 %copy-start.2 = (s32[1,128]{1,0:T(1,128)S(1)}, s32[1,128]{1,0:T(1,128)}, u32[]{:S(2)}) copy-start(s32[1,128]{1,0:T(1,128)} %shard_map.92.info_ref) | copy-start | bytes 1540
  16.1 1.3 %collective-permute-start.1 = (f32[8,4,4,256]{3,2,1,0:T(4,128)S(1)}, f32[8,4,4,256]{3,2,1,0:T(4,128)S(1)}, u32[]{:S(2)}, u32[]{:S(2)}) collective-permute-start(f32[8,4,4,256]{3,2,1,0:T(4,128)S(1)} %all-to-all-done.mine_ref), channel_id=1, source_target_pairs={{1,0},{0,1},{3,2},{2,3},{5,4},{4,5},{7,6},{6,7},{9,8},{8,9},{11,10... | collective-permute-start | bytes 393224 | tf_op jit(solution)/shard_map/ppermute | solution.py:405
  31.2 1.2 %collective-permute-start.2 = (f32[2,384]{1,0:T(2,128)S(1)}, f32[2,384]{1,0:T(2,128)S(1)}, u32[]{:S(2)}, u32[]{:S(2)}) collective-permute-start(f32[2,384]{1,0:T(2,128)S(1)} %shard_map.95.mine_ref), channel_id=1, source_target_pairs={{1,0},{0,1},{3,2},{2,3},{5,4},{4,5},{7,6},{6,7},{9,8},{8,9},{11,10... | collective-permute-start | bytes 9224 | tf_op jit(solution)/shard_map/ppermute | solution.py:427

commit v5 on v4

--- a/solution.py
+++ b/solution.py
@@ -9,7 +9,8 @@
 VMEM = pltpu.VMEM
 LANES = 128
 HEAD = 5
-SPARE = 2
+RING = 4
+AHEAD = 2
 LIMIT = 48 * 1024 * 1024
 
 
@@ -89,7 +90,8 @@
     for i in range(3):
         upto = jnp.where(live & (order >= 3 - i), 1.0, 0.0)
         total = jnp.sum(upto, axis=1, keepdims=True).astype(jnp.int32)
-        info = jnp.where(lane == i + 1, (((total + 1 - parity) >> 1) + 1) >> 1, info)
+        steps = (((total + 1 - parity) >> 1) + RING - 1) // RING
+        info = jnp.where(lane == i + 1, steps, info)
     info_ref[...] = info
 
 
@@ -286,31 +288,32 @@
         _, owner, source, _ = read(k)
         scatter(owner, source, slot)
 
-    def two_pairs(nodes):
+    def some_pairs(nodes):
         def body(step, carry):
-            for slot in range(2):
-                k = 2 * step + slot
-                multiply(k + 1, 1 - slot, nodes)
-                scatter_pair(k - 1, 1 - slot)
+            for slot in range(RING):
+                k = RING * step + slot
+                multiply(k + AHEAD, (slot + AHEAD) % RING, nodes)
+                scatter_pair(k - 1, (slot - 1) % RING)
                 one_pair(k, slot, nodes)
             return carry
 
         return body
 
-    multiply(0, 0, 3)
-    lax.fori_loop(0, info_ref[0, 1], two_pairs(3), 0)
-    lax.fori_loop(info_ref[0, 1], info_ref[0, 2], two_pairs(2), 0)
-    lax.fori_loop(info_ref[0, 2], info_ref[0, 3], two_pairs(1), 0)
-    scatter_pair(2 * info_ref[0, 3] - 1, 1)
+    for k in range(AHEAD):
+        multiply(k, k, 3)
+    lax.fori_loop(0, info_ref[0, 1], some_pairs(3), 0)
+    lax.fori_loop(info_ref[0, 1], info_ref[0, 2], some_pairs(2), 0)
+    lax.fori_loop(info_ref[0, 2], info_ref[0, 3], some_pairs(1), 0)
+    scatter_pair(RING * info_ref[0, 3] - 1, RING - 1)
     for b in range(blocks):
         total = jnp.concatenate(
             [jnp.sum(row_acc[b, c], axis=1, keepdims=True) for c in range(3)]
             + [jnp.zeros((width, 5), jnp.float32)],
             axis=1,
         )
-        sums_ref[2 + b] = -total.T
+        sums_ref[RING + b] = -total.T
     for b in range(blocks):
-        scatter(me, b, 2 + b)
+        scatter(me, b, RING + b)
 
     def collect(dest, carry):
         for c in range(3):
@@ -379,7 +382,7 @@
     pairs = pair_target.shape[0]
     info = pl.pallas_call(
         lambda *refs: sort_kernel(*refs[:-1], blocks, refs[-1]),
-        out_shape=jax.ShapeDtypeStruct((1, -(-(HEAD + pairs // 2 + SPARE + 1) // LANES) * LANES), jnp.int32),
+        out_shape=jax.ShapeDtypeStruct((1, -(-(HEAD + pairs // 2 + 1 + RING + AHEAD) // LANES) * LANES), jnp.int32),
         in_specs=[smem] * 2 + [vmem] * 4 + [smem],
         out_specs=vmem,
         cost_estimate=pl.CostEstimate(flops=4000000, bytes_accessed=900000, transcendentals=0),
@@ -409,9 +412,9 @@
         in_specs=[smem] + [vmem] * 4,
         out_specs=vmem,
         scratch_shapes=[
-            VMEM((2, width, 4 * width), jnp.float32),
+            VMEM((RING, width, 4 * width), jnp.float32),
             VMEM((blocks, 3, width, width), jnp.float32),
-            VMEM((2 + blocks, 8, width), jnp.float32),
+            VMEM((RING + blocks, 8, width), jnp.float32),
             VMEM((tiles, 3, 4 * high, LANES), jnp.float32),
             VMEM((tiles, 2 * blocks, 4, width), jnp.float32),
         ],

time: 33.4 us -> 34 us (1.018)
  Pallas kernels: 7.07 us -> 7.84 us
    pallas_call x1, Pallas kernels: 3.31 us -> 4.09 us  [per_device(): pl.pallas_call(pair_kernel, out_shape=jax.ShapeDtypeStruct((tiles, far, h...]
where the time goes in v5:
time: 34 us; the launch traced here: 33.6 us
  blocking collectives  10.2 us (30%)
  Pallas kernels  7.84 us (23%)
  starting transfers between devices  7.64 us (22%)
  waiting for transfers between devices  7.29 us (21%)
  between operations  0.69 us (2%)
    all_to_all x1, blocking collectives, per_device(): lax.all_to_all(partial, ('tiles', 'far'), split_axis=0, concat_axis=0, ti...  10.2 us
    all_to_all x1, starting transfers between devices, per_device(): lax.all_to_all(packed, 'tiles', split_axis=0, concat_axis=0, tiled=True)  7.38 us
    all_to_all x1, waiting for transfers between devices, per_device(): lax.all_to_all(packed, 'tiles', split_axis=0, concat_axis=0, tiled=True)  4.9 us
    pallas_call x1, Pallas kernels, per_device(): pl.pallas_call(pair_kernel, out_shape=jax.ShapeDtypeStruct((tiles, far, h...  4.09 us
    pallas_call x1, Pallas kernels, per_device(): pl.pallas_call(pack_kernel, out_shape=jax.ShapeDtypeStruct((tiles, blocks...  1.41 us
    pallas_call x1, Pallas kernels, per_device(): pl.pallas_call(lambda *refs: sort_kernel(*refs[:-1], blocks, refs[-1]), o...  1.37 us
    ppermute x1, waiting for transfers between devices, per_device(): other = lax.ppermute(got, 'far', swap)  1.35 us
    ppermute x1, waiting for transfers between devices, per_device(): other = lax.ppermute(mine, 'far', swap)  1.05 us
  transfers between devices with their start and end apart: 4, of which 3 were waited for; matrix products, arithmetic and copies ran while one was open for 0% of the time, Pallas kernels for 5%

profile of v5, /device:TPU:0, one launch (start us, length us, event | category | flops | bytes accessed | tf_op | source)
XLA Modules:
  0.0 33.6 jit_solution(13251541765733345935)
XLA Ops:
  0.0 1.4 %shard_map.91 = f32[8,4,4,256]{3,2,1,0:T(4,128)} custom-call(s32[1]{0:T(128)} %bitcast.1.me_ref.refs_0_, s32[1]{0:T(128)} %bitcast.parity_ref.refs_1_, f32[6,4,128]{2,1,0:T(4,128)} %bitcast.9, bf16[4,4,128]{2,1,0:T(4,128)(2,1)} %strength_ref.1, s32[4,4,128]{2,1,0:T(4,128)} %corner_ref.1), custom_call_target="tpu_custom_call" | custom-call | tf_op jit(solution)/shard_map/pallas_call | solution.py:374
  1.4 0.0 copy-start.1
  1.4 7.4 %all-to-all-start = ((f32[8,4,4,256]{3,2,1,0:T(4,128)}), f32[8,4,4,256]{3,2,1,0:T(4,128)S(1)}, u32[]{:S(2)}, u32[]{:S(2)}) async-start(f32[8,4,4,256]{3,2,1,0:T(4,128)} %shard_map.91), calls=%async_computation | async-start | bytes 262144 | tf_op jit(solution)/shard_map/all_to_all | solution.py:380
  8.8 0.0 copy-done.1
  8.8 0.0 copy-start
  8.8 0.1 collective-permute-start
  9.5 1.4 %shard_map.92.info_ref = s32[1,128]{1,0:T(1,128)} custom-call(s32[1]{0:T(128)} %bitcast.1.me_ref.refs_0_, s32[1]{0:T(128)} %bitcast.parity_ref.refs_1_, s32[1,32]{1,0:T(1,128)} %bitcast.11, s32[1,32]{1,0:T(1,128)} %bitcast.12, s32[1,32]{1,0:T(1,128)} %bitcast.13, s32[1,32]{1,0:T(1,128)} %bitcast.14, s32[1]{0:T(128)S(6)} %copy.10.refs_6_), custom_call_target="tpu_custom_call" | custom-call | flops 4000000 | bytes 900000 | tf_op jit(solution)/shard_map/pallas_call | solution.py:383
  10.9 0.0 collective-permute-done.partner_ref
  10.9 0.0 copy-done
  10.9 0.3 shard_map.93
  11.2 4.9 %all-to-all-done.mine_ref = f32[8,4,4,256]{3,2,1,0:T(4,128)S(1)} async-done(((f32[8,4,4,256]{3,2,1,0:T(4,128)}), f32[8,4,4,256]{3,2,1,0:T(4,128)S(1)}, u32[]{:S(2)}, u32[]{:S(2)}) %all-to-all-start) | async-done | bytes 131104 | tf_op jit(solution)/shard_map/all_to_all | solution.py:380
  16.1 0.0 copy-start.2
  16.1 0.0 collective-permute-start.1
  16.1 1.3 %collective-permute-done.1.other_ref = f32[8,4,4,256]{3,2,1,0:T(4,128)S(1)} collective-permute-done((f32[8,4,4,256]{3,2,1,0:T(4,128)S(1)}, f32[8,4,4,256]{3,2,1,0:T(4,128)S(1)}, u32[]{:S(2)}, u32[]{:S(2)}) %collective-permute-start.1) | collective-permute-done | bytes 131104 | tf_op jit(solution)/shard_map/ppermute | solution.py:408
  17.5 0.0 copy-done.2
  17.5 4.1 %shard_map.94 = f32[8,4,2,384]{3,2,1,0:T(2,128)S(1)} custom-call(s32[1,128]{1,0:T(1,128)S(1)} %copy-done.2, f32[4,3,128,128]{3,2,1,0:T(8,128)S(1)} %get-tuple-element.12.centre_ref, bf16[4,128,56]{2,1,0:T(8,128)(2,1)S(1)} %get-tuple-element.13.left_ref, f32[8,4,4,256]{3,2,1,0:T(4,128)S(1)} %all-to-all-done.mine_ref, ...), custom_call_target="tpu_custom_call" | custom-call | tf_op jit(solution)/shard_map/pallas_call | solution.py:409
  21.6 10.2 %all_to_all.10.got_ref = f32[32,2,384]{2,1,0:T(2,128)S(1)} all-to-all(f32[32,2,384]{2,1,0:T(2,128)S(1)} %bitcast.8), channel_id=1, replica_groups=mesh['tiles'=8,'far'=4] {'tiles','far'}, dimensions={0} | all-to-all | bytes 196608 | tf_op jit(solution)/shard_map/all_to_all | solution.py:424
  31.8 0.1 shard_map.95.mine_ref
  31.8 0.2 collective-permute-start.2
  32.0 1.0 %collective-permute-done.2.other_ref = f32[2,384]{1,0:T(2,128)S(1)} collective-permute-done((f32[2,384]{1,0:T(2,128)S(1)}, f32[2,384]{1,0:T(2,128)S(1)}, u32[]{:S(2)}, u32[]{:S(2)}) %collective-permute-start.2) | collective-permute-done | bytes 3104 | tf_op jit(solution)/shard_map/ppermute | solution.py:430
  33.0 0.6 %shard_map.96 = f32[3,512]{1,0:T(4,128)} custom-call(s32[1]{0:T(128)} %bitcast.parity_ref.refs_1_, f32[2,384]{1,0:T(2,128)S(1)} %shard_map.95.mine_ref, f32[2,384]{1,0:T(2,128)S(1)} %collective-permute-done.2.other_ref), custom_call_target="tpu_custom_call" | custom-call | tf_op jit(solution)/shard_map/pallas_call | solution.py:431
Async XLA Ops:
  1.4 7.4 %copy-start.1 = (bf16[4,4,128]{2,1,0:T(4,128)(2,1)S(1)}, bf16[4,4,128]{2,1,0:T(4,128)(2,1)}, u32[]{:S(2)}) copy-start(bf16[4,4,128]{2,1,0:T(4,128)(2,1)} %adjoint_ref.1) | copy-start | bytes 12292
  1.4 14.7 %all-to-all-start = ((f32[8,4,4,256]{3,2,1,0:T(4,128)}), f32[8,4,4,256]{3,2,1,0:T(4,128)S(1)}, u32[]{:S(2)}, u32[]{:S(2)}) async-start(f32[8,4,4,256]{3,2,1,0:T(4,128)} %shard_map.91), calls=%async_computation | async-start | bytes 262144 | tf_op jit(solution)/shard_map/all_to_all | solution.py:380
  8.8 2.1 %copy-start = (f32[4,6,128]{2,0,1:T(4,128)S(1)}, f32[4,6,128]{2,0,1:T(4,128)}, u32[]{:S(2)}) copy-start(f32[4,6,128]{2,0,1:T(4,128)} %param.9) | copy-start | bytes 36868
  8.8 2.1 %collective-permute-start = (bf16[4,4,128]{2,1,0:T(4,128)(2,1)S(1)}, bf16[4,4,128]{2,1,0:T(4,128)(2,1)S(1)}, u32[]{:S(2)}, u32[]{:S(2)}) collective-permute-start(bf16[4,4,128]{2,1,0:T(4,128)(2,1)S(1)} %copy-done.1), channel_id=1, source_target_pairs={{1,0},{0,1},{3,2},{2,3},{5,4},{4,5},{7,6},{6,7},{9,8},{8,9},{11,10... | collective-permute-start | bytes 12296 | tf_op jit(solution)/shard_map/ppermute | solution.py:381
  16.1 1.4 %copy-start.2 = (s32[1,128]{1,0:T(1,128)S(1)}, s32[1,128]{1,0:T(1,128)}, u32[]{:S(2)}) copy-start(s32[1,128]{1,0:T(1,128)} %shard_map.92.info_ref) | copy-start | bytes 1540
  16.1 1.3 %collective-permute-start.1 = (f32[8,4,4,256]{3,2,1,0:T(4,128)S(1)}, f32[8,4,4,256]{3,2,1,0:T(4,128)S(1)}, u32[]{:S(2)}, u32[]{:S(2)}) collective-permute-start(f32[8,4,4,256]{3,2,1,0:T(4,128)S(1)} %all-to-all-done.mine_ref), channel_id=1, source_target_pairs={{1,0},{0,1},{3,2},{2,3},{5,4},{4,5},{7,6},{6,7},{9,8},{8,9},{11,10... | collective-permute-start | bytes 393224 | tf_op jit(solution)/shard_map/ppermute | solution.py:408
  31.8 1.2 %collective-permute-start.2 = (f32[2,384]{1,0:T(2,128)S(1)}, f32[2,384]{1,0:T(2,128)S(1)}, u32[]{:S(2)}, u32[]{:S(2)}) collective-permute-start(f32[2,384]{1,0:T(2,128)S(1)} %shard_map.95.mine_ref), channel_id=1, source_target_pairs={{1,0},{0,1},{3,2},{2,3},{5,4},{4,5},{7,6},{6,7},{9,8},{8,9},{11,10... | collective-permute-start | bytes 9224 | tf_op jit(solution)/shard_map/ppermute | solution.py:430

commit v6 on v4

--- a/solution.py
+++ b/solution.py
@@ -9,6 +9,9 @@
 VMEM = pltpu.VMEM
 LANES = 128
 HEAD = 5
+SCALE_MID = (4.0 / 9.0 / 512.0) ** (-2.0 / 3.0)
+SCALE_SIDE = (5.0 / 18.0 / 512.0) ** (-2.0 / 3.0)
+SCALE_TWO = (0.5 / 512.0) ** (-2.0 / 3.0)
 SPARE = 2
 LIMIT = 48 * 1024 * 1024
 
@@ -153,41 +156,31 @@
         outer = inner >> bits
         return inner & (blocks - 1), outer >> bits, outer & (blocks - 1), word & 3
 
-    def multiply(k, slot, nodes):
+    def scale_of(order):
+        return jnp.where(order == 3, SCALE_SIDE, SCALE_TWO)
+
+    def multiply(k, slot):
         target, owner, source, order = read(k)
-        third = order == 3
         alive = jnp.where(order > 0, 1.0, 0.0).astype(jnp.float32)
-        reach = reach_of(order)
-        scale_mid = jnp.where(third, (4.0 / 9.0 / 512.0) ** (-2.0 / 3.0), 0.0)
-        scale_side = jnp.where(
-            third, (5.0 / 18.0 / 512.0) ** (-2.0 / 3.0), (0.5 / 512.0) ** (-2.0 / 3.0)
+        scale = scale_of(order)
+        inside = row_ids < 3
+        point = jnp.concatenate([shape_ref[owner, 2 * source], blank], axis=0)
+        extent = jnp.concatenate([shape_ref[owner, 2 * source + 1], blank], axis=0)
+        node = jnp.where(inside, point + extent * reach_of(order), 0.0)
+        norm = (jnp.sum(node * node, axis=0, keepdims=True) + 0.0625) * scale
+        rows = jnp.where(
+            row_ids == 3,
+            norm,
+            jnp.where(row_ids == 4, scale, node * (-2.0 * scale)),
         )
-        floor_mid = jnp.where(third, 0.0625 * (4.0 / 9.0 / 512.0) ** (-2.0 / 3.0), 3.0e38)
-        floor_side = 0.0625 * scale_side
-        point = shape_ref[owner, 2 * source]
-        extent = shape_ref[owner, 2 * source + 1] * reach
-        inside = row_ids < 3
-        point = jnp.where(inside, jnp.concatenate([point, blank], axis=0), 0.0)
-        extent = jnp.where(inside, jnp.concatenate([extent, blank], axis=0), 0.0)
+        p1, p2, p3 = split3(rows)
+        empty = jnp.zeros((8, width), jnp.float32)
         values = [ref[owner, source, :, 0:width] * alive for ref in (mine_ref, other_ref)]
-        empty = jnp.zeros((8, width), jnp.float32)
-        quadrature = (
-            (point + extent, scale_side, floor_side),
-            (point - extent, scale_side, floor_side),
-            (point, scale_mid, floor_mid),
-        )
-        columns = []
-        for node, scale, floor in quadrature[:nodes]:
-            norm = jnp.sum(node * node, axis=0, keepdims=True) * scale + floor
-            rows = jnp.where(
-                row_ids == 3,
-                norm,
-                jnp.where(row_ids == 4, scale, node * (-2.0 * scale)),
-            )
-            p1, p2, p3 = split3(rows)
-            columns.append(jnp.concatenate([p1, p2, p3, p1, p2, p1, empty], axis=0))
-        columns.insert(1, jnp.concatenate([empty] * 6 + values, axis=0))
-        product_ref[slot, :, 0 : (nodes + 1) * width] = jnp.dot(
+        columns = [
+            jnp.concatenate([p1, p2, p3, p1, p2, p1, empty], axis=0),
+            jnp.concatenate([empty] * 6 + values, axis=0),
+        ]
+        product_ref[slot] = jnp.dot(
             left_ref[target],
             jnp.concatenate(columns, axis=1).astype(jnp.bfloat16),
             preferred_element_type=jnp.float32,
@@ -202,26 +195,36 @@
             jnp.broadcast_to(shape_ref[owner, 2 * source + 1, c : c + 1], eight) * reach
             for c in range(3)
         ]
+        gap = [e * (4.0 * scale_of(order)) for e in extent]
+        third = order == 3
+        ratio = jnp.where(third, SCALE_MID / SCALE_SIDE / 2.0, 0.0)
+        drop = extent[0] * extent[0] + extent[1] * extent[1] + extent[2] * extent[2]
+        drop = jnp.where(third, drop * SCALE_MID, -3.0e38)
         columns = [jnp.zeros(eight, jnp.float32) for _ in range(3)]
         for start in range(0, width, 8):
             rows = slice(start, start + 8)
             sums = [row_acc[target, c, rows] for c in range(3)]
-
-            def cubed(part):
-                i = lax.rsqrt(product_ref[slot, rows, part * width : (part + 1) * width])
+            away = [centre_ref[target, c, rows] - point[c] for c in range(3)]
+
+            def cubed(squared):
+                i = lax.rsqrt(squared)
                 return i * i * i
 
+            plus = product_ref[slot, rows, 0:width]
             coupling = product_ref[slot, rows, width : 2 * width]
-            f_plus = cubed(0)
+            f_plus = cubed(plus)
             if nodes == 1:
                 even = (coupling + coupling) * f_plus
             else:
-                f_minus = cubed(2)
-                both = f_plus + f_minus
-                even = coupling * (both + cubed(3) if nodes == 3 else both)
+                minus = plus + (away[0] * gap[0] + away[1] * gap[1] + away[2] * gap[2])
+                f_minus = cubed(minus)
+                total = f_plus + f_minus
+                if nodes == 3:
+                    total = total + cubed((plus + minus) * ratio - drop)
+                even = coupling * total
                 odd = coupling * (f_plus - f_minus)
             for c in range(3):
-                pulled = even * (centre_ref[target, c, rows] - point[c])
+                pulled = even * away[c]
                 if nodes > 1:
                     pulled = pulled - odd * extent[c]
                 columns[c] = columns[c] + pulled
@@ -243,13 +246,12 @@
     def narrow(value):
         return value.astype(jnp.float32).astype(jnp.bfloat16)
 
-    def scatter(tile, b, slot):
+    def spread_out(tile, b, slot, result):
         spread = []
         for c in range(3):
             grad = wide(sums_ref[slot, c : c + 1])
             upper = grad.astype(jnp.bfloat16)
             spread += [upper, (grad - upper.astype(jnp.float32)).astype(jnp.bfloat16)]
-        result = None
         for half in range(2):
             parts = []
             hots = []
@@ -274,6 +276,12 @@
                 preferred_element_type=jnp.float32,
             )
             result = product if result is None else result + product
+        return result
+
+    def scatter(tile, places):
+        result = None
+        for b, slot in places:
+            result = spread_out(tile, b, slot, result)
         before = [joined_ref[tile, c] for c in range(3)]
         for c in range(3):
             joined_ref[tile, c] = (
@@ -284,20 +292,20 @@
 
     def scatter_pair(k, slot):
         _, owner, source, _ = read(k)
-        scatter(owner, source, slot)
+        scatter(owner, [(source, slot)])
 
     def two_pairs(nodes):
         def body(step, carry):
             for slot in range(2):
                 k = 2 * step + slot
-                multiply(k + 1, 1 - slot, nodes)
+                multiply(k + 1, 1 - slot)
                 scatter_pair(k - 1, 1 - slot)
                 one_pair(k, slot, nodes)
             return carry
 
         return body
 
-    multiply(0, 0, 3)
+    multiply(0, 0)
     lax.fori_loop(0, info_ref[0, 1], two_pairs(3), 0)
     lax.fori_loop(info_ref[0, 1], info_ref[0, 2], two_pairs(2), 0)
     lax.fori_loop(info_ref[0, 2], info_ref[0, 3], two_pairs(1), 0)
@@ -309,8 +317,7 @@
             axis=1,
         )
         sums_ref[2 + b] = -total.T
-    for b in range(blocks):
-        scatter(me, b, 2 + b)
+    scatter(me, [(b, 2 + b) for b in range(blocks)])
 
     def collect(dest, carry):
         for c in range(3):
@@ -409,7 +416,7 @@
         in_specs=[smem] + [vmem] * 4,
         out_specs=vmem,
         scratch_shapes=[
-            VMEM((2, width, 4 * width), jnp.float32),
+            VMEM((2, width, 2 * width), jnp.float32),
             VMEM((blocks, 3, width, width), jnp.float32),
             VMEM((2 + blocks, 8, width), jnp.float32),
             VMEM((tiles, 3, 4 * high, LANES), jnp.float32),

time: 33.4 us -> 33.6 us (level)
  blocking collectives: 10.4 us -> 9.74 us
  Pallas kernels: 7.07 us -> 7.67 us
    all_to_all x1, blocking collectives: 10.4 us -> 9.74 us  [per_device(): lax.all_to_all(partial, ('tiles', 'far'), split_axis=0, concat_axis=0, ti...]
    pallas_call x1, Pallas kernels: 3.31 us -> 3.92 us  [per_device(): pl.pallas_call(pair_kernel, out_shape=jax.ShapeDtypeStruct((tiles, far, h...]
where the time goes in v6:
time: 33.6 us; the launch traced here: 33 us
  blocking collectives  9.74 us (29%)
  Pallas kernels  7.67 us (23%)
  starting transfers between devices  7.64 us (23%)
  waiting for transfers between devices  7.3 us (22%)
  between operations  0.69 us (2%)
    all_to_all x1, blocking collectives, per_device(): lax.all_to_all(partial, ('tiles', 'far'), split_axis=0, concat_axis=0, ti...  9.74 us
    all_to_all x1, starting transfers between devices, per_device(): lax.all_to_all(packed, 'tiles', split_axis=0, concat_axis=0, tiled=True)  7.38 us
    all_to_all x1, waiting for transfers between devices, per_device(): lax.all_to_all(packed, 'tiles', split_axis=0, concat_axis=0, tiled=True)  4.9 us
    pallas_call x1, Pallas kernels, per_device(): pl.pallas_call(pair_kernel, out_shape=jax.ShapeDtypeStruct((tiles, far, h...  3.92 us
    pallas_call x1, Pallas kernels, per_device(): pl.pallas_call(pack_kernel, out_shape=jax.ShapeDtypeStruct((tiles, blocks...  1.41 us
    pallas_call x1, Pallas kernels, per_device(): pl.pallas_call(lambda *refs: sort_kernel(*refs[:-1], blocks, refs[-1]), o...  1.37 us
    ppermute x1, waiting for transfers between devices, per_device(): other = lax.ppermute(got, 'far', swap)  1.35 us
    ppermute x1, waiting for transfers between devices, per_device(): other = lax.ppermute(mine, 'far', swap)  1.05 us
  transfers between devices with their start and end apart: 4, of which 3 were waited for; matrix products, arithmetic and copies ran while one was open for 0% of the time, Pallas kernels for 5%

profile of v6, /device:TPU:0, one launch (start us, length us, event | category | flops | bytes accessed | tf_op | source)
XLA Modules:
  0.0 33.0 jit_solution(13442832242728212096)
XLA Ops:
  0.0 1.4 %shard_map.91 = f32[8,4,4,256]{3,2,1,0:T(4,128)} custom-call(s32[1]{0:T(128)} %bitcast.1.me_ref.refs_0_, s32[1]{0:T(128)} %bitcast.parity_ref.refs_1_, f32[6,4,128]{2,1,0:T(4,128)} %bitcast.9, bf16[4,4,128]{2,1,0:T(4,128)(2,1)} %strength_ref.1, s32[4,4,128]{2,1,0:T(4,128)} %corner_ref.1), custom_call_target="tpu_custom_call" | custom-call | tf_op jit(solution)/shard_map/pallas_call | solution.py:378
  1.4 0.0 copy-start.1
  1.4 7.4 %all-to-all-start = ((f32[8,4,4,256]{3,2,1,0:T(4,128)}), f32[8,4,4,256]{3,2,1,0:T(4,128)S(1)}, u32[]{:S(2)}, u32[]{:S(2)}) async-start(f32[8,4,4,256]{3,2,1,0:T(4,128)} %shard_map.91), calls=%async_computation | async-start | bytes 262144 | tf_op jit(solution)/shard_map/all_to_all | solution.py:384
  8.8 0.0 copy-done.1
  8.8 0.0 copy-start
  8.8 0.1 collective-permute-start
  9.5 1.4 %shard_map.92.info_ref = s32[1,128]{1,0:T(1,128)} custom-call(s32[1]{0:T(128)} %bitcast.1.me_ref.refs_0_, s32[1]{0:T(128)} %bitcast.parity_ref.refs_1_, s32[1,32]{1,0:T(1,128)} %bitcast.11, s32[1,32]{1,0:T(1,128)} %bitcast.12, s32[1,32]{1,0:T(1,128)} %bitcast.13, s32[1,32]{1,0:T(1,128)} %bitcast.14, s32[1]{0:T(128)S(6)} %copy.10.refs_6_), custom_call_target="tpu_custom_call" | custom-call | flops 4000000 | bytes 900000 | tf_op jit(solution)/shard_map/pallas_call | solution.py:387
  10.9 0.0 collective-permute-done.partner_ref
  10.9 0.0 copy-done
  10.9 0.3 shard_map.93
  11.2 4.9 %all-to-all-done.mine_ref = f32[8,4,4,256]{3,2,1,0:T(4,128)S(1)} async-done(((f32[8,4,4,256]{3,2,1,0:T(4,128)}), f32[8,4,4,256]{3,2,1,0:T(4,128)S(1)}, u32[]{:S(2)}, u32[]{:S(2)}) %all-to-all-start) | async-done | bytes 131104 | tf_op jit(solution)/shard_map/all_to_all | solution.py:384
  16.1 0.0 copy-start.2
  16.1 0.0 collective-permute-start.1
  16.1 1.3 %collective-permute-done.1.other_ref = f32[8,4,4,256]{3,2,1,0:T(4,128)S(1)} collective-permute-done((f32[8,4,4,256]{3,2,1,0:T(4,128)S(1)}, f32[8,4,4,256]{3,2,1,0:T(4,128)S(1)}, u32[]{:S(2)}, u32[]{:S(2)}) %collective-permute-start.1) | collective-permute-done | bytes 131104 | tf_op jit(solution)/shard_map/ppermute | solution.py:412
  17.5 0.0 copy-done.2
  17.5 3.9 %shard_map.94 = f32[8,4,2,384]{3,2,1,0:T(2,128)S(1)} custom-call(s32[1,128]{1,0:T(1,128)S(1)} %copy-done.2, f32[4,3,128,128]{3,2,1,0:T(8,128)S(1)} %get-tuple-element.12.centre_ref, bf16[4,128,56]{2,1,0:T(8,128)(2,1)S(1)} %get-tuple-element.13.left_ref, f32[8,4,4,256]{3,2,1,0:T(4,128)S(1)} %all-to-all-done.mine_ref, ...), custom_call_target="tpu_custom_call" | custom-call | tf_op jit(solution)/shard_map/pallas_call | solution.py:413
  21.4 9.7 %all_to_all.10.got_ref = f32[32,2,384]{2,1,0:T(2,128)S(1)} all-to-all(f32[32,2,384]{2,1,0:T(2,128)S(1)} %bitcast.8), channel_id=1, replica_groups=mesh['tiles'=8,'far'=4] {'tiles','far'}, dimensions={0} | all-to-all | bytes 196608 | tf_op jit(solution)/shard_map/all_to_all | solution.py:428
  31.2 0.1 shard_map.95.mine_ref
  31.2 0.2 collective-permute-start.2
  31.4 1.0 %collective-permute-done.2.other_ref = f32[2,384]{1,0:T(2,128)S(1)} collective-permute-done((f32[2,384]{1,0:T(2,128)S(1)}, f32[2,384]{1,0:T(2,128)S(1)}, u32[]{:S(2)}, u32[]{:S(2)}) %collective-permute-start.2) | collective-permute-done | bytes 3104 | tf_op jit(solution)/shard_map/ppermute | solution.py:434
  32.4 0.6 %shard_map.96 = f32[3,512]{1,0:T(4,128)} custom-call(s32[1]{0:T(128)} %bitcast.parity_ref.refs_1_, f32[2,384]{1,0:T(2,128)S(1)} %shard_map.95.mine_ref, f32[2,384]{1,0:T(2,128)S(1)} %collective-permute-done.2.other_ref), custom_call_target="tpu_custom_call" | custom-call | tf_op jit(solution)/shard_map/pallas_call | solution.py:435
Async XLA Ops:
  1.4 7.4 %copy-start.1 = (bf16[4,4,128]{2,1,0:T(4,128)(2,1)S(1)}, bf16[4,4,128]{2,1,0:T(4,128)(2,1)}, u32[]{:S(2)}) copy-start(bf16[4,4,128]{2,1,0:T(4,128)(2,1)} %adjoint_ref.1) | copy-start | bytes 12292
  1.4 14.7 %all-to-all-start = ((f32[8,4,4,256]{3,2,1,0:T(4,128)}), f32[8,4,4,256]{3,2,1,0:T(4,128)S(1)}, u32[]{:S(2)}, u32[]{:S(2)}) async-start(f32[8,4,4,256]{3,2,1,0:T(4,128)} %shard_map.91), calls=%async_computation | async-start | bytes 262144 | tf_op jit(solution)/shard_map/all_to_all | solution.py:384
  8.8 2.1 %copy-start = (f32[4,6,128]{2,0,1:T(4,128)S(1)}, f32[4,6,128]{2,0,1:T(4,128)}, u32[]{:S(2)}) copy-start(f32[4,6,128]{2,0,1:T(4,128)} %param.9) | copy-start | bytes 36868
  8.8 2.1 %collective-permute-start = (bf16[4,4,128]{2,1,0:T(4,128)(2,1)S(1)}, bf16[4,4,128]{2,1,0:T(4,128)(2,1)S(1)}, u32[]{:S(2)}, u32[]{:S(2)}) collective-permute-start(bf16[4,4,128]{2,1,0:T(4,128)(2,1)S(1)} %copy-done.1), channel_id=1, source_target_pairs={{1,0},{0,1},{3,2},{2,3},{5,4},{4,5},{7,6},{6,7},{9,8},{8,9},{11,10... | collective-permute-start | bytes 12296 | tf_op jit(solution)/shard_map/ppermute | solution.py:385
  16.1 1.4 %copy-start.2 = (s32[1,128]{1,0:T(1,128)S(1)}, s32[1,128]{1,0:T(1,128)}, u32[]{:S(2)}) copy-start(s32[1,128]{1,0:T(1,128)} %shard_map.92.info_ref) | copy-start | bytes 1540
  16.1 1.3 %collective-permute-start.1 = (f32[8,4,4,256]{3,2,1,0:T(4,128)S(1)}, f32[8,4,4,256]{3,2,1,0:T(4,128)S(1)}, u32[]{:S(2)}, u32[]{:S(2)}) collective-permute-start(f32[8,4,4,256]{3,2,1,0:T(4,128)S(1)} %all-to-all-done.mine_ref), channel_id=1, source_target_pairs={{1,0},{0,1},{3,2},{2,3},{5,4},{4,5},{7,6},{6,7},{9,8},{8,9},{11,10... | collective-permute-start | bytes 393224 | tf_op jit(solution)/shard_map/ppermute | solution.py:412
  31.2 1.2 %collective-permute-start.2 = (f32[2,384]{1,0:T(2,128)S(1)}, f32[2,384]{1,0:T(2,128)S(1)}, u32[]{:S(2)}, u32[]{:S(2)}) collective-permute-start(f32[2,384]{1,0:T(2,128)S(1)} %shard_map.95.mine_ref), channel_id=1, source_target_pairs={{1,0},{0,1},{3,2},{2,3},{5,4},{4,5},{7,6},{6,7},{9,8},{8,9},{11,10... | collective-permute-start | bytes 9224 | tf_op jit(solution)/shard_map/ppermute | solution.py:434

commit v7 on v6

--- a/solution.py
+++ b/solution.py
@@ -374,6 +374,8 @@
     smem = pl.BlockSpec(memory_space=SMEM)
     vmem = pl.BlockSpec(memory_space=VMEM)
     params = pltpu.CompilerParams(vmem_limit_bytes=LIMIT)
+    partner = lax.ppermute(adjoint, "far", swap)
+    panel_geometry, partner = lax.optimization_barrier((panel_geometry, partner))
     geometry = panel_geometry.transpose(1, 0, 2)
     packed = pl.pallas_call(
         pack_kernel,
@@ -382,7 +384,6 @@
         out_specs=vmem,
     )(me, parity, geometry, strengths, corner_vertex)
     got = lax.all_to_all(packed, "tiles", split_axis=0, concat_axis=0, tiled=True)
-    partner = lax.ppermute(adjoint, "far", swap)
     pairs = pair_target.shape[0]
     info = pl.pallas_call(
         lambda *refs: sort_kernel(*refs[:-1], blocks, refs[-1]),

time: 33.6 us -> 35.1 us (1.045)
  waiting for transfers between devices: 7.3 us -> 8.39 us
  blocking collectives: 9.74 us -> 10.3 us
    ppermute x1, waiting for transfers between devices: 0.01 us -> 1.03 us  [per_device(): partner = lax.ppermute(adjoint, 'far', swap)]
    all_to_all x1, blocking collectives: 9.74 us -> 10.3 us  [per_device(): lax.all_to_all(partial, ('tiles', 'far'), split_axis=0, concat_axis=0, ti...]
    ppermute x1, starting transfers between devices: 0.07 us -> 0.45 us  [per_device(): partner = lax.ppermute(adjoint, 'far', swap)]
  transfers between devices with their start and end apart: 4 -> 4, of which waited for: 3 -> 4; matrix products, arithmetic and copies ran while one was open for 0% -> 0% of each run, Pallas kernels for 5% -> 5%
where the time goes in v7:
time: 35.1 us; the launch traced here: 34.5 us
  blocking collectives  10.3 us (29%)
  waiting for transfers between devices  8.39 us (24%)
  starting transfers between devices  7.78 us (22%)
  Pallas kernels  7.39 us (21%)
  between operations  0.69 us (2%)
    all_to_all x1, blocking collectives, per_device(): lax.all_to_all(partial, ('tiles', 'far'), split_axis=0, concat_axis=0, ti...  10.3 us
    all_to_all x1, starting transfers between devices, per_device(): lax.all_to_all(packed, 'tiles', split_axis=0, concat_axis=0, tiled=True)  7.14 us
    all_to_all x1, waiting for transfers between devices, per_device(): lax.all_to_all(packed, 'tiles', split_axis=0, concat_axis=0, tiled=True)  4.97 us
    pallas_call x1, Pallas kernels, per_device(): pl.pallas_call(pair_kernel, out_shape=jax.ShapeDtypeStruct((tiles, far, h...  3.64 us
    pallas_call x1, Pallas kernels, per_device(): pl.pallas_call(pack_kernel, out_shape=jax.ShapeDtypeStruct((tiles, blocks...  1.41 us
    pallas_call x1, Pallas kernels, per_device(): pl.pallas_call(lambda *refs: sort_kernel(*refs[:-1], blocks, refs[-1]), o...  1.37 us
    ppermute x1, waiting for transfers between devices, per_device(): other = lax.ppermute(got, 'far', swap)  1.35 us
    ppermute x1, waiting for transfers between devices, per_device(): other = lax.ppermute(mine, 'far', swap)  1.05 us
  transfers between devices with their start and end apart: 4, of which 4 were waited for; matrix products, arithmetic and copies ran while one was open for 0% of the time, Pallas kernels for 5%

profile of v7, /device:TPU:0, one launch (start us, length us, event | category | flops | bytes accessed | tf_op | source)
XLA Modules:
  0.0 34.5 jit_solution(2286971180894038700)
XLA Ops:
  0.0 0.5 %collective-permute-start = (bf16[4,4,128]{2,1,0:T(4,128)(2,1)}, bf16[4,4,128]{2,1,0:T(4,128)(2,1)S(1)}, u32[]{:S(2)}, u32[]{:S(2)}) collective-permute-start(bf16[4,4,128]{2,1,0:T(4,128)(2,1)} %adjoint_ref.1), channel_id=1, source_target_pairs={{1,0},{0,1},{3,2},{2,3},{5,4},{4,5},{7,6},{6,7},{9,8},{8,9},{11,10... | collective-permute-start | bytes 12296 | tf_op jit(solution)/shard_map/ppermute | solution.py:377
  0.5 1.0 %collective-permute-done.partner_ref = bf16[4,4,128]{2,1,0:T(4,128)(2,1)S(1)} collective-permute-done((bf16[4,4,128]{2,1,0:T(4,128)(2,1)}, bf16[4,4,128]{2,1,0:T(4,128)(2,1)S(1)}, u32[]{:S(2)}, u32[]{:S(2)}) %collective-permute-start) | collective-permute-done | bytes 4128 | tf_op jit(solution)/shard_map/ppermute | solution.py:377
  1.5 1.4 %shard_map.91 = f32[8,4,4,256]{3,2,1,0:T(4,128)} custom-call(s32[1]{0:T(128)} %bitcast.1.me_ref.refs_0_, s32[1]{0:T(128)} %bitcast.parity_ref.refs_1_, f32[6,4,128]{2,1,0:T(4,128)} %bitcast.9, bf16[4,4,128]{2,1,0:T(4,128)(2,1)} %strength_ref.1, s32[4,4,128]{2,1,0:T(4,128)} %corner_ref.1), custom_call_target="tpu_custom_call" | custom-call | tf_op jit(solution)/shard_map/pallas_call | solution.py:380
  2.9 7.1 %all-to-all-start = ((f32[8,4,4,256]{3,2,1,0:T(4,128)}), f32[8,4,4,256]{3,2,1,0:T(4,128)S(1)}, u32[]{:S(2)}, u32[]{:S(2)}) async-start(f32[8,4,4,256]{3,2,1,0:T(4,128)} %shard_map.91), calls=%async_computation | async-start | bytes 262144 | tf_op jit(solution)/shard_map/all_to_all | solution.py:386
  10.0 0.0 copy-start
  10.7 0.0 copy-start.1
  10.7 1.4 %shard_map.92.info_ref = s32[1,128]{1,0:T(1,128)} custom-call(s32[1]{0:T(128)} %bitcast.1.me_ref.refs_0_, s32[1]{0:T(128)} %bitcast.parity_ref.refs_1_, s32[1,32]{1,0:T(1,128)} %bitcast.11, s32[1,32]{1,0:T(1,128)} %bitcast.12, s32[1,32]{1,0:T(1,128)} %bitcast.13, s32[1,32]{1,0:T(1,128)} %bitcast.14, s32[1]{0:T(128)S(6)} %copy.10.refs_6_), custom_call_target="tpu_custom_call" | custom-call | flops 4000000 | bytes 900000 | tf_op jit(solution)/shard_map/pallas_call | solution.py:388
  12.1 0.0 copy-done
  12.1 0.0 copy-done.1
  12.1 0.3 shard_map.93
  12.4 5.0 %all-to-all-done.mine_ref = f32[8,4,4,256]{3,2,1,0:T(4,128)S(1)} async-done(((f32[8,4,4,256]{3,2,1,0:T(4,128)}), f32[8,4,4,256]{3,2,1,0:T(4,128)S(1)}, u32[]{:S(2)}, u32[]{:S(2)}) %all-to-all-start) | async-done | bytes 131104 | tf_op jit(solution)/shard_map/all_to_all | solution.py:386
  17.4 0.0 copy-start.2
  17.4 0.0 collective-permute-start.1
  17.4 1.3 %collective-permute-done.1.other_ref = f32[8,4,4,256]{3,2,1,0:T(4,128)S(1)} collective-permute-done((f32[8,4,4,256]{3,2,1,0:T(4,128)S(1)}, f32[8,4,4,256]{3,2,1,0:T(4,128)S(1)}, u32[]{:S(2)}, u32[]{:S(2)}) %collective-permute-start.1) | collective-permute-done | bytes 131104 | tf_op jit(solution)/shard_map/ppermute | solution.py:413
  18.7 0.0 copy-done.2
  18.7 3.6 %shard_map.94 = f32[8,4,2,384]{3,2,1,0:T(2,128)S(1)} custom-call(s32[1,128]{1,0:T(1,128)S(1)} %copy-done.2, f32[4,3,128,128]{3,2,1,0:T(8,128)S(1)} %get-tuple-element.16.centre_ref, bf16[4,128,56]{2,1,0:T(8,128)(2,1)S(1)} %get-tuple-element.17.left_ref, f32[8,4,4,256]{3,2,1,0:T(4,128)S(1)} %all-to-all-done.mine_ref, ...), custom_call_target="tpu_custom_call" | custom-call | tf_op jit(solution)/shard_map/pallas_call | solution.py:414
  22.4 10.3 %all_to_all.10.got_ref = f32[32,2,384]{2,1,0:T(2,128)S(1)} all-to-all(f32[32,2,384]{2,1,0:T(2,128)S(1)} %bitcast.8), channel_id=1, replica_groups=mesh['tiles'=8,'far'=4] {'tiles','far'}, dimensions={0} | all-to-all | bytes 196608 | tf_op jit(solution)/shard_map/all_to_all | solution.py:429
  32.7 0.1 shard_map.95.mine_ref
  32.7 0.2 collective-permute-start.2
  32.9 1.0 %collective-permute-done.2.other_ref = f32[2,384]{1,0:T(2,128)S(1)} collective-permute-done((f32[2,384]{1,0:T(2,128)S(1)}, f32[2,384]{1,0:T(2,128)S(1)}, u32[]{:S(2)}, u32[]{:S(2)}) %collective-permute-start.2) | collective-permute-done | bytes 3104 | tf_op jit(solution)/shard_map/ppermute | solution.py:435
  33.9 0.6 %shard_map.96 = f32[3,512]{1,0:T(4,128)} custom-call(s32[1]{0:T(128)} %bitcast.parity_ref.refs_1_, f32[2,384]{1,0:T(2,128)S(1)} %shard_map.95.mine_ref, f32[2,384]{1,0:T(2,128)S(1)} %collective-permute-done.2.other_ref), custom_call_target="tpu_custom_call" | custom-call | tf_op jit(solution)/shard_map/pallas_call | solution.py:436
Async XLA Ops:
  0.0 1.5 %collective-permute-start = (bf16[4,4,128]{2,1,0:T(4,128)(2,1)}, bf16[4,4,128]{2,1,0:T(4,128)(2,1)S(1)}, u32[]{:S(2)}, u32[]{:S(2)}) collective-permute-start(bf16[4,4,128]{2,1,0:T(4,128)(2,1)} %adjoint_ref.1), channel_id=1, source_target_pairs={{1,0},{0,1},{3,2},{2,3},{5,4},{4,5},{7,6},{6,7},{9,8},{8,9},{11,10... | collective-permute-start | bytes 12296 | tf_op jit(solution)/shard_map/ppermute | solution.py:377
  2.9 14.5 %all-to-all-start = ((f32[8,4,4,256]{3,2,1,0:T(4,128)}), f32[8,4,4,256]{3,2,1,0:T(4,128)S(1)}, u32[]{:S(2)}, u32[]{:S(2)}) async-start(f32[8,4,4,256]{3,2,1,0:T(4,128)} %shard_map.91), calls=%async_computation | async-start | bytes 262144 | tf_op jit(solution)/shard_map/all_to_all | solution.py:386
  10.0 2.1 %copy-start = (f32[4,6,128]{2,0,1:T(4,128)S(1)}, f32[4,6,128]{2,0,1:T(4,128)}, u32[]{:S(2)}) copy-start(f32[4,6,128]{2,0,1:T(4,128)} %param.9) | copy-start | bytes 36868
  10.7 1.4 %copy-start.1 = (bf16[4,4,128]{2,1,0:T(4,128)(2,1)S(1)}, bf16[4,4,128]{2,1,0:T(4,128)(2,1)}, u32[]{:S(2)}) copy-start(bf16[4,4,128]{2,1,0:T(4,128)(2,1)} %adjoint_ref.1) | copy-start | bytes 12292
  17.4 1.4 %copy-start.2 = (s32[1,128]{1,0:T(1,128)S(1)}, s32[1,128]{1,0:T(1,128)}, u32[]{:S(2)}) copy-start(s32[1,128]{1,0:T(1,128)} %shard_map.92.info_ref) | copy-start | bytes 1540
  17.4 1.3 %collective-permute-start.1 = (f32[8,4,4,256]{3,2,1,0:T(4,128)S(1)}, f32[8,4,4,256]{3,2,1,0:T(4,128)S(1)}, u32[]{:S(2)}, u32[]{:S(2)}) collective-permute-start(f32[8,4,4,256]{3,2,1,0:T(4,128)S(1)} %all-to-all-done.mine_ref), channel_id=1, source_target_pairs={{1,0},{0,1},{3,2},{2,3},{5,4},{4,5},{7,6},{6,7},{9,8},{8,9},{11,10... | collective-permute-start | bytes 393224 | tf_op jit(solution)/shard_map/ppermute | solution.py:413
  32.7 1.2 %collective-permute-start.2 = (f32[2,384]{1,0:T(2,128)S(1)}, f32[2,384]{1,0:T(2,128)S(1)}, u32[]{:S(2)}, u32[]{:S(2)}) collective-permute-start(f32[2,384]{1,0:T(2,128)S(1)} %shard_map.95.mine_ref), channel_id=1, source_target_pairs={{1,0},{0,1},{3,2},{2,3},{5,4},{4,5},{7,6},{6,7},{9,8},{8,9},{11,10... | collective-permute-start | bytes 9224 | tf_op jit(solution)/shard_map/ppermute | solution.py:435

commit v8 on v4

--- a/solution.py
+++ b/solution.py
@@ -238,18 +238,18 @@
     one = jnp.ones((keys, width), jnp.bfloat16)
 
     def wide(row):
-        return jnp.broadcast_to(row, (keys, width))
+        return jnp.broadcast_to(row, (8, width))
 
     def narrow(value):
-        return value.astype(jnp.float32).astype(jnp.bfloat16)
-
-    def scatter(tile, b, slot):
+        value = value.astype(jnp.float32)
+        return jnp.concatenate([value] * (keys // 8), axis=0).astype(jnp.bfloat16)
+
+    def spread_out(tile, b, slot, result):
         spread = []
         for c in range(3):
             grad = wide(sums_ref[slot, c : c + 1])
-            upper = grad.astype(jnp.bfloat16)
-            spread += [upper, (grad - upper.astype(jnp.float32)).astype(jnp.bfloat16)]
-        result = None
+            upper = grad.astype(jnp.bfloat16).astype(jnp.float32)
+            spread += [narrow(upper), narrow(grad - upper)]
         for half in range(2):
             parts = []
             hots = []
@@ -274,6 +274,12 @@
                 preferred_element_type=jnp.float32,
             )
             result = product if result is None else result + product
+        return result
+
+    def scatter(tile, places):
+        result = None
+        for b, slot in places:
+            result = spread_out(tile, b, slot, result)
         before = [joined_ref[tile, c] for c in range(3)]
         for c in range(3):
             joined_ref[tile, c] = (
@@ -284,7 +290,7 @@
 
     def scatter_pair(k, slot):
         _, owner, source, _ = read(k)
-        scatter(owner, source, slot)
+        scatter(owner, [(source, slot)])
 
     def two_pairs(nodes):
         def body(step, carry):
@@ -309,8 +315,7 @@
             axis=1,
         )
         sums_ref[2 + b] = -total.T
-    for b in range(blocks):
-        scatter(me, b, 2 + b)
+    scatter(me, [(b, 2 + b) for b in range(blocks)])
 
     def collect(dest, carry):
         for c in range(3):

time: 33.4 us -> 33.6 us (level)
  Pallas kernels: 7.07 us -> 7.77 us
  blocking collectives: 10.4 us -> 9.96 us
    pallas_call x1, Pallas kernels: 3.31 us -> 4.02 us  [per_device(): pl.pallas_call(pair_kernel, out_shape=jax.ShapeDtypeStruct((tiles, far, h...]
    all_to_all x1, blocking collectives: 10.4 us -> 9.96 us  [per_device(): lax.all_to_all(partial, ('tiles', 'far'), split_axis=0, concat_axis=0, ti...]
where the time goes in v8:
time: 33.6 us; the launch traced here: 33.4 us
  blocking collectives  9.96 us (30%)
  Pallas kernels  7.77 us (23%)
  starting transfers between devices  7.64 us (23%)
  waiting for transfers between devices  7.3 us (22%)
  between operations  0.69 us (2%)
    all_to_all x1, blocking collectives, per_device(): lax.all_to_all(partial, ('tiles', 'far'), split_axis=0, concat_axis=0, ti...  9.96 us
    all_to_all x1, starting transfers between devices, per_device(): lax.all_to_all(packed, 'tiles', split_axis=0, concat_axis=0, tiled=True)  7.38 us
    all_to_all x1, waiting for transfers between devices, per_device(): lax.all_to_all(packed, 'tiles', split_axis=0, concat_axis=0, tiled=True)  4.9 us
    pallas_call x1, Pallas kernels, per_device(): pl.pallas_call(pair_kernel, out_shape=jax.ShapeDtypeStruct((tiles, far, h...  4.02 us
    pallas_call x1, Pallas kernels, per_device(): pl.pallas_call(pack_kernel, out_shape=jax.ShapeDtypeStruct((tiles, blocks...  1.41 us
    pallas_call x1, Pallas kernels, per_device(): pl.pallas_call(lambda *refs: sort_kernel(*refs[:-1], blocks, refs[-1]), o...  1.37 us
    ppermute x1, waiting for transfers between devices, per_device(): other = lax.ppermute(got, 'far', swap)  1.35 us
    ppermute x1, waiting for transfers between devices, per_device(): other = lax.ppermute(mine, 'far', swap)  1.05 us
  transfers between devices with their start and end apart: 4, of which 3 were waited for; matrix products, arithmetic and copies ran while one was open for 0% of the time, Pallas kernels for 5%

profile of v8, /device:TPU:0, one launch (start us, length us, event | category | flops | bytes accessed | tf_op | source)
XLA Modules:
  0.0 33.4 jit_solution(8721955481206575299)
XLA Ops:
  0.0 1.4 %shard_map.91 = f32[8,4,4,256]{3,2,1,0:T(4,128)} custom-call(s32[1]{0:T(128)} %bitcast.1.me_ref.refs_0_, s32[1]{0:T(128)} %bitcast.parity_ref.refs_1_, f32[6,4,128]{2,1,0:T(4,128)} %bitcast.9, bf16[4,4,128]{2,1,0:T(4,128)(2,1)} %strength_ref.1, s32[4,4,128]{2,1,0:T(4,128)} %corner_ref.1), custom_call_target="tpu_custom_call" | custom-call | tf_op jit(solution)/shard_map/pallas_call | solution.py:376
  1.4 0.0 copy-start.1
  1.4 7.4 %all-to-all-start = ((f32[8,4,4,256]{3,2,1,0:T(4,128)}), f32[8,4,4,256]{3,2,1,0:T(4,128)S(1)}, u32[]{:S(2)}, u32[]{:S(2)}) async-start(f32[8,4,4,256]{3,2,1,0:T(4,128)} %shard_map.91), calls=%async_computation | async-start | bytes 262144 | tf_op jit(solution)/shard_map/all_to_all | solution.py:382
  8.8 0.0 copy-done.1
  8.8 0.0 copy-start
  8.8 0.1 collective-permute-start
  9.5 1.4 %shard_map.92.info_ref = s32[1,128]{1,0:T(1,128)} custom-call(s32[1]{0:T(128)} %bitcast.1.me_ref.refs_0_, s32[1]{0:T(128)} %bitcast.parity_ref.refs_1_, s32[1,32]{1,0:T(1,128)} %bitcast.11, s32[1,32]{1,0:T(1,128)} %bitcast.12, s32[1,32]{1,0:T(1,128)} %bitcast.13, s32[1,32]{1,0:T(1,128)} %bitcast.14, s32[1]{0:T(128)S(6)} %copy.10.refs_6_), custom_call_target="tpu_custom_call" | custom-call | flops 4000000 | bytes 900000 | tf_op jit(solution)/shard_map/pallas_call | solution.py:385
  10.9 0.0 collective-permute-done.partner_ref
  10.9 0.0 copy-done
  10.9 0.3 shard_map.93
  11.2 4.9 %all-to-all-done.mine_ref = f32[8,4,4,256]{3,2,1,0:T(4,128)S(1)} async-done(((f32[8,4,4,256]{3,2,1,0:T(4,128)}), f32[8,4,4,256]{3,2,1,0:T(4,128)S(1)}, u32[]{:S(2)}, u32[]{:S(2)}) %all-to-all-start) | async-done | bytes 131104 | tf_op jit(solution)/shard_map/all_to_all | solution.py:382
  16.1 0.0 copy-start.2
  16.1 0.0 collective-permute-start.1
  16.1 1.3 %collective-permute-done.1.other_ref = f32[8,4,4,256]{3,2,1,0:T(4,128)S(1)} collective-permute-done((f32[8,4,4,256]{3,2,1,0:T(4,128)S(1)}, f32[8,4,4,256]{3,2,1,0:T(4,128)S(1)}, u32[]{:S(2)}, u32[]{:S(2)}) %collective-permute-start.1) | collective-permute-done | bytes 131104 | tf_op jit(solution)/shard_map/ppermute | solution.py:410
  17.5 0.0 copy-done.2
  17.5 4.0 %shard_map.94 = f32[8,4,2,384]{3,2,1,0:T(2,128)S(1)} custom-call(s32[1,128]{1,0:T(1,128)S(1)} %copy-done.2, f32[4,3,128,128]{3,2,1,0:T(8,128)S(1)} %get-tuple-element.12.centre_ref, bf16[4,128,56]{2,1,0:T(8,128)(2,1)S(1)} %get-tuple-element.13.left_ref, f32[8,4,4,256]{3,2,1,0:T(4,128)S(1)} %all-to-all-done.mine_ref, ...), custom_call_target="tpu_custom_call" | custom-call | tf_op jit(solution)/shard_map/pallas_call | solution.py:411
  21.5 10.0 %all_to_all.10.got_ref = f32[32,2,384]{2,1,0:T(2,128)S(1)} all-to-all(f32[32,2,384]{2,1,0:T(2,128)S(1)} %bitcast.8), channel_id=1, replica_groups=mesh['tiles'=8,'far'=4] {'tiles','far'}, dimensions={0} | all-to-all | bytes 196608 | tf_op jit(solution)/shard_map/all_to_all | solution.py:426
  31.5 0.1 shard_map.95.mine_ref
  31.5 0.2 collective-permute-start.2
  31.7 1.0 %collective-permute-done.2.other_ref = f32[2,384]{1,0:T(2,128)S(1)} collective-permute-done((f32[2,384]{1,0:T(2,128)S(1)}, f32[2,384]{1,0:T(2,128)S(1)}, u32[]{:S(2)}, u32[]{:S(2)}) %collective-permute-start.2) | collective-permute-done | bytes 3104 | tf_op jit(solution)/shard_map/ppermute | solution.py:432
  32.8 0.6 %shard_map.96 = f32[3,512]{1,0:T(4,128)} custom-call(s32[1]{0:T(128)} %bitcast.parity_ref.refs_1_, f32[2,384]{1,0:T(2,128)S(1)} %shard_map.95.mine_ref, f32[2,384]{1,0:T(2,128)S(1)} %collective-permute-done.2.other_ref), custom_call_target="tpu_custom_call" | custom-call | tf_op jit(solution)/shard_map/pallas_call | solution.py:433
Async XLA Ops:
  1.4 7.4 %copy-start.1 = (bf16[4,4,128]{2,1,0:T(4,128)(2,1)S(1)}, bf16[4,4,128]{2,1,0:T(4,128)(2,1)}, u32[]{:S(2)}) copy-start(bf16[4,4,128]{2,1,0:T(4,128)(2,1)} %adjoint_ref.1) | copy-start | bytes 12292
  1.4 14.7 %all-to-all-start = ((f32[8,4,4,256]{3,2,1,0:T(4,128)}), f32[8,4,4,256]{3,2,1,0:T(4,128)S(1)}, u32[]{:S(2)}, u32[]{:S(2)}) async-start(f32[8,4,4,256]{3,2,1,0:T(4,128)} %shard_map.91), calls=%async_computation | async-start | bytes 262144 | tf_op jit(solution)/shard_map/all_to_all | solution.py:382
  8.8 2.1 %copy-start = (f32[4,6,128]{2,0,1:T(4,128)S(1)}, f32[4,6,128]{2,0,1:T(4,128)}, u32[]{:S(2)}) copy-start(f32[4,6,128]{2,0,1:T(4,128)} %param.9) | copy-start | bytes 36868
  8.8 2.1 %collective-permute-start = (bf16[4,4,128]{2,1,0:T(4,128)(2,1)S(1)}, bf16[4,4,128]{2,1,0:T(4,128)(2,1)S(1)}, u32[]{:S(2)}, u32[]{:S(2)}) collective-permute-start(bf16[4,4,128]{2,1,0:T(4,128)(2,1)S(1)} %copy-done.1), channel_id=1, source_target_pairs={{1,0},{0,1},{3,2},{2,3},{5,4},{4,5},{7,6},{6,7},{9,8},{8,9},{11,10... | collective-permute-start | bytes 12296 | tf_op jit(solution)/shard_map/ppermute | solution.py:383
  16.1 1.4 %copy-start.2 = (s32[1,128]{1,0:T(1,128)S(1)}, s32[1,128]{1,0:T(1,128)}, u32[]{:S(2)}) copy-start(s32[1,128]{1,0:T(1,128)} %shard_map.92.info_ref) | copy-start | bytes 1540
  16.1 1.3 %collective-permute-start.1 = (f32[8,4,4,256]{3,2,1,0:T(4,128)S(1)}, f32[8,4,4,256]{3,2,1,0:T(4,128)S(1)}, u32[]{:S(2)}, u32[]{:S(2)}) collective-permute-start(f32[8,4,4,256]{3,2,1,0:T(4,128)S(1)} %all-to-all-done.mine_ref), channel_id=1, source_target_pairs={{1,0},{0,1},{3,2},{2,3},{5,4},{4,5},{7,6},{6,7},{9,8},{8,9},{11,10... | collective-permute-start | bytes 393224 | tf_op jit(solution)/shard_map/ppermute | solution.py:410
  31.5 1.2 %collective-permute-start.2 = (f32[2,384]{1,0:T(2,128)S(1)}, f32[2,384]{1,0:T(2,128)S(1)}, u32[]{:S(2)}, u32[]{:S(2)}) collective-permute-start(f32[2,384]{1,0:T(2,128)S(1)} %shard_map.95.mine_ref), channel_id=1, source_target_pairs={{1,0},{0,1},{3,2},{2,3},{5,4},{4,5},{7,6},{6,7},{9,8},{8,9},{11,10... | collective-permute-start | bytes 9224 | tf_op jit(solution)/shard_map/ppermute | solution.py:432

commit v9 on v8

--- a/solution.py
+++ b/solution.py
@@ -9,6 +9,7 @@
 VMEM = pltpu.VMEM
 LANES = 128
 HEAD = 5
+GROUP = 32
 SPARE = 2
 LIMIT = 48 * 1024 * 1024
 
@@ -202,9 +203,11 @@
             jnp.broadcast_to(shape_ref[owner, 2 * source + 1, c : c + 1], eight) * reach
             for c in range(3)
         ]
+        point = [jnp.concatenate([row] * (GROUP // 8), axis=0) for row in point]
+        extent = [jnp.concatenate([row] * (GROUP // 8), axis=0) for row in extent]
         columns = [jnp.zeros(eight, jnp.float32) for _ in range(3)]
-        for start in range(0, width, 8):
-            rows = slice(start, start + 8)
+        for start in range(0, width, GROUP):
+            rows = slice(start, start + GROUP)
             sums = [row_acc[target, c, rows] for c in range(3)]
 
             def cubed(part):
@@ -224,7 +227,8 @@
                 pulled = even * (centre_ref[target, c, rows] - point[c])
                 if nodes > 1:
                     pulled = pulled - odd * extent[c]
-                columns[c] = columns[c] + pulled
+                for r in range(0, GROUP, 8):
+                    columns[c] = columns[c] + pulled[r : r + 8]
                 row_acc[target, c, rows] = sums[c] + pulled
         for c in range(3):
             sums_ref[slot, c : c + 1] = jnp.sum(columns[c], axis=0, keepdims=True)

time: 33.6 us -> 33.3 us (level)
  Pallas kernels: 7.77 us -> 7.37 us
    pallas_call x1, Pallas kernels: 4.02 us -> 3.62 us  [per_device(): pl.pallas_call(pair_kernel, out_shape=jax.ShapeDtypeStruct((tiles, far, h...]
where the time goes in v9:
time: 33.3 us; the launch traced here: 33.1 us
  blocking collectives  10.1 us (30%)
  starting transfers between devices  7.64 us (23%)
  Pallas kernels  7.37 us (22%)
  waiting for transfers between devices  7.3 us (22%)
  between operations  0.69 us (2%)
    all_to_all x1, blocking collectives, per_device(): lax.all_to_all(partial, ('tiles', 'far'), split_axis=0, concat_axis=0, ti...  10.1 us
    all_to_all x1, starting transfers between devices, per_device(): lax.all_to_all(packed, 'tiles', split_axis=0, concat_axis=0, tiled=True)  7.38 us
    all_to_all x1, waiting for transfers between devices, per_device(): lax.all_to_all(packed, 'tiles', split_axis=0, concat_axis=0, tiled=True)  4.9 us
    pallas_call x1, Pallas kernels, per_device(): pl.pallas_call(pair_kernel, out_shape=jax.ShapeDtypeStruct((tiles, far, h...  3.62 us
    pallas_call x1, Pallas kernels, per_device(): pl.pallas_call(pack_kernel, out_shape=jax.ShapeDtypeStruct((tiles, blocks...  1.41 us
    pallas_call x1, Pallas kernels, per_device(): pl.pallas_call(lambda *refs: sort_kernel(*refs[:-1], blocks, refs[-1]), o...  1.37 us
    ppermute x1, waiting for transfers between devices, per_device(): other = lax.ppermute(got, 'far', swap)  1.35 us
    ppermute x1, waiting for transfers between devices, per_device(): other = lax.ppermute(mine, 'far', swap)  1.05 us
  transfers between devices with their start and end apart: 4, of which 3 were waited for; matrix products, arithmetic and copies ran while one was open for 0% of the time, Pallas kernels for 5%

profile of v9, /device:TPU:0, one launch (start us, length us, event | category | flops | bytes accessed | tf_op | source)
XLA Modules:
  0.0 33.1 jit_solution(3038740611649913483)
XLA Ops:
  0.0 1.4 %shard_map.91 = f32[8,4,4,256]{3,2,1,0:T(4,128)} custom-call(s32[1]{0:T(128)} %bitcast.1.me_ref.refs_0_, s32[1]{0:T(128)} %bitcast.parity_ref.refs_1_, f32[6,4,128]{2,1,0:T(4,128)} %bitcast.9, bf16[4,4,128]{2,1,0:T(4,128)(2,1)} %strength_ref.1, s32[4,4,128]{2,1,0:T(4,128)} %corner_ref.1), custom_call_target="tpu_custom_call" | custom-call | tf_op jit(solution)/shard_map/pallas_call | solution.py:380
  1.4 0.0 copy-start.1
  1.4 7.4 %all-to-all-start = ((f32[8,4,4,256]{3,2,1,0:T(4,128)}), f32[8,4,4,256]{3,2,1,0:T(4,128)S(1)}, u32[]{:S(2)}, u32[]{:S(2)}) async-start(f32[8,4,4,256]{3,2,1,0:T(4,128)} %shard_map.91), calls=%async_computation | async-start | bytes 262144 | tf_op jit(solution)/shard_map/all_to_all | solution.py:386
  8.8 0.0 copy-done.1
  8.8 0.0 copy-start
  8.8 0.1 collective-permute-start
  9.5 1.4 %shard_map.92.info_ref = s32[1,128]{1,0:T(1,128)} custom-call(s32[1]{0:T(128)} %bitcast.1.me_ref.refs_0_, s32[1]{0:T(128)} %bitcast.parity_ref.refs_1_, s32[1,32]{1,0:T(1,128)} %bitcast.11, s32[1,32]{1,0:T(1,128)} %bitcast.12, s32[1,32]{1,0:T(1,128)} %bitcast.13, s32[1,32]{1,0:T(1,128)} %bitcast.14, s32[1]{0:T(128)S(6)} %copy.10.refs_6_), custom_call_target="tpu_custom_call" | custom-call | flops 4000000 | bytes 900000 | tf_op jit(solution)/shard_map/pallas_call | solution.py:389
  10.9 0.0 collective-permute-done.partner_ref
  10.9 0.0 copy-done
  10.9 0.3 shard_map.93
  11.2 4.9 %all-to-all-done.mine_ref = f32[8,4,4,256]{3,2,1,0:T(4,128)S(1)} async-done(((f32[8,4,4,256]{3,2,1,0:T(4,128)}), f32[8,4,4,256]{3,2,1,0:T(4,128)S(1)}, u32[]{:S(2)}, u32[]{:S(2)}) %all-to-all-start) | async-done | bytes 131104 | tf_op jit(solution)/shard_map/all_to_all | solution.py:386
  16.1 0.0 copy-start.2
  16.1 0.0 collective-permute-start.1
  16.1 1.3 %collective-permute-done.1.other_ref = f32[8,4,4,256]{3,2,1,0:T(4,128)S(1)} collective-permute-done((f32[8,4,4,256]{3,2,1,0:T(4,128)S(1)}, f32[8,4,4,256]{3,2,1,0:T(4,128)S(1)}, u32[]{:S(2)}, u32[]{:S(2)}) %collective-permute-start.1) | collective-permute-done | bytes 131104 | tf_op jit(solution)/shard_map/ppermute | solution.py:414
  17.5 0.0 copy-done.2
  17.5 3.6 %shard_map.94 = f32[8,4,2,384]{3,2,1,0:T(2,128)S(1)} custom-call(s32[1,128]{1,0:T(1,128)S(1)} %copy-done.2, f32[4,3,128,128]{3,2,1,0:T(8,128)S(1)} %get-tuple-element.12.centre_ref, bf16[4,128,56]{2,1,0:T(8,128)(2,1)S(1)} %get-tuple-element.13.left_ref, f32[8,4,4,256]{3,2,1,0:T(4,128)S(1)} %all-to-all-done.mine_ref, ...), custom_call_target="tpu_custom_call" | custom-call | tf_op jit(solution)/shard_map/pallas_call | solution.py:415
  21.1 10.1 %all_to_all.10.got_ref = f32[32,2,384]{2,1,0:T(2,128)S(1)} all-to-all(f32[32,2,384]{2,1,0:T(2,128)S(1)} %bitcast.8), channel_id=1, replica_groups=mesh['tiles'=8,'far'=4] {'tiles','far'}, dimensions={0} | all-to-all | bytes 196608 | tf_op jit(solution)/shard_map/all_to_all | solution.py:430
  31.2 0.1 shard_map.95.mine_ref
  31.2 0.2 collective-permute-start.2
  31.4 1.0 %collective-permute-done.2.other_ref = f32[2,384]{1,0:T(2,128)S(1)} collective-permute-done((f32[2,384]{1,0:T(2,128)S(1)}, f32[2,384]{1,0:T(2,128)S(1)}, u32[]{:S(2)}, u32[]{:S(2)}) %collective-permute-start.2) | collective-permute-done | bytes 3104 | tf_op jit(solution)/shard_map/ppermute | solution.py:436
  32.5 0.6 %shard_map.96 = f32[3,512]{1,0:T(4,128)} custom-call(s32[1]{0:T(128)} %bitcast.parity_ref.refs_1_, f32[2,384]{1,0:T(2,128)S(1)} %shard_map.95.mine_ref, f32[2,384]{1,0:T(2,128)S(1)} %collective-permute-done.2.other_ref), custom_call_target="tpu_custom_call" | custom-call | tf_op jit(solution)/shard_map/pallas_call | solution.py:437
Async XLA Ops:
  1.4 7.4 %copy-start.1 = (bf16[4,4,128]{2,1,0:T(4,128)(2,1)S(1)}, bf16[4,4,128]{2,1,0:T(4,128)(2,1)}, u32[]{:S(2)}) copy-start(bf16[4,4,128]{2,1,0:T(4,128)(2,1)} %adjoint_ref.1) | copy-start | bytes 12292
  1.4 14.7 %all-to-all-start = ((f32[8,4,4,256]{3,2,1,0:T(4,128)}), f32[8,4,4,256]{3,2,1,0:T(4,128)S(1)}, u32[]{:S(2)}, u32[]{:S(2)}) async-start(f32[8,4,4,256]{3,2,1,0:T(4,128)} %shard_map.91), calls=%async_computation | async-start | bytes 262144 | tf_op jit(solution)/shard_map/all_to_all | solution.py:386
  8.8 2.1 %copy-start = (f32[4,6,128]{2,0,1:T(4,128)S(1)}, f32[4,6,128]{2,0,1:T(4,128)}, u32[]{:S(2)}) copy-start(f32[4,6,128]{2,0,1:T(4,128)} %param.9) | copy-start | bytes 36868
  8.8 2.1 %collective-permute-start = (bf16[4,4,128]{2,1,0:T(4,128)(2,1)S(1)}, bf16[4,4,128]{2,1,0:T(4,128)(2,1)S(1)}, u32[]{:S(2)}, u32[]{:S(2)}) collective-permute-start(bf16[4,4,128]{2,1,0:T(4,128)(2,1)S(1)} %copy-done.1), channel_id=1, source_target_pairs={{1,0},{0,1},{3,2},{2,3},{5,4},{4,5},{7,6},{6,7},{9,8},{8,9},{11,10... | collective-permute-start | bytes 12296 | tf_op jit(solution)/shard_map/ppermute | solution.py:387
  16.1 1.4 %copy-start.2 = (s32[1,128]{1,0:T(1,128)S(1)}, s32[1,128]{1,0:T(1,128)}, u32[]{:S(2)}) copy-start(s32[1,128]{1,0:T(1,128)} %shard_map.92.info_ref) | copy-start | bytes 1540
  16.1 1.3 %collective-permute-start.1 = (f32[8,4,4,256]{3,2,1,0:T(4,128)S(1)}, f32[8,4,4,256]{3,2,1,0:T(4,128)S(1)}, u32[]{:S(2)}, u32[]{:S(2)}) collective-permute-start(f32[8,4,4,256]{3,2,1,0:T(4,128)S(1)} %all-to-all-done.mine_ref), channel_id=1, source_target_pairs={{1,0},{0,1},{3,2},{2,3},{5,4},{4,5},{7,6},{6,7},{9,8},{8,9},{11,10... | collective-permute-start | bytes 393224 | tf_op jit(solution)/shard_map/ppermute | solution.py:414
  31.2 1.2 %collective-permute-start.2 = (f32[2,384]{1,0:T(2,128)S(1)}, f32[2,384]{1,0:T(2,128)S(1)}, u32[]{:S(2)}, u32[]{:S(2)}) collective-permute-start(f32[2,384]{1,0:T(2,128)S(1)} %shard_map.95.mine_ref), channel_id=1, source_target_pairs={{1,0},{0,1},{3,2},{2,3},{5,4},{4,5},{7,6},{6,7},{9,8},{8,9},{11,10... | collective-permute-start | bytes 9224 | tf_op jit(solution)/shard_map/ppermute | solution.py:436

commit v10 on v9

--- a/solution.py
+++ b/solution.py
@@ -68,7 +68,7 @@
     order = order_ref[...]
     place = lax.broadcasted_iota(jnp.int32, (1, pairs), 1)
     live = place < count_ref[0]
-    word = (owner_ref[...] << bits | source_ref[...]) << bits | target_ref[...]
+    word = (owner_ref[...] * blocks + source_ref[...]) << bits | target_ref[...]
     word = (word << 2 | order).astype(jnp.float32)
     key = jnp.where(live, (3 - order) * pairs + place, 3 * pairs + place).astype(jnp.float32)
     across = lax.broadcasted_iota(jnp.int32, (pairs, pairs), 1)
@@ -122,7 +122,8 @@
     joined_ref,
     shape_ref,
 ):
-    tiles, blocks, _, _ = mine_ref.shape
+    blocks = centre_ref.shape[0]
+    tiles = mine_ref.shape[0] // blocks
     width = centre_ref.shape[3]
     bits = (blocks - 1).bit_length()
     me = info_ref[0, 0]
@@ -130,10 +131,10 @@
 
     def settle(tile, carry):
         for b in range(blocks):
-            mine = mine_ref[tile, b, :, width : 2 * width]
-            other = other_ref[tile, b, :, width : 2 * width]
-            shape_ref[tile, b] = jnp.where(even, mine, other)
-            shape_ref[tile, blocks + b] = jnp.where(even, other, mine)
+            mine = mine_ref[tile * blocks + b, :, width : 2 * width]
+            other = other_ref[tile * blocks + b, :, width : 2 * width]
+            shape_ref[tile * 2 * blocks + b] = jnp.where(even, mine, other)
+            shape_ref[tile * 2 * blocks + blocks + b] = jnp.where(even, other, mine)
         return carry
 
     lax.fori_loop(0, tiles, settle, 0, unroll=min(tiles, 8))
@@ -150,12 +151,10 @@
 
     def read(k):
         word = info_ref[0, HEAD + k]
-        inner = word >> 2
-        outer = inner >> bits
-        return inner & (blocks - 1), outer >> bits, outer & (blocks - 1), word & 3
+        return (word >> 2) & ((1 << bits) - 1), word >> (bits + 2), word & 3
 
     def multiply(k, slot, nodes):
-        target, owner, source, order = read(k)
+        target, source, order = read(k)
         third = order == 3
         alive = jnp.where(order > 0, 1.0, 0.0).astype(jnp.float32)
         reach = reach_of(order)
@@ -165,12 +164,12 @@
         )
         floor_mid = jnp.where(third, 0.0625 * (4.0 / 9.0 / 512.0) ** (-2.0 / 3.0), 3.0e38)
         floor_side = 0.0625 * scale_side
-        point = shape_ref[owner, 2 * source]
-        extent = shape_ref[owner, 2 * source + 1] * reach
+        point = shape_ref[2 * source]
+        extent = shape_ref[2 * source + 1] * reach
         inside = row_ids < 3
         point = jnp.where(inside, jnp.concatenate([point, blank], axis=0), 0.0)
         extent = jnp.where(inside, jnp.concatenate([extent, blank], axis=0), 0.0)
-        values = [ref[owner, source, :, 0:width] * alive for ref in (mine_ref, other_ref)]
+        values = [ref[source, :, 0:width] * alive for ref in (mine_ref, other_ref)]
         empty = jnp.zeros((8, width), jnp.float32)
         quadrature = (
             (point + extent, scale_side, floor_side),
@@ -195,12 +194,12 @@
         )
 
     def one_pair(k, slot, nodes):
-        target, owner, source, order = read(k)
+        target, source, order = read(k)
         reach = reach_of(order)
         eight = (8, width)
-        point = [jnp.broadcast_to(shape_ref[owner, 2 * source, c : c + 1], eight) for c in range(3)]
+        point = [jnp.broadcast_to(shape_ref[2 * source, c : c + 1], eight) for c in range(3)]
         extent = [
-            jnp.broadcast_to(shape_ref[owner, 2 * source + 1, c : c + 1], eight) * reach
+            jnp.broadcast_to(shape_ref[2 * source + 1, c : c + 1], eight) * reach
             for c in range(3)
         ]
         point = [jnp.concatenate([row] * (GROUP // 8), axis=0) for row in point]
@@ -248,7 +247,7 @@
         value = value.astype(jnp.float32)
         return jnp.concatenate([value] * (keys // 8), axis=0).astype(jnp.bfloat16)
 
-    def spread_out(tile, b, slot, result):
+    def spread_out(block, slot, result):
         spread = []
         for c in range(3):
             grad = wide(sums_ref[slot, c : c + 1])
@@ -257,7 +256,7 @@
         for half in range(2):
             parts = []
             hots = []
-            code = wide(shape_ref[tile, 2 * b + half, 3:4]).astype(jnp.int32)
+            code = wide(shape_ref[2 * block + half, 3:4]).astype(jnp.int32)
             for place in (code >> shift, code & ((1 << shift) - 1)):
                 mask = key_ids == narrow(place >> 7)
                 low = narrow(place & (LANES - 1))
@@ -282,8 +281,8 @@
 
     def scatter(tile, places):
         result = None
-        for b, slot in places:
-            result = spread_out(tile, b, slot, result)
+        for block, slot in places:
+            result = spread_out(block, slot, result)
         before = [joined_ref[tile, c] for c in range(3)]
         for c in range(3):
             joined_ref[tile, c] = (
@@ -293,8 +292,8 @@
             )
 
     def scatter_pair(k, slot):
-        _, owner, source, _ = read(k)
-        scatter(owner, [(source, slot)])
+        _, source, _ = read(k)
+        scatter(source // blocks, [(source, slot)])
 
     def two_pairs(nodes):
         def body(step, carry):
@@ -319,7 +318,7 @@
             axis=1,
         )
         sums_ref[2 + b] = -total.T
-    scatter(me, [(b, 2 + b) for b in range(blocks)])
+    scatter(me, [(me * blocks + b, 2 + b) for b in range(blocks)])
 
     def collect(dest, carry):
         for c in range(3):
@@ -422,10 +421,10 @@
             VMEM((blocks, 3, width, width), jnp.float32),
             VMEM((2 + blocks, 8, width), jnp.float32),
             VMEM((tiles, 3, 4 * high, LANES), jnp.float32),
-            VMEM((tiles, 2 * blocks, 4, width), jnp.float32),
+            VMEM((tiles * 2 * blocks, 4, width), jnp.float32),
         ],
         compiler_params=params,
-    )(info, centre, left, got, other)
+    )(info, centre, left, *(x.reshape(tiles * blocks, 4, 2 * width) for x in (got, other)))
     partial = partial.reshape(tiles * far, high // 2, 3 * LANES)
     shares = lax.all_to_all(partial, ("tiles", "far"), split_axis=0, concat_axis=0, tiled=True)
     mine = pl.pallas_call(

time: 33.3 us -> 34.1 us (1.024)
  local copies, waits for them, and re-layouts: 0.01 us -> 0.58 us
    unnamed x6, local copies, waits for them, and re-layouts: 0.01 us -> 0.58 us
where the time goes in v10:
time: 34.1 us; the launch traced here: 33.7 us
  blocking collectives  9.82 us (29%)
  Pallas kernels  7.69 us (23%)
  starting transfers between devices  7.64 us (22%)
  waiting for transfers between devices  7.3 us (21%)
  between operations  0.69 us (2%)
  local copies, waits for them, and re-layouts  0.58 us (2%)
    all_to_all x1, blocking collectives, per_device(): lax.all_to_all(partial, ('tiles', 'far'), split_axis=0, concat_axis=0, ti...  9.82 us
    all_to_all x1, starting transfers between devices, per_device(): lax.all_to_all(packed, 'tiles', split_axis=0, concat_axis=0, tiled=True)  7.38 us
    all_to_all x1, waiting for transfers between devices, per_device(): lax.all_to_all(packed, 'tiles', split_axis=0, concat_axis=0, tiled=True)  4.9 us
    pallas_call x1, Pallas kernels, per_device(): pl.pallas_call(pair_kernel, out_shape=jax.ShapeDtypeStruct((tiles, far, h...  3.94 us
    pallas_call x1, Pallas kernels, per_device(): pl.pallas_call(pack_kernel, out_shape=jax.ShapeDtypeStruct((tiles, blocks...  1.41 us
    pallas_call x1, Pallas kernels, per_device(): pl.pallas_call(lambda *refs: sort_kernel(*refs[:-1], blocks, refs[-1]), o...  1.37 us
    ppermute x1, waiting for transfers between devices, per_device(): other = lax.ppermute(got, 'far', swap)  1.35 us
    ppermute x1, waiting for transfers between devices, per_device(): other = lax.ppermute(mine, 'far', swap)  1.05 us
  transfers between devices with their start and end apart: 4, of which 3 were waited for; matrix products, arithmetic and copies ran while one was open for 0% of the time, Pallas kernels for 5%

profile of v10, /device:TPU:0, one launch (start us, length us, event | category | flops | bytes accessed | tf_op | source)
XLA Modules:
  0.0 33.7 jit_solution(14066649931504686695)
XLA Ops:
  0.0 1.4 %shard_map.91 = f32[8,4,4,256]{3,2,1,0:T(4,128)} custom-call(s32[1]{0:T(128)} %bitcast.1.me_ref.refs_0_, s32[1]{0:T(128)} %bitcast.parity_ref.refs_1_, f32[6,4,128]{2,1,0:T(4,128)} %bitcast.13, bf16[4,4,128]{2,1,0:T(4,128)(2,1)} %strength_ref.1, s32[4,4,128]{2,1,0:T(4,128)} %corner_ref.1), custom_call_target="tpu_custom_call" | custom-call | tf_op jit(solution)/shard_map/pallas_call | solution.py:379
  1.4 0.0 copy-start.1
  1.4 7.4 %all-to-all-start = ((f32[8,4,4,256]{3,2,1,0:T(4,128)}), f32[8,4,4,256]{3,2,1,0:T(4,128)S(1)}, u32[]{:S(2)}, u32[]{:S(2)}) async-start(f32[8,4,4,256]{3,2,1,0:T(4,128)} %shard_map.91), calls=%async_computation | async-start | bytes 262144 | tf_op jit(solution)/shard_map/all_to_all | solution.py:385
  8.8 0.0 copy-done.1
  8.8 0.0 copy-start
  8.8 0.1 collective-permute-start
  9.5 1.4 %shard_map.92.info_ref = s32[1,128]{1,0:T(1,128)} custom-call(s32[1]{0:T(128)} %bitcast.1.me_ref.refs_0_, s32[1]{0:T(128)} %bitcast.parity_ref.refs_1_, s32[1,32]{1,0:T(1,128)} %bitcast.15, s32[1,32]{1,0:T(1,128)} %bitcast.16, s32[1,32]{1,0:T(1,128)} %bitcast.17, s32[1,32]{1,0:T(1,128)} %bitcast.18, s32[1]{0:T(128)S(6)} %copy.10.refs_6_), custom_call_target="tpu_custom_call" | custom-call | flops 4000000 | bytes 900000 | tf_op jit(solution)/shard_map/pallas_call | solution.py:388
  10.9 0.0 collective-permute-done.partner_ref
  10.9 0.0 copy-done
  10.9 0.3 shard_map.93
  11.2 4.9 %all-to-all-done = f32[8,4,4,256]{3,2,1,0:T(4,128)S(1)} async-done(((f32[8,4,4,256]{3,2,1,0:T(4,128)}), f32[8,4,4,256]{3,2,1,0:T(4,128)S(1)}, u32[]{:S(2)}, u32[]{:S(2)}) %all-to-all-start) | async-done | bytes 131104 | tf_op jit(solution)/shard_map/all_to_all | solution.py:385
  16.1 0.0 collective-permute-start.1
  16.1 1.3 %collective-permute-done.1 = f32[8,4,4,256]{3,2,1,0:T(4,128)S(1)} collective-permute-done((f32[8,4,4,256]{3,2,1,0:T(4,128)S(1)}, f32[8,4,4,256]{3,2,1,0:T(4,128)S(1)}, u32[]{:S(2)}, u32[]{:S(2)}) %collective-permute-start.1) | collective-permute-done | bytes 131104 | tf_op jit(solution)/shard_map/ppermute | solution.py:413
  17.5 0.0 copy-start.2
  17.5 0.6 %copy-done.2 = s32[1,128]{1,0:T(1,128)S(1)} copy-done((s32[1,128]{1,0:T(1,128)S(1)}, s32[1,128]{1,0:T(1,128)}, u32[]{:S(2)}) %copy-start.2) | copy-done | bytes 536
  18.1 3.9 %shard_map.94 = f32[8,4,2,384]{3,2,1,0:T(2,128)S(1)} custom-call(s32[1,128]{1,0:T(1,128)S(1)} %copy-done.2, f32[4,3,128,128]{3,2,1,0:T(8,128)S(1)} %get-tuple-element.12.centre_ref, bf16[4,128,56]{2,1,0:T(8,128)(2,1)S(1)} %get-tuple-element.13.left_ref, f32[32,4,256]{2,1,0:T(4,128)S(1)} %bitcast.10, f32[32,4,256]{2,1,0:T(4,128)S(1)} %bitcast.12), custom_call_target="tpu_custom_call" | custom-call | tf_op jit(solution)/shard_map/pallas_call | solution.py:414
  22.0 9.8 %all_to_all.10.got_ref = f32[32,2,384]{2,1,0:T(2,128)S(1)} all-to-all(f32[32,2,384]{2,1,0:T(2,128)S(1)} %bitcast.11), channel_id=1, replica_groups=mesh['tiles'=8,'far'=4] {'tiles','far'}, dimensions={0} | all-to-all | bytes 196608 | tf_op jit(solution)/shard_map/all_to_all | solution.py:429
  31.8 0.1 shard_map.95.mine_ref
  31.9 0.2 collective-permute-start.2
  32.1 1.0 %collective-permute-done.2.other_ref = f32[2,384]{1,0:T(2,128)S(1)} collective-permute-done((f32[2,384]{1,0:T(2,128)S(1)}, f32[2,384]{1,0:T(2,128)S(1)}, u32[]{:S(2)}, u32[]{:S(2)}) %collective-permute-start.2) | collective-permute-done | bytes 3104 | tf_op jit(solution)/shard_map/ppermute | solution.py:435
  33.1 0.6 %shard_map.96 = f32[3,512]{1,0:T(4,128)} custom-call(s32[1]{0:T(128)} %bitcast.parity_ref.refs_1_, f32[2,384]{1,0:T(2,128)S(1)} %shard_map.95.mine_ref, f32[2,384]{1,0:T(2,128)S(1)} %collective-permute-done.2.other_ref), custom_call_target="tpu_custom_call" | custom-call | tf_op jit(solution)/shard_map/pallas_call | solution.py:436
Async XLA Ops:
  1.4 7.4 %copy-start.1 = (bf16[4,4,128]{2,1,0:T(4,128)(2,1)S(1)}, bf16[4,4,128]{2,1,0:T(4,128)(2,1)}, u32[]{:S(2)}) copy-start(bf16[4,4,128]{2,1,0:T(4,128)(2,1)} %adjoint_ref.1) | copy-start | bytes 12292
  1.4 14.7 %all-to-all-start = ((f32[8,4,4,256]{3,2,1,0:T(4,128)}), f32[8,4,4,256]{3,2,1,0:T(4,128)S(1)}, u32[]{:S(2)}, u32[]{:S(2)}) async-start(f32[8,4,4,256]{3,2,1,0:T(4,128)} %shard_map.91), calls=%async_computation | async-start | bytes 262144 | tf_op jit(solution)/shard_map/all_to_all | solution.py:385
  8.8 2.1 %copy-start = (f32[4,6,128]{2,0,1:T(4,128)S(1)}, f32[4,6,128]{2,0,1:T(4,128)}, u32[]{:S(2)}) copy-start(f32[4,6,128]{2,0,1:T(4,128)} %param.9) | copy-start | bytes 36868
  8.8 2.1 %collective-permute-start = (bf16[4,4,128]{2,1,0:T(4,128)(2,1)S(1)}, bf16[4,4,128]{2,1,0:T(4,128)(2,1)S(1)}, u32[]{:S(2)}, u32[]{:S(2)}) collective-permute-start(bf16[4,4,128]{2,1,0:T(4,128)(2,1)S(1)} %copy-done.1), channel_id=1, source_target_pairs={{1,0},{0,1},{3,2},{2,3},{5,4},{4,5},{7,6},{6,7},{9,8},{8,9},{11,10... | collective-permute-start | bytes 12296 | tf_op jit(solution)/shard_map/ppermute | solution.py:386
  16.1 1.3 %collective-permute-start.1 = (f32[8,4,4,256]{3,2,1,0:T(4,128)S(1)}, f32[8,4,4,256]{3,2,1,0:T(4,128)S(1)}, u32[]{:S(2)}, u32[]{:S(2)}) collective-permute-start(f32[8,4,4,256]{3,2,1,0:T(4,128)S(1)} %all-to-all-done), channel_id=1, source_target_pairs={{1,0},{0,1},{3,2},{2,3},{5,4},{4,5},{7,6},{6,7},{9,8},{8,9},{11,10... | collective-permute-start | bytes 393224 | tf_op jit(solution)/shard_map/ppermute | solution.py:413
  17.5 0.6 %copy-start.2 = (s32[1,128]{1,0:T(1,128)S(1)}, s32[1,128]{1,0:T(1,128)}, u32[]{:S(2)}) copy-start(s32[1,128]{1,0:T(1,128)} %shard_map.92.info_ref) | copy-start | bytes 1540
  31.9 1.2 %collective-permute-start.2 = (f32[2,384]{1,0:T(2,128)S(1)}, f32[2,384]{1,0:T(2,128)S(1)}, u32[]{:S(2)}, u32[]{:S(2)}) collective-permute-start(f32[2,384]{1,0:T(2,128)S(1)} %shard_map.95.mine_ref), channel_id=1, source_target_pairs={{1,0},{0,1},{3,2},{2,3},{5,4},{4,5},{7,6},{6,7},{9,8},{8,9},{11,10... | collective-permute-start | bytes 9224 | tf_op jit(solution)/shard_map/ppermute | solution.py:435

commit v11 on v9

--- a/solution.py
+++ b/solution.py
@@ -116,6 +116,7 @@
     mine_ref,
     other_ref,
     out_ref,
+    side_ref,
     product_ref,
     row_acc,
     sums_ref,
@@ -127,6 +128,7 @@
     bits = (blocks - 1).bit_length()
     me = info_ref[0, 0]
     even = info_ref[0, 4] == 0
+    side_ref[...] = jnp.full(side_ref.shape, info_ref[0, 4].astype(jnp.float32))
 
     def settle(tile, carry):
         for b in range(blocks):
@@ -340,9 +342,13 @@
     out_ref[...] = jnp.sum(got_ref[...], axis=0)
 
 
-def last_kernel(parity_ref, mine_ref, other_ref, out_ref):
+def choice_kernel(side_ref, out_ref):
+    out_ref[...] = jnp.broadcast_to(side_ref[0:1, 0:1], out_ref.shape) * 2.0 - 1.0
+
+
+def last_kernel(choice_ref, mine_ref, other_ref, out_ref):
     part = mine_ref.shape[0]
-    even = parity_ref[0] == 0
+    even = choice_ref[...] < 0.0
     mine, other = mine_ref[...], other_ref[...]
     halves = (jnp.where(even, mine, other), jnp.where(even, other, mine))
     for i, half in enumerate(halves):
@@ -412,11 +418,14 @@
     )(geometry, adjoint, partner)
     got, info, left = lax.optimization_barrier((got, info, left))
     other = lax.ppermute(got, "far", swap)
-    partial = pl.pallas_call(
+    partial, side = pl.pallas_call(
         pair_kernel,
-        out_shape=jax.ShapeDtypeStruct((tiles, far, high // 2, 3 * LANES), jnp.float32),
+        out_shape=(
+            jax.ShapeDtypeStruct((tiles, far, high // 2, 3 * LANES), jnp.float32),
+            jax.ShapeDtypeStruct((8, LANES), jnp.float32),
+        ),
         in_specs=[smem] + [vmem] * 4,
-        out_specs=vmem,
+        out_specs=(vmem, vmem),
         scratch_shapes=[
             VMEM((2, width, 4 * width), jnp.float32),
             VMEM((blocks, 3, width, width), jnp.float32),
@@ -428,6 +437,12 @@
     )(info, centre, left, got, other)
     partial = partial.reshape(tiles * far, high // 2, 3 * LANES)
     shares = lax.all_to_all(partial, ("tiles", "far"), split_axis=0, concat_axis=0, tiled=True)
+    choice = pl.pallas_call(
+        choice_kernel,
+        out_shape=jax.ShapeDtypeStruct((high // 2, 3 * LANES), jnp.float32),
+        compiler_params=params,
+        cost_estimate=pl.CostEstimate(flops=4000000, bytes_accessed=900000, transcendentals=0),
+    )(side)
     mine = pl.pallas_call(
         sum_kernel,
         out_shape=jax.ShapeDtypeStruct((high // 2, 3 * LANES), jnp.float32),
@@ -437,10 +452,8 @@
     return pl.pallas_call(
         last_kernel,
         out_shape=jax.ShapeDtypeStruct((3, blocks * width), jnp.float32),
-        in_specs=[smem, vmem, vmem],
-        out_specs=vmem,
         compiler_params=params,
-    )(parity, mine, other)
+    )(choice, mine, other)
 
 
 def solution(mesh):

time: 33.3 us -> 33.8 us (1.015)
    pallas_call x1 -> x2, Pallas kernels: 3.62 us -> 3.74 us  [the longest x1 3.7 us: per_device(): pl.pallas_call(pair_kernel, out_shape=(jax.ShapeDtypeStruct((tiles, far,...]
where the time goes in v11:
time: 33.8 us; the launch traced here: 33.4 us
  blocking collectives  10.3 us (30%)
  starting transfers between devices  7.64 us (23%)
  Pallas kernels  7.59 us (22%)
  waiting for transfers between devices  7.14 us (21%)
  between operations  0.69 us (2%)
    all_to_all x1, blocking collectives, per_device(): lax.all_to_all(partial, ('tiles', 'far'), split_axis=0, concat_axis=0, ti...  10.3 us
    all_to_all x1, starting transfers between devices, per_device(): lax.all_to_all(packed, 'tiles', split_axis=0, concat_axis=0, tiled=True)  7.38 us
    all_to_all x1, waiting for transfers between devices, per_device(): lax.all_to_all(packed, 'tiles', split_axis=0, concat_axis=0, tiled=True)  4.79 us
    pallas_call x1, Pallas kernels, per_device(): pl.pallas_call(pair_kernel, out_shape=(jax.ShapeDtypeStruct((tiles, far,...  3.7 us
    pallas_call x1, Pallas kernels, per_device(): pl.pallas_call(lambda *refs: sort_kernel(*refs[:-1], blocks, refs[-1]), o...  1.48 us
    pallas_call x1, Pallas kernels, per_device(): pl.pallas_call(pack_kernel, out_shape=jax.ShapeDtypeStruct((tiles, blocks...  1.4 us
    ppermute x1, waiting for transfers between devices, per_device(): other = lax.ppermute(got, 'far', swap)  1.35 us
    ppermute x1, waiting for transfers between devices, per_device(): other = lax.ppermute(mine, 'far', swap)  1 us
  transfers between devices with their start and end apart: 4, of which 3 were waited for; matrix products, arithmetic and copies ran while one was open for 0% of the time, Pallas kernels for 5%

profile of v11, /device:TPU:0, one launch (start us, length us, event | category | flops | bytes accessed | tf_op | source)
XLA Modules:
  0.0 33.4 jit_solution(9260544211017416764)
XLA Ops:
  0.0 1.4 %shard_map.91 = f32[8,4,4,256]{3,2,1,0:T(4,128)} custom-call(s32[1]{0:T(128)} %bitcast.me_ref.refs_0_, s32[1]{0:T(128)} %bitcast.1.parity_ref.refs_1_, f32[6,4,128]{2,1,0:T(4,128)} %bitcast.9, bf16[4,4,128]{2,1,0:T(4,128)(2,1)} %strength_ref.1, s32[4,4,128]{2,1,0:T(4,128)} %corner_ref.1), custom_call_target="tpu_custom_call" | custom-call | tf_op jit(solution)/shard_map/pallas_call | solution.py:386
  1.4 0.0 copy-start.1
  1.4 7.4 %all-to-all-start = ((f32[8,4,4,256]{3,2,1,0:T(4,128)}), f32[8,4,4,256]{3,2,1,0:T(4,128)S(1)}, u32[]{:S(2)}, u32[]{:S(2)}) async-start(f32[8,4,4,256]{3,2,1,0:T(4,128)} %shard_map.91), calls=%async_computation | async-start | bytes 262144 | tf_op jit(solution)/shard_map/all_to_all | solution.py:392
  8.8 0.0 copy-done.1
  8.8 0.0 copy-start
  8.8 0.1 collective-permute-start
  9.5 1.5 %shard_map.92.info_ref = s32[1,128]{1,0:T(1,128)} custom-call(s32[1]{0:T(128)} %bitcast.me_ref.refs_0_, s32[1]{0:T(128)} %bitcast.1.parity_ref.refs_1_, s32[1,32]{1,0:T(1,128)} %bitcast.11, s32[1,32]{1,0:T(1,128)} %bitcast.12, s32[1,32]{1,0:T(1,128)} %bitcast.13, s32[1,32]{1,0:T(1,128)} %bitcast.14, s32[1]{0:T(128)S(6)} %copy.10.refs_6_), custom_call_target="tpu_custom_call" | custom-call | flops 4000000 | bytes 900000 | tf_op jit(solution)/shard_map/pallas_call | solution.py:395
  11.0 0.0 collective-permute-done.partner_ref
  11.0 0.0 copy-done
  11.0 0.3 shard_map.93
  11.3 4.8 %all-to-all-done.mine_ref = f32[8,4,4,256]{3,2,1,0:T(4,128)S(1)} async-done(((f32[8,4,4,256]{3,2,1,0:T(4,128)}), f32[8,4,4,256]{3,2,1,0:T(4,128)S(1)}, u32[]{:S(2)}, u32[]{:S(2)}) %all-to-all-start) | async-done | bytes 131104 | tf_op jit(solution)/shard_map/all_to_all | solution.py:392
  16.1 0.0 copy-start.2
  16.1 0.0 collective-permute-start.1
  16.1 1.3 %collective-permute-done.1.other_ref = f32[8,4,4,256]{3,2,1,0:T(4,128)S(1)} collective-permute-done((f32[8,4,4,256]{3,2,1,0:T(4,128)S(1)}, f32[8,4,4,256]{3,2,1,0:T(4,128)S(1)}, u32[]{:S(2)}, u32[]{:S(2)}) %collective-permute-start.1) | collective-permute-done | bytes 131104 | tf_op jit(solution)/shard_map/ppermute | solution.py:420
  17.5 0.0 copy-done.2
  17.5 3.7 %shard_map.94 = (f32[8,4,2,384]{3,2,1,0:T(2,128)S(1)}, f32[8,128]{1,0:T(8,128)S(1)}) custom-call(s32[1,128]{1,0:T(1,128)S(1)} %copy-done.2, f32[4,3,128,128]{3,2,1,0:T(8,128)S(1)} %get-tuple-element.14.centre_ref, bf16[4,128,56]{2,1,0:T(8,128)(2,1)S(1)} %get-tuple-element.15.left_ref, f32[8,4,4,256]{3,2,1,0:T(4,128)S(1)} %all-to-all-done.mine_ref, ...), custom_call_target="tpu_custom_call" | custom-call | tf_op jit(solution)/shard_map/pallas_call | solution.py:421
  21.2 10.3 %all_to_all.10.got_ref = f32[32,2,384]{2,1,0:T(2,128)S(1)} all-to-all(f32[32,2,384]{2,1,0:T(2,128)S(1)} %bitcast.8), channel_id=1, replica_groups=mesh['tiles'=8,'far'=4] {'tiles','far'}, dimensions={0} | all-to-all | bytes 196608 | tf_op jit(solution)/shard_map/all_to_all | solution.py:439
  31.5 0.1 shard_map.96.mine_ref
  31.5 0.2 collective-permute-start.2
  31.8 1.0 %collective-permute-done.2.other_ref = f32[2,384]{1,0:T(2,128)S(1)} collective-permute-done((f32[2,384]{1,0:T(2,128)S(1)}, f32[2,384]{1,0:T(2,128)S(1)}, u32[]{:S(2)}, u32[]{:S(2)}) %collective-permute-start.2) | collective-permute-done | bytes 3104 | tf_op jit(solution)/shard_map/ppermute | solution.py:451
  32.8 0.6 %shard_map.97 = f32[3,512]{1,0:T(4,128)} custom-call(f32[2,384]{1,0:T(2,128)S(1)} %shard_map.95.choice_ref, f32[2,384]{1,0:T(2,128)S(1)} %shard_map.96.mine_ref, f32[2,384]{1,0:T(2,128)S(1)} %collective-permute-done.2.other_ref), custom_call_target="tpu_custom_call" | custom-call | tf_op jit(solution)/shard_map/pallas_call | solution.py:452
  (1 shorter events, 0.0 us)
Async XLA Ops:
  1.4 7.4 %copy-start.1 = (bf16[4,4,128]{2,1,0:T(4,128)(2,1)S(1)}, bf16[4,4,128]{2,1,0:T(4,128)(2,1)}, u32[]{:S(2)}) copy-start(bf16[4,4,128]{2,1,0:T(4,128)(2,1)} %adjoint_ref.1) | copy-start | bytes 12292
  1.4 14.7 %all-to-all-start = ((f32[8,4,4,256]{3,2,1,0:T(4,128)}), f32[8,4,4,256]{3,2,1,0:T(4,128)S(1)}, u32[]{:S(2)}, u32[]{:S(2)}) async-start(f32[8,4,4,256]{3,2,1,0:T(4,128)} %shard_map.91), calls=%async_computation | async-start | bytes 262144 | tf_op jit(solution)/shard_map/all_to_all | solution.py:392
  8.8 2.2 %copy-start = (f32[4,6,128]{2,0,1:T(4,128)S(1)}, f32[4,6,128]{2,0,1:T(4,128)}, u32[]{:S(2)}) copy-start(f32[4,6,128]{2,0,1:T(4,128)} %param.9) | copy-start | bytes 36868
  8.8 2.2 %collective-permute-start = (bf16[4,4,128]{2,1,0:T(4,128)(2,1)S(1)}, bf16[4,4,128]{2,1,0:T(4,128)(2,1)S(1)}, u32[]{:S(2)}, u32[]{:S(2)}) collective-permute-start(bf16[4,4,128]{2,1,0:T(4,128)(2,1)S(1)} %copy-done.1), channel_id=1, source_target_pairs={{1,0},{0,1},{3,2},{2,3},{5,4},{4,5},{7,6},{6,7},{9,8},{8,9},{11,10... | collective-permute-start | bytes 12296 | tf_op jit(solution)/shard_map/ppermute | solution.py:393
  16.1 1.4 %copy-start.2 = (s32[1,128]{1,0:T(1,128)S(1)}, s32[1,128]{1,0:T(1,128)}, u32[]{:S(2)}) copy-start(s32[1,128]{1,0:T(1,128)} %shard_map.92.info_ref) | copy-start | bytes 1540
  16.1 1.3 %collective-permute-start.1 = (f32[8,4,4,256]{3,2,1,0:T(4,128)S(1)}, f32[8,4,4,256]{3,2,1,0:T(4,128)S(1)}, u32[]{:S(2)}, u32[]{:S(2)}) collective-permute-start(f32[8,4,4,256]{3,2,1,0:T(4,128)S(1)} %all-to-all-done.mine_ref), channel_id=1, source_target_pairs={{1,0},{0,1},{3,2},{2,3},{5,4},{4,5},{7,6},{6,7},{9,8},{8,9},{11,10... | collective-permute-start | bytes 393224 | tf_op jit(solution)/shard_map/ppermute | solution.py:420
  31.5 1.2 %collective-permute-start.2 = (f32[2,384]{1,0:T(2,128)S(1)}, f32[2,384]{1,0:T(2,128)S(1)}, u32[]{:S(2)}, u32[]{:S(2)}) collective-permute-start(f32[2,384]{1,0:T(2,128)S(1)} %shard_map.96.mine_ref), channel_id=1, source_target_pairs={{1,0},{0,1},{3,2},{2,3},{5,4},{4,5},{7,6},{6,7},{9,8},{8,9},{11,10... | collective-permute-start | bytes 9224 | tf_op jit(solution)/shard_map/ppermute | solution.py:451

commit v12 on v11

--- a/solution.py
+++ b/solution.py
@@ -443,6 +443,7 @@
         compiler_params=params,
         cost_estimate=pl.CostEstimate(flops=4000000, bytes_accessed=900000, transcendentals=0),
     )(side)
+    shares, choice = lax.optimization_barrier((shares, choice))
     mine = pl.pallas_call(
         sum_kernel,
         out_shape=jax.ShapeDtypeStruct((high // 2, 3 * LANES), jnp.float32),

time: 33.8 us -> 34.7 us (1.027)
  blocking collectives: 10.3 us -> 0 us
  waiting for transfers between devices: 7.14 us -> 15 us
  starting transfers between devices: 7.64 us -> 10.4 us
  Pallas kernels: 7.59 us -> 8.06 us
    all_to_all x1 -> x0, blocking collectives: 10.3 us -> none  [per_device(): lax.all_to_all(partial, ('tiles', 'far'), split_axis=0, concat_axis=0, ti...]
    all_to_all x0 -> x1, waiting for transfers between devices: none -> 7.77 us  [per_device(): lax.all_to_all(partial, ('tiles', 'far'), split_axis=0, concat_axis=0, ti...]
    all_to_all x0 -> x1, starting transfers between devices: none -> 2.74 us  [per_device(): lax.all_to_all(partial, ('tiles', 'far'), split_axis=0, concat_axis=0, ti...]
    pallas_call x1, Pallas kernels: 3.7 us -> 4.25 us  [per_device(): pl.pallas_call(pair_kernel, out_shape=(jax.ShapeDtypeStruct((tiles, far,...]
  transfers between devices with their start and end apart: 4 -> 5, of which waited for: 3 -> 4; matrix products, arithmetic and copies ran while one was open for 0% -> 0% of each run, Pallas kernels for 5% -> 5%
where the time goes in v12:
time: 34.7 us; the launch traced here: 34.2 us
  waiting for transfers between devices  15 us (43%)
  starting transfers between devices  10.4 us (30%)
  Pallas kernels  8.06 us (23%)
  between operations  0.69 us (2%)
    all_to_all x1, waiting for transfers between devices, per_device(): lax.all_to_all(partial, ('tiles', 'far'), split_axis=0, concat_axis=0, ti...  7.77 us
    all_to_all x1, starting transfers between devices, per_device(): lax.all_to_all(packed, 'tiles', split_axis=0, concat_axis=0, tiled=True)  7.38 us
    all_to_all x1, waiting for transfers between devices, per_device(): lax.all_to_all(packed, 'tiles', split_axis=0, concat_axis=0, tiled=True)  4.87 us
    pallas_call x1, Pallas kernels, per_device(): pl.pallas_call(pair_kernel, out_shape=(jax.ShapeDtypeStruct((tiles, far,...  4.25 us
    all_to_all x1, starting transfers between devices, per_device(): lax.all_to_all(partial, ('tiles', 'far'), split_axis=0, concat_axis=0, ti...  2.74 us
    pallas_call x1, Pallas kernels, per_device(): pl.pallas_call(lambda *refs: sort_kernel(*refs[:-1], blocks, refs[-1]), o...  1.4 us
    pallas_call x1, Pallas kernels, per_device(): pl.pallas_call(pack_kernel, out_shape=jax.ShapeDtypeStruct((tiles, blocks...  1.39 us
    ppermute x1, waiting for transfers between devices, per_device(): other = lax.ppermute(got, 'far', swap)  1.35 us
  transfers between devices with their start and end apart: 5, of which 4 were waited for; matrix products, arithmetic and copies ran while one was open for 0% of the time, Pallas kernels for 5%

profile of v12, /device:TPU:0, one launch (start us, length us, event | category | flops | bytes accessed | tf_op | source)
XLA Modules:
  0.0 34.2 jit_solution(6437104000467147324)
XLA Ops:
  0.0 1.4 %shard_map.91 = f32[8,4,4,256]{3,2,1,0:T(4,128)} custom-call(s32[1]{0:T(128)} %bitcast.me_ref.refs_0_, s32[1]{0:T(128)} %bitcast.1.parity_ref.refs_1_, f32[6,4,128]{2,1,0:T(4,128)} %bitcast.8, bf16[4,4,128]{2,1,0:T(4,128)(2,1)} %strength_ref.1, s32[4,4,128]{2,1,0:T(4,128)} %corner_ref.1), custom_call_target="tpu_custom_call" | custom-call | tf_op jit(solution)/shard_map/pallas_call | solution.py:386
  1.4 0.0 copy-start.1
  1.4 7.4 %all-to-all-start = ((f32[8,4,4,256]{3,2,1,0:T(4,128)}), f32[8,4,4,256]{3,2,1,0:T(4,128)S(1)}, u32[]{:S(2)}, u32[]{:S(2)}) async-start(f32[8,4,4,256]{3,2,1,0:T(4,128)} %shard_map.91), calls=%async_computation | async-start | bytes 262144 | tf_op jit(solution)/shard_map/all_to_all | solution.py:392
  8.8 0.0 copy-done.1
  8.8 0.0 copy-start
  8.8 0.1 collective-permute-start
  9.5 1.4 %shard_map.92.info_ref = s32[1,128]{1,0:T(1,128)} custom-call(s32[1]{0:T(128)} %bitcast.me_ref.refs_0_, s32[1]{0:T(128)} %bitcast.1.parity_ref.refs_1_, s32[1,32]{1,0:T(1,128)} %bitcast.10, s32[1,32]{1,0:T(1,128)} %bitcast.11, s32[1,32]{1,0:T(1,128)} %bitcast.12, s32[1,32]{1,0:T(1,128)} %bitcast.13, s32[1]{0:T(128)S(6)} %copy.10.refs_6_), custom_call_target="tpu_custom_call" | custom-call | flops 4000000 | bytes 900000 | tf_op jit(solution)/shard_map/pallas_call | solution.py:395
  10.9 0.0 collective-permute-done.partner_ref
  10.9 0.0 copy-done
  10.9 0.3 shard_map.93
  11.3 4.9 %all-to-all-done.mine_ref = f32[8,4,4,256]{3,2,1,0:T(4,128)S(1)} async-done(((f32[8,4,4,256]{3,2,1,0:T(4,128)}), f32[8,4,4,256]{3,2,1,0:T(4,128)S(1)}, u32[]{:S(2)}, u32[]{:S(2)}) %all-to-all-start) | async-done | bytes 131104 | tf_op jit(solution)/shard_map/all_to_all | solution.py:392
  16.1 0.0 copy-start.2
  16.1 0.0 collective-permute-start.1
  16.1 1.3 %collective-permute-done.1.other_ref = f32[8,4,4,256]{3,2,1,0:T(4,128)S(1)} collective-permute-done((f32[8,4,4,256]{3,2,1,0:T(4,128)S(1)}, f32[8,4,4,256]{3,2,1,0:T(4,128)S(1)}, u32[]{:S(2)}, u32[]{:S(2)}) %collective-permute-start.1) | collective-permute-done | bytes 131104 | tf_op jit(solution)/shard_map/ppermute | solution.py:420
  17.5 0.0 copy-done.2
  17.5 4.3 %shard_map.94 = (f32[8,4,2,384]{3,2,1,0:T(2,128)}, f32[8,128]{1,0:T(8,128)S(1)}) custom-call(s32[1,128]{1,0:T(1,128)S(1)} %copy-done.2, f32[4,3,128,128]{3,2,1,0:T(8,128)S(1)} %get-tuple-element.16.centre_ref, bf16[4,128,56]{2,1,0:T(8,128)(2,1)S(1)} %get-tuple-element.17.left_ref, f32[8,4,4,256]{3,2,1,0:T(4,128)S(1)} %all-to-all-done.mine_ref, ...), custom_call_target="tpu_custom_call" | custom-call | tf_op jit(solution)/shard_map/pallas_call | solution.py:421
  21.7 2.7 %all-to-all-start.1 = ((f32[32,2,384]{2,1,0:T(2,128)}), f32[32,2,384]{2,1,0:T(2,128)S(1)}, u32[]{:S(2)}, u32[]{:S(2)}) async-start(f32[32,2,384]{2,1,0:T(2,128)} %bitcast.7), calls=%async_computation.1 | async-start | bytes 196608 | tf_op jit(solution)/shard_map/all_to_all | solution.py:439
  24.5 7.8 %all-to-all-done.1.got_ref = f32[32,2,384]{2,1,0:T(2,128)S(1)} async-done(((f32[32,2,384]{2,1,0:T(2,128)}), f32[32,2,384]{2,1,0:T(2,128)S(1)}, u32[]{:S(2)}, u32[]{:S(2)}) %all-to-all-start.1) | async-done | bytes 98336 | tf_op jit(solution)/shard_map/all_to_all | solution.py:439
  32.3 0.1 shard_map.96.mine_ref
  32.3 0.2 collective-permute-start.2
  32.5 1.0 %collective-permute-done.2.other_ref = f32[2,384]{1,0:T(2,128)S(1)} collective-permute-done((f32[2,384]{1,0:T(2,128)S(1)}, f32[2,384]{1,0:T(2,128)S(1)}, u32[]{:S(2)}, u32[]{:S(2)}) %collective-permute-start.2) | collective-permute-done | bytes 3104 | tf_op jit(solution)/shard_map/ppermute | solution.py:452
  33.6 0.6 %shard_map.97 = f32[3,512]{1,0:T(4,128)} custom-call(f32[2,384]{1,0:T(2,128)S(1)} %shard_map.95.choice_ref, f32[2,384]{1,0:T(2,128)S(1)} %shard_map.96.mine_ref, f32[2,384]{1,0:T(2,128)S(1)} %collective-permute-done.2.other_ref), custom_call_target="tpu_custom_call" | custom-call | tf_op jit(solution)/shard_map/pallas_call | solution.py:453
  (1 shorter events, 0.0 us)
Async XLA Ops:
  1.4 7.4 %copy-start.1 = (bf16[4,4,128]{2,1,0:T(4,128)(2,1)S(1)}, bf16[4,4,128]{2,1,0:T(4,128)(2,1)}, u32[]{:S(2)}) copy-start(bf16[4,4,128]{2,1,0:T(4,128)(2,1)} %adjoint_ref.1) | copy-start | bytes 12292
  1.4 14.7 %all-to-all-start = ((f32[8,4,4,256]{3,2,1,0:T(4,128)}), f32[8,4,4,256]{3,2,1,0:T(4,128)S(1)}, u32[]{:S(2)}, u32[]{:S(2)}) async-start(f32[8,4,4,256]{3,2,1,0:T(4,128)} %shard_map.91), calls=%async_computation | async-start | bytes 262144 | tf_op jit(solution)/shard_map/all_to_all | solution.py:392
  8.8 2.1 %copy-start = (f32[4,6,128]{2,0,1:T(4,128)S(1)}, f32[4,6,128]{2,0,1:T(4,128)}, u32[]{:S(2)}) copy-start(f32[4,6,128]{2,0,1:T(4,128)} %param.9) | copy-start | bytes 36868
  8.8 2.1 %collective-permute-start = (bf16[4,4,128]{2,1,0:T(4,128)(2,1)S(1)}, bf16[4,4,128]{2,1,0:T(4,128)(2,1)S(1)}, u32[]{:S(2)}, u32[]{:S(2)}) collective-permute-start(bf16[4,4,128]{2,1,0:T(4,128)(2,1)S(1)} %copy-done.1), channel_id=1, source_target_pairs={{1,0},{0,1},{3,2},{2,3},{5,4},{4,5},{7,6},{6,7},{9,8},{8,9},{11,10... | collective-permute-start | bytes 12296 | tf_op jit(solution)/shard_map/ppermute | solution.py:393
  16.1 1.4 %copy-start.2 = (s32[1,128]{1,0:T(1,128)S(1)}, s32[1,128]{1,0:T(1,128)}, u32[]{:S(2)}) copy-start(s32[1,128]{1,0:T(1,128)} %shard_map.92.info_ref) | copy-start | bytes 1540
  16.1 1.3 %collective-permute-start.1 = (f32[8,4,4,256]{3,2,1,0:T(4,128)S(1)}, f32[8,4,4,256]{3,2,1,0:T(4,128)S(1)}, u32[]{:S(2)}, u32[]{:S(2)}) collective-permute-start(f32[8,4,4,256]{3,2,1,0:T(4,128)S(1)} %all-to-all-done.mine_ref), channel_id=1, source_target_pairs={{1,0},{0,1},{3,2},{2,3},{5,4},{4,5},{7,6},{6,7},{9,8},{8,9},{11,10... | collective-permute-start | bytes 393224 | tf_op jit(solution)/shard_map/ppermute | solution.py:420
  21.7 10.6 %all-to-all-start.1 = ((f32[32,2,384]{2,1,0:T(2,128)}), f32[32,2,384]{2,1,0:T(2,128)S(1)}, u32[]{:S(2)}, u32[]{:S(2)}) async-start(f32[32,2,384]{2,1,0:T(2,128)} %bitcast.7), calls=%async_computation.1 | async-start | bytes 196608 | tf_op jit(solution)/shard_map/all_to_all | solution.py:439
  32.3 1.2 %collective-permute-start.2 = (f32[2,384]{1,0:T(2,128)S(1)}, f32[2,384]{1,0:T(2,128)S(1)}, u32[]{:S(2)}, u32[]{:S(2)}) collective-permute-start(f32[2,384]{1,0:T(2,128)S(1)} %shard_map.96.mine_ref), channel_id=1, source_target_pairs={{1,0},{0,1},{3,2},{2,3},{5,4},{4,5},{7,6},{6,7},{9,8},{8,9},{11,10... | collective-permute-start | bytes 9224 | tf_op jit(solution)/shard_map/ppermute | solution.py:452

commit v13 on v9

--- a/solution.py
+++ b/solution.py
@@ -308,9 +308,7 @@
         return body
 
     multiply(0, 0, 3)
-    lax.fori_loop(0, info_ref[0, 1], two_pairs(3), 0)
-    lax.fori_loop(info_ref[0, 1], info_ref[0, 2], two_pairs(2), 0)
-    lax.fori_loop(info_ref[0, 2], info_ref[0, 3], two_pairs(1), 0)
+    lax.fori_loop(0, info_ref[0, 3], two_pairs(3), 0)
     scatter_pair(2 * info_ref[0, 3] - 1, 1)
     for b in range(blocks):
         total = jnp.concatenate(

time: 33.3 us -> 33.9 us (1.018)
  no operation moved by 1% of the time
where the time goes in v13:
time: 33.9 us; the launch traced here: 33.5 us
  blocking collectives  10.4 us (31%)
  starting transfers between devices  7.64 us (23%)
  Pallas kernels  7.54 us (22%)
  waiting for transfers between devices  7.3 us (22%)
  between operations  0.69 us (2%)
    all_to_all x1, blocking collectives, per_device(): lax.all_to_all(partial, ('tiles', 'far'), split_axis=0, concat_axis=0, ti...  10.4 us
    all_to_all x1, starting transfers between devices, per_device(): lax.all_to_all(packed, 'tiles', split_axis=0, concat_axis=0, tiled=True)  7.38 us
    all_to_all x1, waiting for transfers between devices, per_device(): lax.all_to_all(packed, 'tiles', split_axis=0, concat_axis=0, tiled=True)  4.9 us
    pallas_call x1, Pallas kernels, per_device(): pl.pallas_call(pair_kernel, out_shape=jax.ShapeDtypeStruct((tiles, far, h...  3.79 us
    pallas_call x1, Pallas kernels, per_device(): pl.pallas_call(pack_kernel, out_shape=jax.ShapeDtypeStruct((tiles, blocks...  1.41 us
    pallas_call x1, Pallas kernels, per_device(): pl.pallas_call(lambda *refs: sort_kernel(*refs[:-1], blocks, refs[-1]), o...  1.37 us
    ppermute x1, waiting for transfers between devices, per_device(): other = lax.ppermute(got, 'far', swap)  1.35 us
    ppermute x1, waiting for transfers between devices, per_device(): other = lax.ppermute(mine, 'far', swap)  1.05 us
  transfers between devices with their start and end apart: 4, of which 3 were waited for; matrix products, arithmetic and copies ran while one was open for 0% of the time, Pallas kernels for 5%

profile of v13, /device:TPU:0, one launch (start us, length us, event | category | flops | bytes accessed | tf_op | source)
XLA Modules:
  0.0 33.5 jit_solution(13097739208999123900)
XLA Ops:
  0.0 1.4 %shard_map.91 = f32[8,4,4,256]{3,2,1,0:T(4,128)} custom-call(s32[1]{0:T(128)} %bitcast.1.me_ref.refs_0_, s32[1]{0:T(128)} %bitcast.parity_ref.refs_1_, f32[6,4,128]{2,1,0:T(4,128)} %bitcast.9, bf16[4,4,128]{2,1,0:T(4,128)(2,1)} %strength_ref.1, s32[4,4,128]{2,1,0:T(4,128)} %corner_ref.1), custom_call_target="tpu_custom_call" | custom-call | tf_op jit(solution)/shard_map/pallas_call | solution.py:378
  1.4 0.0 copy-start.1
  1.4 7.4 %all-to-all-start = ((f32[8,4,4,256]{3,2,1,0:T(4,128)}), f32[8,4,4,256]{3,2,1,0:T(4,128)S(1)}, u32[]{:S(2)}, u32[]{:S(2)}) async-start(f32[8,4,4,256]{3,2,1,0:T(4,128)} %shard_map.91), calls=%async_computation | async-start | bytes 262144 | tf_op jit(solution)/shard_map/all_to_all | solution.py:384
  8.8 0.0 copy-done.1
  8.8 0.0 copy-start
  8.8 0.1 collective-permute-start
  9.5 1.4 %shard_map.92.info_ref = s32[1,128]{1,0:T(1,128)} custom-call(s32[1]{0:T(128)} %bitcast.1.me_ref.refs_0_, s32[1]{0:T(128)} %bitcast.parity_ref.refs_1_, s32[1,32]{1,0:T(1,128)} %bitcast.11, s32[1,32]{1,0:T(1,128)} %bitcast.12, s32[1,32]{1,0:T(1,128)} %bitcast.13, s32[1,32]{1,0:T(1,128)} %bitcast.14, s32[1]{0:T(128)S(6)} %copy.10.refs_6_), custom_call_target="tpu_custom_call" | custom-call | flops 4000000 | bytes 900000 | tf_op jit(solution)/shard_map/pallas_call | solution.py:387
  10.9 0.0 collective-permute-done.partner_ref
  10.9 0.0 copy-done
  10.9 0.3 shard_map.93
  11.2 4.9 %all-to-all-done.mine_ref = f32[8,4,4,256]{3,2,1,0:T(4,128)S(1)} async-done(((f32[8,4,4,256]{3,2,1,0:T(4,128)}), f32[8,4,4,256]{3,2,1,0:T(4,128)S(1)}, u32[]{:S(2)}, u32[]{:S(2)}) %all-to-all-start) | async-done | bytes 131104 | tf_op jit(solution)/shard_map/all_to_all | solution.py:384
  16.1 0.0 copy-start.2
  16.1 0.0 collective-permute-start.1
  16.1 1.3 %collective-permute-done.1.other_ref = f32[8,4,4,256]{3,2,1,0:T(4,128)S(1)} collective-permute-done((f32[8,4,4,256]{3,2,1,0:T(4,128)S(1)}, f32[8,4,4,256]{3,2,1,0:T(4,128)S(1)}, u32[]{:S(2)}, u32[]{:S(2)}) %collective-permute-start.1) | collective-permute-done | bytes 131104 | tf_op jit(solution)/shard_map/ppermute | solution.py:412
  17.5 0.0 copy-done.2
  17.5 3.8 %shard_map.94 = f32[8,4,2,384]{3,2,1,0:T(2,128)S(1)} custom-call(s32[1,128]{1,0:T(1,128)S(1)} %copy-done.2, f32[4,3,128,128]{3,2,1,0:T(8,128)S(1)} %get-tuple-element.12.centre_ref, bf16[4,128,56]{2,1,0:T(8,128)(2,1)S(1)} %get-tuple-element.13.left_ref, f32[8,4,4,256]{3,2,1,0:T(4,128)S(1)} %all-to-all-done.mine_ref, ...), custom_call_target="tpu_custom_call" | custom-call | tf_op jit(solution)/shard_map/pallas_call | solution.py:413
  21.3 10.4 %all_to_all.10.got_ref = f32[32,2,384]{2,1,0:T(2,128)S(1)} all-to-all(f32[32,2,384]{2,1,0:T(2,128)S(1)} %bitcast.8), channel_id=1, replica_groups=mesh['tiles'=8,'far'=4] {'tiles','far'}, dimensions={0} | all-to-all | bytes 196608 | tf_op jit(solution)/shard_map/all_to_all | solution.py:428
  31.6 0.1 shard_map.95.mine_ref
  31.7 0.2 collective-permute-start.2
  31.9 1.0 %collective-permute-done.2.other_ref = f32[2,384]{1,0:T(2,128)S(1)} collective-permute-done((f32[2,384]{1,0:T(2,128)S(1)}, f32[2,384]{1,0:T(2,128)S(1)}, u32[]{:S(2)}, u32[]{:S(2)}) %collective-permute-start.2) | collective-permute-done | bytes 3104 | tf_op jit(solution)/shard_map/ppermute | solution.py:434
  32.9 0.6 %shard_map.96 = f32[3,512]{1,0:T(4,128)} custom-call(s32[1]{0:T(128)} %bitcast.parity_ref.refs_1_, f32[2,384]{1,0:T(2,128)S(1)} %shard_map.95.mine_ref, f32[2,384]{1,0:T(2,128)S(1)} %collective-permute-done.2.other_ref), custom_call_target="tpu_custom_call" | custom-call | tf_op jit(solution)/shard_map/pallas_call | solution.py:435
Async XLA Ops:
  1.4 7.4 %copy-start.1 = (bf16[4,4,128]{2,1,0:T(4,128)(2,1)S(1)}, bf16[4,4,128]{2,1,0:T(4,128)(2,1)}, u32[]{:S(2)}) copy-start(bf16[4,4,128]{2,1,0:T(4,128)(2,1)} %adjoint_ref.1) | copy-start | bytes 12292
  1.4 14.7 %all-to-all-start = ((f32[8,4,4,256]{3,2,1,0:T(4,128)}), f32[8,4,4,256]{3,2,1,0:T(4,128)S(1)}, u32[]{:S(2)}, u32[]{:S(2)}) async-start(f32[8,4,4,256]{3,2,1,0:T(4,128)} %shard_map.91), calls=%async_computation | async-start | bytes 262144 | tf_op jit(solution)/shard_map/all_to_all | solution.py:384
  8.8 2.1 %copy-start = (f32[4,6,128]{2,0,1:T(4,128)S(1)}, f32[4,6,128]{2,0,1:T(4,128)}, u32[]{:S(2)}) copy-start(f32[4,6,128]{2,0,1:T(4,128)} %param.9) | copy-start | bytes 36868
  8.8 2.1 %collective-permute-start = (bf16[4,4,128]{2,1,0:T(4,128)(2,1)S(1)}, bf16[4,4,128]{2,1,0:T(4,128)(2,1)S(1)}, u32[]{:S(2)}, u32[]{:S(2)}) collective-permute-start(bf16[4,4,128]{2,1,0:T(4,128)(2,1)S(1)} %copy-done.1), channel_id=1, source_target_pairs={{1,0},{0,1},{3,2},{2,3},{5,4},{4,5},{7,6},{6,7},{9,8},{8,9},{11,10... | collective-permute-start | bytes 12296 | tf_op jit(solution)/shard_map/ppermute | solution.py:385
  16.1 1.4 %copy-start.2 = (s32[1,128]{1,0:T(1,128)S(1)}, s32[1,128]{1,0:T(1,128)}, u32[]{:S(2)}) copy-start(s32[1,128]{1,0:T(1,128)} %shard_map.92.info_ref) | copy-start | bytes 1540
  16.1 1.3 %collective-permute-start.1 = (f32[8,4,4,256]{3,2,1,0:T(4,128)S(1)}, f32[8,4,4,256]{3,2,1,0:T(4,128)S(1)}, u32[]{:S(2)}, u32[]{:S(2)}) collective-permute-start(f32[8,4,4,256]{3,2,1,0:T(4,128)S(1)} %all-to-all-done.mine_ref), channel_id=1, source_target_pairs={{1,0},{0,1},{3,2},{2,3},{5,4},{4,5},{7,6},{6,7},{9,8},{8,9},{11,10... | collective-permute-start | bytes 393224 | tf_op jit(solution)/shard_map/ppermute | solution.py:412
  31.7 1.2 %collective-permute-start.2 = (f32[2,384]{1,0:T(2,128)S(1)}, f32[2,384]{1,0:T(2,128)S(1)}, u32[]{:S(2)}, u32[]{:S(2)}) collective-permute-start(f32[2,384]{1,0:T(2,128)S(1)} %shard_map.95.mine_ref), channel_id=1, source_target_pairs={{1,0},{0,1},{3,2},{2,3},{5,4},{4,5},{7,6},{6,7},{9,8},{8,9},{11,10... | collective-permute-start | bytes 9224 | tf_op jit(solution)/shard_map/ppermute | solution.py:434

commit v14 on v9

--- a/solution.py
+++ b/solution.py
@@ -1,3 +1,5 @@
+import functools
+
 import jax
 import jax.numpy as jnp
 from jax import lax
@@ -280,10 +282,13 @@
             result = product if result is None else result + product
         return result
 
-    def scatter(tile, places):
+    def gather_up(places):
         result = None
-        for b, slot in places:
+        for tile, b, slot in places:
             result = spread_out(tile, b, slot, result)
+        return result
+
+    def add_up(tile, result):
         before = [joined_ref[tile, c] for c in range(3)]
         for c in range(3):
             joined_ref[tile, c] = (
@@ -292,17 +297,18 @@
                 + result[(2 * c + 1) * keys : (2 * c + 2) * keys]
             )
 
-    def scatter_pair(k, slot):
+    def scatter_pair(k, slot, work):
         _, owner, source, _ = read(k)
-        scatter(owner, [(source, slot)])
+        result = gather_up([(owner, source, slot)])
+        work()
+        add_up(owner, result)
 
     def two_pairs(nodes):
         def body(step, carry):
             for slot in range(2):
                 k = 2 * step + slot
                 multiply(k + 1, 1 - slot, nodes)
-                scatter_pair(k - 1, 1 - slot)
-                one_pair(k, slot, nodes)
+                scatter_pair(k - 1, 1 - slot, functools.partial(one_pair, k, slot, nodes))
             return carry
 
         return body
@@ -311,7 +317,7 @@
     lax.fori_loop(0, info_ref[0, 1], two_pairs(3), 0)
     lax.fori_loop(info_ref[0, 1], info_ref[0, 2], two_pairs(2), 0)
     lax.fori_loop(info_ref[0, 2], info_ref[0, 3], two_pairs(1), 0)
-    scatter_pair(2 * info_ref[0, 3] - 1, 1)
+    scatter_pair(2 * info_ref[0, 3] - 1, 1, lambda: None)
     for b in range(blocks):
         total = jnp.concatenate(
             [jnp.sum(row_acc[b, c], axis=1, keepdims=True) for c in range(3)]
@@ -319,7 +325,7 @@
             axis=1,
         )
         sums_ref[2 + b] = -total.T
-    scatter(me, [(b, 2 + b) for b in range(blocks)])
+    add_up(me, gather_up([(me, b, 2 + b) for b in range(blocks)]))
 
     def collect(dest, carry):
         for c in range(3):

time: 33.3 us -> 33.8 us (1.015)
  Pallas kernels: 7.37 us -> 7.76 us
    pallas_call x1, Pallas kernels: 3.62 us -> 4.01 us  [per_device(): pl.pallas_call(pair_kernel, out_shape=jax.ShapeDtypeStruct((tiles, far, h...]
where the time goes in v14:
time: 33.8 us; the launch traced here: 33.4 us
  blocking collectives  10 us (30%)
  Pallas kernels  7.76 us (23%)
  starting transfers between devices  7.64 us (23%)
  waiting for transfers between devices  7.3 us (22%)
  between operations  0.69 us (2%)
    all_to_all x1, blocking collectives, per_device(): lax.all_to_all(partial, ('tiles', 'far'), split_axis=0, concat_axis=0, ti...  10 us
    all_to_all x1, starting transfers between devices, per_device(): lax.all_to_all(packed, 'tiles', split_axis=0, concat_axis=0, tiled=True)  7.38 us
    all_to_all x1, waiting for transfers between devices, per_device(): lax.all_to_all(packed, 'tiles', split_axis=0, concat_axis=0, tiled=True)  4.9 us
    pallas_call x1, Pallas kernels, per_device(): pl.pallas_call(pair_kernel, out_shape=jax.ShapeDtypeStruct((tiles, far, h...  4.01 us
    pallas_call x1, Pallas kernels, per_device(): pl.pallas_call(pack_kernel, out_shape=jax.ShapeDtypeStruct((tiles, blocks...  1.41 us
    pallas_call x1, Pallas kernels, per_device(): pl.pallas_call(lambda *refs: sort_kernel(*refs[:-1], blocks, refs[-1]), o...  1.37 us
    ppermute x1, waiting for transfers between devices, per_device(): other = lax.ppermute(got, 'far', swap)  1.35 us
    ppermute x1, waiting for transfers between devices, per_device(): other = lax.ppermute(mine, 'far', swap)  1.05 us
  transfers between devices with their start and end apart: 4, of which 3 were waited for; matrix products, arithmetic and copies ran while one was open for 0% of the time, Pallas kernels for 5%

profile of v14, /device:TPU:0, one launch (start us, length us, event | category | flops | bytes accessed | tf_op | source)
XLA Modules:
  0.0 33.4 jit_solution(17459102427541095509)
XLA Ops:
  0.0 1.4 %shard_map.91 = f32[8,4,4,256]{3,2,1,0:T(4,128)} custom-call(s32[1]{0:T(128)} %bitcast.1.me_ref.refs_0_, s32[1]{0:T(128)} %bitcast.parity_ref.refs_1_, f32[6,4,128]{2,1,0:T(4,128)} %bitcast.9, bf16[4,4,128]{2,1,0:T(4,128)(2,1)} %strength_ref.1, s32[4,4,128]{2,1,0:T(4,128)} %corner_ref.1), custom_call_target="tpu_custom_call" | custom-call | tf_op jit(solution)/shard_map/pallas_call | solution.py:386
  1.4 0.0 copy-start.1
  1.4 7.4 %all-to-all-start = ((f32[8,4,4,256]{3,2,1,0:T(4,128)}), f32[8,4,4,256]{3,2,1,0:T(4,128)S(1)}, u32[]{:S(2)}, u32[]{:S(2)}) async-start(f32[8,4,4,256]{3,2,1,0:T(4,128)} %shard_map.91), calls=%async_computation | async-start | bytes 262144 | tf_op jit(solution)/shard_map/all_to_all | solution.py:392
  8.8 0.0 copy-done.1
  8.8 0.0 copy-start
  8.8 0.1 collective-permute-start
  9.5 1.4 %shard_map.92.info_ref = s32[1,128]{1,0:T(1,128)} custom-call(s32[1]{0:T(128)} %bitcast.1.me_ref.refs_0_, s32[1]{0:T(128)} %bitcast.parity_ref.refs_1_, s32[1,32]{1,0:T(1,128)} %bitcast.11, s32[1,32]{1,0:T(1,128)} %bitcast.12, s32[1,32]{1,0:T(1,128)} %bitcast.13, s32[1,32]{1,0:T(1,128)} %bitcast.14, s32[1]{0:T(128)S(6)} %copy.10.refs_6_), custom_call_target="tpu_custom_call" | custom-call | flops 4000000 | bytes 900000 | tf_op jit(solution)/shard_map/pallas_call | solution.py:395
  10.9 0.0 collective-permute-done.partner_ref
  10.9 0.0 copy-done
  10.9 0.3 shard_map.93
  11.2 4.9 %all-to-all-done.mine_ref = f32[8,4,4,256]{3,2,1,0:T(4,128)S(1)} async-done(((f32[8,4,4,256]{3,2,1,0:T(4,128)}), f32[8,4,4,256]{3,2,1,0:T(4,128)S(1)}, u32[]{:S(2)}, u32[]{:S(2)}) %all-to-all-start) | async-done | bytes 131104 | tf_op jit(solution)/shard_map/all_to_all | solution.py:392
  16.1 0.0 copy-start.2
  16.1 0.0 collective-permute-start.1
  16.1 1.3 %collective-permute-done.1.other_ref = f32[8,4,4,256]{3,2,1,0:T(4,128)S(1)} collective-permute-done((f32[8,4,4,256]{3,2,1,0:T(4,128)S(1)}, f32[8,4,4,256]{3,2,1,0:T(4,128)S(1)}, u32[]{:S(2)}, u32[]{:S(2)}) %collective-permute-start.1) | collective-permute-done | bytes 131104 | tf_op jit(solution)/shard_map/ppermute | solution.py:420
  17.5 0.0 copy-done.2
  17.5 4.0 %shard_map.94 = f32[8,4,2,384]{3,2,1,0:T(2,128)S(1)} custom-call(s32[1,128]{1,0:T(1,128)S(1)} %copy-done.2, f32[4,3,128,128]{3,2,1,0:T(8,128)S(1)} %get-tuple-element.12.centre_ref, bf16[4,128,56]{2,1,0:T(8,128)(2,1)S(1)} %get-tuple-element.13.left_ref, f32[8,4,4,256]{3,2,1,0:T(4,128)S(1)} %all-to-all-done.mine_ref, ...), custom_call_target="tpu_custom_call" | custom-call | tf_op jit(solution)/shard_map/pallas_call | solution.py:421
  21.5 10.0 %all_to_all.10.got_ref = f32[32,2,384]{2,1,0:T(2,128)S(1)} all-to-all(f32[32,2,384]{2,1,0:T(2,128)S(1)} %bitcast.8), channel_id=1, replica_groups=mesh['tiles'=8,'far'=4] {'tiles','far'}, dimensions={0} | all-to-all | bytes 196608 | tf_op jit(solution)/shard_map/all_to_all | solution.py:436
  31.5 0.1 shard_map.95.mine_ref
  31.6 0.2 collective-permute-start.2
  31.8 1.0 %collective-permute-done.2.other_ref = f32[2,384]{1,0:T(2,128)S(1)} collective-permute-done((f32[2,384]{1,0:T(2,128)S(1)}, f32[2,384]{1,0:T(2,128)S(1)}, u32[]{:S(2)}, u32[]{:S(2)}) %collective-permute-start.2) | collective-permute-done | bytes 3104 | tf_op jit(solution)/shard_map/ppermute | solution.py:442
  32.8 0.6 %shard_map.96 = f32[3,512]{1,0:T(4,128)} custom-call(s32[1]{0:T(128)} %bitcast.parity_ref.refs_1_, f32[2,384]{1,0:T(2,128)S(1)} %shard_map.95.mine_ref, f32[2,384]{1,0:T(2,128)S(1)} %collective-permute-done.2.other_ref), custom_call_target="tpu_custom_call" | custom-call | tf_op jit(solution)/shard_map/pallas_call | solution.py:443
Async XLA Ops:
  1.4 7.4 %copy-start.1 = (bf16[4,4,128]{2,1,0:T(4,128)(2,1)S(1)}, bf16[4,4,128]{2,1,0:T(4,128)(2,1)}, u32[]{:S(2)}) copy-start(bf16[4,4,128]{2,1,0:T(4,128)(2,1)} %adjoint_ref.1) | copy-start | bytes 12292
  1.4 14.7 %all-to-all-start = ((f32[8,4,4,256]{3,2,1,0:T(4,128)}), f32[8,4,4,256]{3,2,1,0:T(4,128)S(1)}, u32[]{:S(2)}, u32[]{:S(2)}) async-start(f32[8,4,4,256]{3,2,1,0:T(4,128)} %shard_map.91), calls=%async_computation | async-start | bytes 262144 | tf_op jit(solution)/shard_map/all_to_all | solution.py:392
  8.8 2.1 %copy-start = (f32[4,6,128]{2,0,1:T(4,128)S(1)}, f32[4,6,128]{2,0,1:T(4,128)}, u32[]{:S(2)}) copy-start(f32[4,6,128]{2,0,1:T(4,128)} %param.9) | copy-start | bytes 36868
  8.8 2.1 %collective-permute-start = (bf16[4,4,128]{2,1,0:T(4,128)(2,1)S(1)}, bf16[4,4,128]{2,1,0:T(4,128)(2,1)S(1)}, u32[]{:S(2)}, u32[]{:S(2)}) collective-permute-start(bf16[4,4,128]{2,1,0:T(4,128)(2,1)S(1)} %copy-done.1), channel_id=1, source_target_pairs={{1,0},{0,1},{3,2},{2,3},{5,4},{4,5},{7,6},{6,7},{9,8},{8,9},{11,10... | collective-permute-start | bytes 12296 | tf_op jit(solution)/shard_map/ppermute | solution.py:393
  16.1 1.4 %copy-start.2 = (s32[1,128]{1,0:T(1,128)S(1)}, s32[1,128]{1,0:T(1,128)}, u32[]{:S(2)}) copy-start(s32[1,128]{1,0:T(1,128)} %shard_map.92.info_ref) | copy-start | bytes 1540
  16.1 1.3 %collective-permute-start.1 = (f32[8,4,4,256]{3,2,1,0:T(4,128)S(1)}, f32[8,4,4,256]{3,2,1,0:T(4,128)S(1)}, u32[]{:S(2)}, u32[]{:S(2)}) collective-permute-start(f32[8,4,4,256]{3,2,1,0:T(4,128)S(1)} %all-to-all-done.mine_ref), channel_id=1, source_target_pairs={{1,0},{0,1},{3,2},{2,3},{5,4},{4,5},{7,6},{6,7},{9,8},{8,9},{11,10... | collective-permute-start | bytes 393224 | tf_op jit(solution)/shard_map/ppermute | solution.py:420
  31.6 1.2 %collective-permute-start.2 = (f32[2,384]{1,0:T(2,128)S(1)}, f32[2,384]{1,0:T(2,128)S(1)}, u32[]{:S(2)}, u32[]{:S(2)}) collective-permute-start(f32[2,384]{1,0:T(2,128)S(1)} %shard_map.95.mine_ref), channel_id=1, source_target_pairs={{1,0},{0,1},{3,2},{2,3},{5,4},{4,5},{7,6},{6,7},{9,8},{8,9},{11,10... | collective-permute-start | bytes 9224 | tf_op jit(solution)/shard_map/ppermute | solution.py:442
